TPU v7x, 256 devices: a whole 4x4x8 slice. The times are simulated.
256 devices in a mesh: seq: 16 (over x, y), head: 16 (over z, core).
Axes of the slice: x: 4, y: 4, z: 8, core: 2. Of those that a mesh axis runs over, the one named last changes fastest.
Arguments:
- video_q: bfloat16 [32768, 3072], P(('seq', 'head')), may hold values from -8 to 8
- video_k: bfloat16 [32768, 3072], P(('seq', 'head')), may hold values from -8 to 8
- video_v: bfloat16 [32768, 3072], P(('seq', 'head')), may hold values from -1.8984375 to 1.8984375
- text_q: bfloat16 [226, 3072], P(None, 'head'), may hold values from -8 to 8
- text_k: bfloat16 [226, 3072], P(None, 'head'), may hold values from -8 to 8
- text_v: bfloat16 [226, 3072], P(None, 'head'), may hold values from -1.8984375 to 1.8984375
- offsets: int32 [27, 3], replicated, may hold values from -1 to 1, as said below
- block_mask: int32 [256, 27], P('seq'), may hold values 0 or 1
- text_mask: int32 [226], replicated, may hold values from 0 to 1, as said below
Outputs:
- video_out: bfloat16 [32768, 3072], P(('seq', 'head'))
- text_out: bfloat16 [226, 3072], P(None, 'head')
Inputs may be any that keep to these rules, and one draw needn't show every extreme that they name: `offsets`: each row is a distinct tile offset; a third of the rows each have time offset -1, 0 and +1. `text_mask`: text slot 0 is always live.
All inputs are finite; a program needn't handle non-finite values. No bound on the sum of `block_mask` on one device may be relied on, other than what follows from the above.
Results may differ from a plain program's by a relative error of at most 0.008.
Values may be sent and summed in bfloat16 or wider, within the bound.
No kernel may reach another device: no remote copies, remote signals or barrier semaphores. Data moves between devices by JAX's collectives and lax.ppermute only.
A program may use at most 128 MiB of HBM per device.

v0:
```python
import math

import jax
import jax.numpy as jnp
from jax import lax
from jax.sharding import PartitionSpec as P

HD = 64
TEXT = 226
TILE = 128
TH = 4
TW = 4
NB = 27


NEG_FILL = -jnp.inf


def padded(shard, sides, width):
    for axis, dim in sides:
        count, length = (lax.axis_size(axis), shard.shape[dim])
        up = [(i, (i + 1) % count) for i in range(count - 1)]
        down = [(j, i) for i, j in up]
        last = lax.slice_in_dim(shard, length - width, length, axis=dim)
        leading = lax.slice_in_dim(shard, 0, width, axis=dim)
        before = lax.ppermute(last, axis, up)
        after = lax.ppermute(leading, axis, down)
        shard = jnp.concatenate([before, shard, after], axis=dim)
    return shard


def neighbour_table(offsets, block_mask):
    tiles_here = block_mask.shape[0]
    layer_tiles = TH * TW
    layer_count = tiles_here // layer_tiles
    tile_spots = jnp.arange(tiles_here, dtype=jnp.int32)
    local_layer = tile_spots // layer_tiles
    spot_height = tile_spots % layer_tiles // TW
    spot_across = tile_spots % TW
    first_layer = lax.axis_index("seq") * layer_count
    layers_all = layer_count * lax.axis_size("seq")
    moved_t = local_layer[:, None] + offsets[None, :, 0]
    moved_h = spot_height[:, None] + offsets[None, :, 1]
    moved_w = spot_across[:, None] + offsets[None, :, 2]
    global_layer = first_layer + moved_t
    live_rows = (
        (moved_h >= 0)
        & (moved_h < TH)
        & (moved_w >= 0)
        & (moved_w < TW)
        & (global_layer >= 0)
        & (global_layer < layers_all)
        & (block_mask == 1)
    )
    target_rows = jnp.where(live_rows, ((moved_t + 1) * TH + moved_h) * TW + moved_w, 0)
    return (target_rows, live_rows)


def widen(key_here, value_here):
    joined = jnp.concatenate([key_here, value_here], axis=2)
    layered = joined.reshape(-1, TH * TW, joined.shape[1], joined.shape[2])
    grown = padded(layered, (("seq", 0),), 1)
    return grown.reshape(-1, joined.shape[1], joined.shape[2])


def attend_rows(query_rows, kv_flat, target_rows, live_rows, text_keys, text_vals, text_live):
    tiles_here, row_count, feature_width = query_rows.shape
    head_count = feature_width // HD
    scale = 1.0 / math.sqrt(HD)
    group_size = 1
    while (
        group_size * 2 * row_count <= 512
        and group_size * 2 <= 16
        and (tiles_here % (group_size * 2) == 0)
    ):
        group_size = group_size * 2
    group_total = tiles_here // group_size

    def one_group(group_index):
        start_tile = group_index * group_size
        query_block = lax.dynamic_slice_in_dim(query_rows, start_tile, group_size, 0).reshape(
            group_size, row_count, head_count, HD
        )
        target_block = lax.dynamic_slice_in_dim(target_rows, start_tile, group_size, 0)
        live_block = lax.dynamic_slice_in_dim(live_rows, start_tile, group_size, 0)
        nearby = kv_flat[target_block]
        nearby_k = nearby[..., :feature_width].reshape(group_size, NB * TILE, head_count, HD)
        nearby_v = nearby[..., feature_width:].reshape(group_size, NB * TILE, head_count, HD)
        live_keys = jnp.repeat(live_block, TILE, axis=1)
        video_scores = (
            jnp.einsum("grhd,gkhd->ghrk", query_block, nearby_k, preferred_element_type=jnp.float32)
            * scale
        )
        video_scores = jnp.where(live_keys[:, None, None, :], video_scores, NEG_FILL)
        own_scores = (
            jnp.einsum("grhd,khd->ghrk", query_block, text_keys, preferred_element_type=jnp.float32)
            * scale
        )
        own_scores = jnp.where(text_live[None, None, None, :], own_scores, NEG_FILL)
        highest = jnp.maximum(jnp.max(video_scores, -1), jnp.max(own_scores, -1))
        video_exp = jnp.exp(video_scores - highest[..., None])
        own_exp = jnp.exp(own_scores - highest[..., None])
        totals = jnp.sum(video_exp, -1) + jnp.sum(own_exp, -1)
        mixed = jnp.einsum(
            "ghrk,gkhd->grhd",
            video_exp.astype(jnp.bfloat16),
            nearby_v,
            preferred_element_type=jnp.float32,
        )
        mixed = mixed + jnp.einsum(
            "ghrk,khd->grhd",
            own_exp.astype(jnp.bfloat16),
            text_vals,
            preferred_element_type=jnp.float32,
        )
        result = mixed / jnp.transpose(totals, (0, 2, 1))[..., None]
        return result.astype(jnp.bfloat16).reshape(group_size, row_count, feature_width)

    answers = lax.map(one_group, jnp.arange(group_total, dtype=jnp.int32))
    return answers.reshape(tiles_here, row_count, feature_width)


def text_attention(text_query, text_keys, text_vals, slab_keys, slab_vals, text_live):
    scale = 1.0 / math.sqrt(HD)
    video_scores = (
        jnp.einsum("thd,khd->htk", text_query, slab_keys, preferred_element_type=jnp.float32)
        * scale
    )
    own_scores = (
        jnp.einsum("thd,khd->htk", text_query, text_keys, preferred_element_type=jnp.float32)
        * scale
    )
    own_scores = jnp.where(text_live[None, None, :], own_scores, NEG_FILL)
    own_top = jnp.max(own_scores, -1)
    video_top = lax.pmax(jnp.max(video_scores, -1), "seq")
    highest = jnp.maximum(video_top, own_top)
    video_exp = jnp.exp(video_scores - highest[..., None])
    video_mixed = jnp.einsum(
        "htk,khd->thd",
        video_exp.astype(jnp.bfloat16),
        slab_vals,
        preferred_element_type=jnp.float32,
    )
    video_mixed, video_totals = lax.psum((video_mixed, jnp.sum(video_exp, -1)), "seq")
    own_exp = jnp.exp(own_scores - highest[..., None])
    mixed = video_mixed + jnp.einsum(
        "htk,khd->thd", own_exp.astype(jnp.bfloat16), text_vals, preferred_element_type=jnp.float32
    )
    totals = video_totals + jnp.sum(own_exp, -1)
    return (mixed / jnp.transpose(totals)[:, :, None]).astype(jnp.bfloat16)


def body(video_q, video_k, video_v, text_q, text_k, text_v, offsets, block_mask, text_mask):
    feature_width = text_q.shape[1]
    head_count = feature_width // HD
    target_rows, live_rows = neighbour_table(offsets, block_mask)
    text_live = text_mask == 1
    text_keys = text_k.reshape(TEXT, head_count, HD)
    text_vals = text_v.reshape(TEXT, head_count, HD)
    query_tiles = video_q.reshape(-1, TILE, video_q.shape[1])
    key_tiles = video_k.reshape(-1, TILE, video_k.shape[1])
    value_tiles = video_v.reshape(-1, TILE, video_v.shape[1])
    query_here, key_here, value_here = (
        lax.all_to_all(query_tiles, "head", split_axis=2, concat_axis=0, tiled=True),
        lax.all_to_all(key_tiles, "head", split_axis=2, concat_axis=0, tiled=True),
        lax.all_to_all(value_tiles, "head", split_axis=2, concat_axis=0, tiled=True),
    )
    kv_flat = widen(key_here, value_here)
    answer_here = attend_rows(
        query_here, kv_flat, target_rows, live_rows, text_keys, text_vals, text_live
    )
    video_back = lax.all_to_all(answer_here, "head", split_axis=0, concat_axis=2, tiled=True)
    video_out = video_back.reshape(video_q.shape)
    slab_rows = key_here.shape[0] * TILE
    text_result = text_attention(
        text_q.reshape(TEXT, head_count, HD),
        text_keys,
        text_vals,
        key_here.reshape(slab_rows, head_count, HD),
        value_here.reshape(slab_rows, head_count, HD),
        text_live,
    )
    return (video_out, text_result.reshape(TEXT, feature_width))


def solution(mesh):
    return jax.shard_map(
        body,
        mesh=mesh,
        in_specs=(
            P(("seq", "head"), None),
            P(("seq", "head"), None),
            P(("seq", "head"), None),
            P(None, "head"),
            P(None, "head"),
            P(None, "head"),
            P(),
            P("seq", None),
            P(),
        ),
        out_specs=(P(("seq", "head"), None), P(None, "head")),
        check_vma=False,
    )
```

profile of v0, /device:TPU:2, one launch (start us, length us, event | category | flops | bytes accessed | tf_op | source)
XLA Modules:
  0.0 742.6 jit_solution(11255993191149167608)
XLA Ops:
  11.4 17.0 %reduce = bf16[3072,128]{1,0:T(8,128)(2,1)S(1)} reduce(bf16[3072,1,128]{2,1,0:T(2,128)(2,1)S(1)} %bitcast.152, bf16[]{:T(256)} %broadcast.167), dimensions={1}, to_apply=%bitcast.93.reduce_sub_computation | reduce | bytes 1572866
  41.7 17.0 %reduce.1 = bf16[3072,128]{1,0:T(8,128)(2,1)S(1)} reduce(bf16[3072,1,128]{2,1,0:T(2,128)(2,1)S(1)} %bitcast.157, bf16[]{:T(256)} %broadcast.167), dimensions={1}, to_apply=%bitcast.95.reduce_sub_computation | reduce | bytes 1572866
  68.1 19.8 %all-to-all-done = bf16[16,2,12288]{2,1,0:T(2,128)(2,1)} async-done(((bf16[16,2,12288]{2,1,0:T(2,128)(2,1)}), bf16[16,2,12288]{2,1,0:T(2,128)(2,1)}, u32[]{:S(2)}, u32[]{:S(2)}) %all-to-all-start) | async-done | bytes 786464 | tf_op jit(solution)/shard_map/all_to_all | solution.py:165
  103.8 18.9 %reduce.2 = bf16[3072,128]{1,0:T(8,128)(2,1)} reduce(bf16[3072,1,128]{2,1,0:T(2,128)(2,1)} %bitcast.155, bf16[]{:T(256)} %broadcast.167), dimensions={1}, to_apply=%bitcast.97.reduce_sub_computation | reduce | bytes 1572866
  133.0 18.3 %all-to-all-done.2 = bf16[16,2,12288]{2,1,0:T(2,128)(2,1)S(1)} async-done(((bf16[16,2,12288]{2,1,0:T(2,128)(2,1)}), bf16[16,2,12288]{2,1,0:T(2,128)(2,1)S(1)}, u32[]{:S(2)}, u32[]{:S(2)}) %all-to-all-start.2) | async-done | bytes 786464 | tf_op jit(solution)/shard_map/all_to_all | solution.py:164
  168.9 420.4 %while.10 = (s32[]{:T(128)}, bf16[4,4,128,192]{2,3,1,0:T(8,128)(2,1)}, s32[4]{0:T(128)S(1)}, s32[16,27]{1,0:T(8,128)S(1)}, bf16[48,128,384]{2,1,0:T(8,128)(2,1)}...) while((s32[]{:T(128)}, ...), condition=%wide.region_5.6_spmd, body=%wide.region_0.5_spmd.sunk | while | flops 1508589824 | bytes 172234592 | solution.py:119
  181.1 11.4 %fusion.85 = (bf16[4,27,128,192]{3,2,1,0:T(8,128)(2,1)}, bf16[4,27,128,192]{3,2,1,0:T(8,128)(2,1)}) fusion(bf16[4,27,128,384]{3,2,1,0:T(8,128)(2,1)} %bitcast.141), kind=kLoop, calls=%fused_computation.90.clone.1 | loop fusion | bytes 21233664 | tf_op jit(solution)/shard_map/while/body/eval_jaxpr/slice | solution.py:87
  192.5 13.0 %copy.125 = bf16[4,27,128,192]{2,1,3,0:T(8,128)(2,1)} copy(bf16[4,27,128,192]{3,2,1,0:T(8,128)(2,1)} %get-tuple-element.223) | data formatting | bytes 10616832 | tf_op jit(solution)/shard_map/while
  215.5 13.0 %copy.127 = bf16[4,27,128,192]{2,1,3,0:T(8,128)(2,1)} copy(bf16[4,27,128,192]{3,2,1,0:T(8,128)(2,1)} %get-tuple-element.224) | data formatting | bytes 10616832 | tf_op jit(solution)/shard_map/while
  238.4 12.5 %fusion.86 = (f32[4,3,128]{2,1,0:T(4,128)S(1)}, f32[4,3,128,3456]{3,2,1,0:T(8,128)}) fusion(pred[4,3456]{1,0:T(4,128)(4,1)S(1)} %bitcast.145, bf16[4,128,3,64]{1,3,2,0:T(8,128)(2,1)S(1)} %bitcast.142, bf16[4,3456,3,64]{1,3,2,0:T(8,128)(2,1)} %reshape.160), kind=kOutput, calls=%fused_computation.3.clone.1 | convolution fusion | flops 695400960 | bytes 26758656 | tf_op jit(solution)/shard_map/while/body/eval_jaxpr/grhd,gkhd->ghrk/dot_general | solution.py:91
  297.6 13.0 %copy.125 = bf16[4,27,128,192]{2,1,3,0:T(8,128)(2,1)} copy(bf16[4,27,128,192]{3,2,1,0:T(8,128)(2,1)} %get-tuple-element.223) | data formatting | bytes 10616832 | tf_op jit(solution)/shard_map/while
  320.6 13.0 %copy.127 = bf16[4,27,128,192]{2,1,3,0:T(8,128)(2,1)} copy(bf16[4,27,128,192]{3,2,1,0:T(8,128)(2,1)} %get-tuple-element.224) | data formatting | bytes 10616832 | tf_op jit(solution)/shard_map/while
  343.5 12.5 %fusion.86 = (f32[4,3,128]{2,1,0:T(4,128)S(1)}, f32[4,3,128,3456]{3,2,1,0:T(8,128)}) fusion(pred[4,3456]{1,0:T(4,128)(4,1)S(1)} %bitcast.145, bf16[4,128,3,64]{1,3,2,0:T(8,128)(2,1)S(1)} %bitcast.142, bf16[4,3456,3,64]{1,3,2,0:T(8,128)(2,1)} %reshape.160), kind=kOutput, calls=%fused_computation.3.clone.1 | convolution fusion | flops 695400960 | bytes 26758656 | tf_op jit(solution)/shard_map/while/body/eval_jaxpr/grhd,gkhd->ghrk/dot_general | solution.py:91
  391.3 11.4 %fusion.85 = (bf16[4,27,128,192]{3,2,1,0:T(8,128)(2,1)}, bf16[4,27,128,192]{3,2,1,0:T(8,128)(2,1)}) fusion(bf16[4,27,128,384]{3,2,1,0:T(8,128)(2,1)} %bitcast.141), kind=kLoop, calls=%fused_computation.90.clone.1 | loop fusion | bytes 21233664 | tf_op jit(solution)/shard_map/while/body/eval_jaxpr/slice | solution.py:87
  402.7 13.0 %copy.125 = bf16[4,27,128,192]{2,1,3,0:T(8,128)(2,1)} copy(bf16[4,27,128,192]{3,2,1,0:T(8,128)(2,1)} %get-tuple-element.223) | data formatting | bytes 10616832 | tf_op jit(solution)/shard_map/while
  425.7 13.0 %copy.127 = bf16[4,27,128,192]{2,1,3,0:T(8,128)(2,1)} copy(bf16[4,27,128,192]{3,2,1,0:T(8,128)(2,1)} %get-tuple-element.224) | data formatting | bytes 10616832 | tf_op jit(solution)/shard_map/while
  448.6 12.5 %fusion.86 = (f32[4,3,128]{2,1,0:T(4,128)S(1)}, f32[4,3,128,3456]{3,2,1,0:T(8,128)}) fusion(pred[4,3456]{1,0:T(4,128)(4,1)S(1)} %bitcast.145, bf16[4,128,3,64]{1,3,2,0:T(8,128)(2,1)S(1)} %bitcast.142, bf16[4,3456,3,64]{1,3,2,0:T(8,128)(2,1)} %reshape.160), kind=kOutput, calls=%fused_computation.3.clone.1 | convolution fusion | flops 695400960 | bytes 26758656 | tf_op jit(solution)/shard_map/while/body/eval_jaxpr/grhd,gkhd->ghrk/dot_general | solution.py:91
  496.4 11.4 %fusion.85 = (bf16[4,27,128,192]{3,2,1,0:T(8,128)(2,1)}, bf16[4,27,128,192]{3,2,1,0:T(8,128)(2,1)}) fusion(bf16[4,27,128,384]{3,2,1,0:T(8,128)(2,1)} %bitcast.141), kind=kLoop, calls=%fused_computation.90.clone.1 | loop fusion | bytes 21233664 | tf_op jit(solution)/shard_map/while/body/eval_jaxpr/slice | solution.py:87
  507.8 13.0 %copy.125 = bf16[4,27,128,192]{2,1,3,0:T(8,128)(2,1)} copy(bf16[4,27,128,192]{3,2,1,0:T(8,128)(2,1)} %get-tuple-element.223) | data formatting | bytes 10616832 | tf_op jit(solution)/shard_map/while
  530.8 13.0 %copy.127 = bf16[4,27,128,192]{2,1,3,0:T(8,128)(2,1)} copy(bf16[4,27,128,192]{3,2,1,0:T(8,128)(2,1)} %get-tuple-element.224) | data formatting | bytes 10616832 | tf_op jit(solution)/shard_map/while
  553.6 12.5 %fusion.86 = (f32[4,3,128]{2,1,0:T(4,128)S(1)}, f32[4,3,128,3456]{3,2,1,0:T(8,128)}) fusion(pred[4,3456]{1,0:T(4,128)(4,1)S(1)} %bitcast.145, bf16[4,128,3,64]{1,3,2,0:T(8,128)(2,1)S(1)} %bitcast.142, bf16[4,3456,3,64]{1,3,2,0:T(8,128)(2,1)} %reshape.160), kind=kOutput, calls=%fused_computation.3.clone.1 | convolution fusion | flops 695400960 | bytes 26758656 | tf_op jit(solution)/shard_map/while/body/eval_jaxpr/grhd,gkhd->ghrk/dot_general | solution.py:91
  599.2 34.7 %pmax.7 = f32[3,226]{1,0:T(4,128)S(1)} all-reduce(f32[3,226]{1,0:T(4,128)S(1)} %get-tuple-element.148), channel_id=1, replica_groups=mesh['seq'=16,'head'=16] {'seq'}, use_global_device_ids=true, to_apply=%region_7.8 | all-reduce | flops 678 | bytes 5424 | tf_op jit(solution)/shard_map/pmax | solution.py:135
  642.2 33.3 %psum.15 = f32[3,226]{1,0:T(4,128)S(1)} all-reduce(f32[3,226]{1,0:T(4,128)S(1)} %fusion.23), channel_id=1, replica_groups=mesh['seq'=16,'head'=16] {'seq'}, use_global_device_ids=true, to_apply=%region_11.12 | all-reduce | flops 678 | bytes 5424 | tf_op jit(solution)/shard_map/psum | solution.py:144
  675.7 56.6 %all-reduce.2.cloned.1.call-done = f32[226,3,64]{0,2,1:T(8,128)} async-done(((f32[226,3,64]{0,2,1:T(8,128)}), f32[226,3,64]{0,2,1:T(8,128)}) %all-reduce.2.cloned.1.call-update) | async-done | bytes 173584 | tf_op jit(solution)/shard_map/psum | solution.py:144
  (171 shorter events, 320.7 us)
Async XLA Ops:
  7.2 123.7 %copy-start = (bf16[226,192]{0,1:T(8,128)(2,1)S(1)}, bf16[226,192]{0,1:T(8,128)(2,1)}, u32[]{:S(2)}) copy-start(bf16[226,192]{0,1:T(8,128)(2,1)} %param.14) | copy-start | bytes 260356
  29.4 30.3 %all-to-all-start.1 = ((bf16[16,2,12288]{2,1,0:T(2,128)(2,1)}), bf16[16,2,12288]{2,1,0:T(2,128)(2,1)S(1)}, u32[]{:S(2)}, u32[]{:S(2)}) async-start(bf16[16,2,12288]{2,1,0:T(2,128)(2,1)} %reshape.145), calls=%async_computation.1 | async-start | bytes 1572864 | tf_op jit(solution)/shard_map/all_to_all | solution.py:166
  59.8 28.2 %all-to-all-start = ((bf16[16,2,12288]{2,1,0:T(2,128)(2,1)}), bf16[16,2,12288]{2,1,0:T(2,128)(2,1)}, u32[]{:S(2)}, u32[]{:S(2)}) async-start(bf16[16,2,12288]{2,1,0:T(2,128)(2,1)} %reshape.147), calls=%async_computation | async-start | bytes 1572864 | tf_op jit(solution)/shard_map/all_to_all | solution.py:165
  68.1 54.6 %copy-start.1 = (bf16[1,128,3072]{1,2,0:T(8,128)(2,1)}, bf16[1,128,3072]{1,2,0:T(8,128)(2,1)S(1)}, u32[]{:S(2)}) copy-start(bf16[1,128,3072]{1,2,0:T(8,128)(2,1)S(1)} %copy.98) | copy-start | bytes 2359300
  92.4 38.3 %copy-start.14 = (s32[226]{0:T(256)S(1)}, s32[226]{0:T(256)}, u32[]{:S(2)}) copy-start(s32[226]{0:T(256)} %param.19) | copy-start | bytes 2716
  92.4 38.3 %copy-start.12 = (s32[27,3]{0,1:T(4,128)S(1)}, s32[27,3]{0,1:T(4,128)}, u32[]{:S(2)}) copy-start(s32[27,3]{0,1:T(4,128)} %param.17) | copy-start | bytes 976
  92.5 38.3 %copy-start.11 = (s32[16,27]{1,0:T(8,128)S(1)}, s32[16,27]{1,0:T(8,128)}, u32[]{:S(2)}) copy-start(s32[16,27]{1,0:T(8,128)} %param.18) | copy-start | bytes 5188
  92.5 38.8 %copy-start.5 = (bf16[226,192]{0,1:T(8,128)(2,1)S(1)}, bf16[226,192]{0,1:T(8,128)(2,1)}, u32[]{:S(2)}) copy-start(bf16[226,192]{0,1:T(8,128)(2,1)} %param.15) | copy-start | bytes 260356
  92.6 65.9 %collective-permute-start.1 = (bf16[1,16,128,384]{2,3,1,0:T(8,128)(2,1)S(1)}, bf16[1,16,128,384]{2,3,1,0:T(8,128)(2,1)}, u32[]{:S(2)}, u32[]{:S(2)}) collective-permute-start(bf16[1,16,128,384]{2,3,1,0:T(8,128)(2,1)S(1)} %maximum_bitcast_fusion), channel_id=1, source_target_pairs={{16,0},{32,16},{48,32},{64,48},{80,64},{96,80},{112,96},{128,112},... | collective-permute-start | bytes 4718600 | tf_op jit(solution)/shard_map/ppermute | solution.py:27
  97.5 61.0 %collective-permute-start = (bf16[1,16,128,384]{2,3,1,0:T(8,128)(2,1)S(1)}, bf16[1,16,128,384]{2,3,1,0:T(8,128)(2,1)}, u32[]{:S(2)}, u32[]{:S(2)}) collective-permute-start(bf16[1,16,128,384]{2,3,1,0:T(8,128)(2,1)S(1)} %maximum_bitcast_fusion), channel_id=1, source_target_pairs={{0,16},{16,32},{32,48},{48,64},{64,80},{80,96},{96,112},{112,128},... | collective-permute-start | bytes 4718600 | tf_op jit(solution)/shard_map/ppermute | solution.py:26
  125.5 25.8 %all-to-all-start.2 = ((bf16[16,2,12288]{2,1,0:T(2,128)(2,1)}), bf16[16,2,12288]{2,1,0:T(2,128)(2,1)S(1)}, u32[]{:S(2)}, u32[]{:S(2)}) async-start(bf16[16,2,12288]{2,1,0:T(2,128)(2,1)} %reshape.149), calls=%async_computation.2 | async-start | bytes 1572864 | tf_op jit(solution)/shard_map/all_to_all | solution.py:164
  168.9 426.0 %copy-start.6 = (bf16[2048,3,64]{0,2,1:T(8,128)(2,1)S(1)}, bf16[2048,3,64]{0,2,1:T(8,128)(2,1)}, u32[]{:S(2)}) copy-start(bf16[2048,3,64]{0,2,1:T(8,128)(2,1)} %reshape.130) | copy-start | bytes 2359300
  169.2 46.3 %copy-start.3 = (bf16[16,128,192]{1,2,0:T(8,128)(2,1)}, bf16[16,128,192]{1,2,0:T(8,128)(2,1)S(1)}, u32[]{:S(2)}) copy-start(bf16[16,128,192]{1,2,0:T(8,128)(2,1)S(1)} %get-tuple-element.265) | copy-start | bytes 2359300 | tf_op jit(solution)/shard_map/while
  262.8 11.3 %copy-start.4 = (bf16[16,128,192]{1,2,0:T(8,128)(2,1)S(1)}, bf16[16,128,192]{1,2,0:T(8,128)(2,1)}, u32[]{:S(2)}) copy-start(bf16[16,128,192]{1,2,0:T(8,128)(2,1)} %copy-done.3) | copy-start | bytes 2359300 | tf_op jit(solution)/shard_map/while
  274.1 46.5 %copy-start.3 = (bf16[16,128,192]{1,2,0:T(8,128)(2,1)}, bf16[16,128,192]{1,2,0:T(8,128)(2,1)S(1)}, u32[]{:S(2)}) copy-start(bf16[16,128,192]{1,2,0:T(8,128)(2,1)S(1)} %get-tuple-element.265) | copy-start | bytes 2359300 | tf_op jit(solution)/shard_map/while
  367.9 11.3 %copy-start.4 = (bf16[16,128,192]{1,2,0:T(8,128)(2,1)S(1)}, bf16[16,128,192]{1,2,0:T(8,128)(2,1)}, u32[]{:S(2)}) copy-start(bf16[16,128,192]{1,2,0:T(8,128)(2,1)} %copy-done.3) | copy-start | bytes 2359300 | tf_op jit(solution)/shard_map/while
  379.2 46.5 %copy-start.3 = (bf16[16,128,192]{1,2,0:T(8,128)(2,1)}, bf16[16,128,192]{1,2,0:T(8,128)(2,1)S(1)}, u32[]{:S(2)}) copy-start(bf16[16,128,192]{1,2,0:T(8,128)(2,1)S(1)} %get-tuple-element.265) | copy-start | bytes 2359300 | tf_op jit(solution)/shard_map/while
  473.0 11.3 %copy-start.4 = (bf16[16,128,192]{1,2,0:T(8,128)(2,1)S(1)}, bf16[16,128,192]{1,2,0:T(8,128)(2,1)}, u32[]{:S(2)}) copy-start(bf16[16,128,192]{1,2,0:T(8,128)(2,1)} %copy-done.3) | copy-start | bytes 2359300 | tf_op jit(solution)/shard_map/while
  484.3 46.4 %copy-start.3 = (bf16[16,128,192]{1,2,0:T(8,128)(2,1)}, bf16[16,128,192]{1,2,0:T(8,128)(2,1)S(1)}, u32[]{:S(2)}) copy-start(bf16[16,128,192]{1,2,0:T(8,128)(2,1)S(1)} %get-tuple-element.265) | copy-start | bytes 2359300 | tf_op jit(solution)/shard_map/while
  578.1 11.3 %copy-start.4 = (bf16[16,128,192]{1,2,0:T(8,128)(2,1)S(1)}, bf16[16,128,192]{1,2,0:T(8,128)(2,1)}, u32[]{:S(2)}) copy-start(bf16[16,128,192]{1,2,0:T(8,128)(2,1)} %copy-done.3) | copy-start | bytes 2359300 | tf_op jit(solution)/shard_map/while
  589.4 44.6 %copy-start.10 = (f32[3,226]{1,0:T(4,128)S(1)}, f32[3,226]{1,0:T(4,128)}, u32[]{:S(2)}) copy-start(f32[3,226]{1,0:T(4,128)} %get-tuple-element.150) | copy-start | bytes 8140
  589.4 144.7 %all-to-all-start.3 = ((bf16[16,128,192]{1,2,0:T(8,128)(2,1)}), bf16[16,128,192]{1,2,0:T(8,128)(2,1)S(1)}, u32[]{:S(2)}, u32[]{:S(2)}) async-start(bf16[16,128,192]{1,2,0:T(8,128)(2,1)} %bitcast.163), calls=%async_computation.3 | async-start | bytes 1572864 | tf_op jit(solution)/shard_map/all_to_all | solution.py:172
  594.7 137.6 %all-reduce.2.cloned.1.call-start = ((), (), s32[]{:S(2)}) async-start(), calls=%async_computation.4 | async-start | bytes 393216 | tf_op jit(solution)/shard_map/psum | solution.py:144
  633.9 41.6 %copy-start.7 = (f32[3,226,226]{1,2,0:T(8,128)S(1)}, f32[3,226,226]{1,2,0:T(8,128)}, u32[]{:S(2)}) copy-start(f32[3,226,226]{1,2,0:T(8,128)} %get-tuple-element.151) | copy-start | bytes 1838740
  (4 other events, 22.9 us)
Sparse Core Ops, SparseCore 0:
  638.6 93.6 all-reduce.1
where the time goes:
time: 756 us; the launch traced here: 743 us
  local copies, waits for them, and re-layouts  316 us (42%)
  matrix products  109 us (14%)
  other arithmetic  103 us (14%)
  waiting for transfers between devices  94.8 us (13%)
  blocking collectives  68 us (9%)
  starting transfers between devices  33.5 us (4%)
  between operations  14.8 us (2%)
    while x32, local copies, waits for them, and re-layouts  104 us
    psum x1, waiting for transfers between devices, text_attention(): lax.psum((video_mixed, jnp.sum(video_exp, -1)), 'seq')  56.6 us
    unnamed x3, other arithmetic  52.8 us
    dot_general x4, matrix products, one_group(): jnp.einsum('grhd,gkhd->ghrk', query_block, nearby_k, preferred_element_ty...  50.1 us
    slice x4, local copies, waits for them, and re-layouts, one_group(): nearby[..., :feature_width].reshape(group_size, NB * TILE, head_count, HD)  45.6 us
    dot_general x4, matrix products, one_group(): jnp.einsum('ghrk,gkhd->grhd', video_exp.astype(jnp.bfloat16), nearby_v, p...  44.8 us
    reduce_sum x8, other arithmetic, one_group(): totals = jnp.sum(video_exp, -1) + jnp.sum(own_exp, -1)  42.3 us
    gather x4, local copies, waits for them, and re-layouts, one_group(): nearby = kv_flat[target_block]  42 us
  transfers between devices with their start and end apart: 7, of which 3 were waited for; matrix products, arithmetic and copies ran while one was open for 10% of the time, Pallas kernels for 0%

commit v1 on v0

v1 whole, which is shorter than its diff:
```python
import functools
import math

import jax
import jax.numpy as jnp
from jax import lax
from jax.experimental import pallas as pl
from jax.experimental.pallas import tpu as pltpu
from jax.sharding import PartitionSpec as P

HD = 64
TEXT = 226
TEXT_ROWS = 256
TILE = 128
HALF = TILE // 2
TH = 4
TW = 4
LAYER = TH * TW
NB = 27
GROUP = 4
SLOTS = 28
LANES = 128
NEG_FILL = -jnp.inf
FACTOR = math.log2(math.e) / math.sqrt(HD)
BF16 = jnp.bfloat16
F32 = jnp.float32
VMEM_LIMIT = 56 * 1024 * 1024


def low_lanes(rows):
    return lax.broadcasted_iota(jnp.int32, (rows, LANES), 1) < HD


def swapped(block):
    return jnp.concatenate([block[:, HD:], block[:, :HD]], axis=1)


def dot_nt(a, b):
    return lax.dot_general(a, b, (((1,), (1,)), ((), ())), preferred_element_type=F32)


def dot_nn(a, b):
    return lax.dot_general(a, b, (((1,), (0,)), ((), ())), preferred_element_type=F32)


def pack_kernel(q_ref, k_ref, v_ref, single_ref, pair_kv_ref, pair_q_ref):
    low = low_lanes(HALF)
    for n, ref in enumerate((k_ref, v_ref, q_ref)):
        middle = ref[:, LANES : 2 * LANES].astype(F32)
        upper, lower = middle[:HALF], middle[HALF:]
        rows = slice(n * HALF, (n + 1) * HALF)
        single_ref[0, rows, :] = jnp.where(low, upper, swapped(lower)).astype(BF16)
        single_ref[1, rows, :] = jnp.where(low, swapped(upper), lower).astype(BF16)
        first, last = ref[:, :LANES], ref[:, 2 * LANES :]
        if n < 2:
            rows = slice(n * TILE, (n + 1) * TILE)
            pair_kv_ref[0, rows, :] = first
            pair_kv_ref[1, rows, :] = last
        else:
            pair_q_ref[0] = first
            pair_q_ref[1] = last


def pack(video_q, video_k, video_v):
    groups = video_q.shape[1] // (3 * HD)
    block = pl.BlockSpec((TILE, 3 * LANES), lambda i: (0, i))
    rows = (3 * HALF, 2 * TILE, TILE)
    return pl.pallas_call(
        pack_kernel,
        grid=(groups // 2,),
        in_specs=[block] * 3,
        out_specs=[pl.BlockSpec((2, r, LANES), lambda i: (i, 0, 0)) for r in rows],
        out_shape=[jax.ShapeDtypeStruct((groups, r, LANES), BF16) for r in rows],
        cost_estimate=pl.CostEstimate(flops=0, bytes_accessed=4 * 3 * video_q.size, transcendentals=0),
        name="pack",
    )(video_q, video_k, video_v)


def unpack_kernel(single_ref, pair_ref, out_ref):
    low = low_lanes(HALF)
    even = single_ref[0].astype(F32)
    odd = single_ref[1].astype(F32)
    out_ref[:, :LANES] = pair_ref[0]
    out_ref[:HALF, LANES : 2 * LANES] = jnp.where(low, even, swapped(odd)).astype(BF16)
    out_ref[HALF:, LANES : 2 * LANES] = jnp.where(low, swapped(even), odd).astype(BF16)
    out_ref[:, 2 * LANES :] = pair_ref[1]


def unpack(single, pair):
    groups = single.shape[0]
    return pl.pallas_call(
        unpack_kernel,
        grid=(groups // 2,),
        in_specs=[
            pl.BlockSpec((2, HALF, LANES), lambda i: (i, 0, 0)),
            pl.BlockSpec((2, TILE, LANES), lambda i: (i, 0, 0)),
        ],
        out_specs=pl.BlockSpec((TILE, 3 * LANES), lambda i: (0, i)),
        out_shape=jax.ShapeDtypeStruct((TILE, groups * 3 * HD), BF16),
        name="unpack",
    )(single, pair)


def neighbour_lists(offsets, block_mask):
    spots = jnp.arange(LAYER, dtype=jnp.int32)
    layer = lax.axis_index("seq") + offsets[None, :, 0]
    moved_h = spots[:, None] // TW + offsets[None, :, 1]
    moved_w = spots[:, None] % TW + offsets[None, :, 2]
    live = (
        (moved_h >= 0)
        & (moved_h < TH)
        & (moved_w >= 0)
        & (moved_w < TW)
        & (layer >= 0)
        & (layer < lax.axis_size("seq"))
        & (block_mask == 1)
    )
    target = ((offsets[None, :, 0] + 1) * TH + moved_h) * TW + moved_w
    ones = live.astype(jnp.int32)
    earlier = jnp.arange(NB)[:, None] < jnp.arange(NB)[None, :]
    place = jnp.sum(jnp.where(earlier[None], ones[:, :, None], 0), axis=1)
    slots = jnp.arange(SLOTS, dtype=jnp.int32)
    chosen = live[:, :, None] & (place[:, :, None] == slots[None, None, :])
    table = jnp.sum(jnp.where(chosen, target[:, :, None], 0), axis=1)
    counts = jnp.sum(ones, axis=1)
    table = jnp.where(slots[None, :] < counts[:, None], table, table[:, :1])
    return counts, table.reshape(-1)


def attend_rows(queries, text_k, text_v, text_bias, count, keys_of, values_of, score_ref, top_ref, total_ref, mixed_ref):
    scores = dot_nt(queries, text_k) + text_bias
    left, right = scores[:, :LANES], scores[:, LANES:]
    score_ref[0] = left
    score_ref[1] = right
    top_ref[...] = jnp.maximum(left, right)
    groups = (count + (GROUP - 1)) // GROUP

    def first_pass(g, carry):
        keys = jnp.concatenate([keys_of(g * GROUP + j) for j in range(GROUP)], axis=0)
        found = dot_nt(queries, keys)
        parts = [found[:, j * LANES : (j + 1) * LANES] for j in range(GROUP)]
        for j in range(GROUP):
            score_ref[2 + g * GROUP + j] = parts[j]
        top_ref[...] = jnp.maximum(
            top_ref[...], jnp.maximum(jnp.maximum(parts[0], parts[1]), jnp.maximum(parts[2], parts[3]))
        )
        return carry

    lax.fori_loop(0, groups, first_pass, 0)
    for j in range(GROUP - 1):

        @pl.when(count + j < groups * GROUP)
        def _():
            score_ref[2 + count + j] = jnp.full(score_ref.shape[1:], NEG_FILL, F32)

    highest = jnp.max(top_ref[...], axis=1, keepdims=True)
    shift = highest * FACTOR
    weights = [jnp.exp2(score_ref[j] * FACTOR - shift) for j in range(2)]
    total_ref[...] = weights[0] + weights[1]
    mixed_ref[...] = dot_nn(jnp.concatenate([w.astype(BF16) for w in weights], axis=1), text_v)

    def second_pass(g, carry):
        parts = [jnp.exp2(score_ref[2 + g * GROUP + j] * FACTOR - shift) for j in range(GROUP)]
        total_ref[...] += (parts[0] + parts[1]) + (parts[2] + parts[3])
        values = jnp.concatenate([values_of(g * GROUP + j) for j in range(GROUP)], axis=0)
        mixed_ref[...] += dot_nn(jnp.concatenate([p.astype(BF16) for p in parts], axis=1), values)
        return carry

    lax.fori_loop(0, groups, second_pass, 0)
    return highest, jnp.sum(total_ref[...], axis=1, keepdims=True)


def spread_single(packed):
    wide = packed.astype(F32)
    return jnp.concatenate([wide, swapped(wide)], axis=0).astype(BF16)


def video_kernel(
    heads, counts_ref, table_ref, q_ref, before_ref, own_ref, after_ref, text_k_ref, text_v_ref, bias_ref, out_ref,
    kv_ref, wide_ref, score_ref, top_ref, total_ref, mixed_ref, sems,
):
    copies = [
        pltpu.make_async_copy(ref, kv_ref.at[pl.ds(n * LAYER, LAYER)], sems.at[n])
        for n, ref in enumerate((before_ref, own_ref, after_ref))
    ]
    for copy in copies:
        copy.start()
    for copy in copies:
        copy.wait()
    if heads == 1:

        def widen(t, carry):
            for n in range(2):
                wide_ref[t, n * TILE : (n + 1) * TILE, :] = spread_single(kv_ref[t, n * HALF : (n + 1) * HALF, :])
            return carry

        lax.fori_loop(0, 3 * LAYER, widen, 0)
        tiles_ref = wide_ref
    else:
        tiles_ref = kv_ref

    def one_tile(i, carry):
        low = low_lanes(TILE)
        if heads == 1:
            wide = q_ref[i].astype(F32)
            block = jnp.concatenate([wide, swapped(wide)], axis=0)
            queries = jnp.where(low, block, 0.0).astype(BF16)
        else:
            block = q_ref[i].astype(F32)
            queries = jnp.concatenate([jnp.where(low, block, 0.0), jnp.where(low, 0.0, block)], axis=0).astype(BF16)
        _, total = attend_rows(
            queries,
            text_k_ref[...],
            text_v_ref[...],
            bias_ref[...],
            counts_ref[i],
            lambda slot: tiles_ref[table_ref[i * SLOTS + slot], :TILE, :],
            lambda slot: tiles_ref[table_ref[i * SLOTS + slot], TILE:, :],
            score_ref,
            top_ref,
            total_ref,
            mixed_ref,
        )
        result = mixed_ref[...] / total
        if heads == 1:
            out_ref[i] = jnp.where(low_lanes(HALF), result[:HALF], swapped(result[HALF:])).astype(BF16)
        else:
            out_ref[i] = jnp.where(low, result[:TILE], result[TILE:]).astype(BF16)
        return carry

    lax.fori_loop(0, LAYER, one_tile, 0)


def video_attention(heads, counts, table, queries, before, own, after, text_k, text_v, text_bias):
    rows = heads * TILE
    smem = pl.BlockSpec(memory_space=pltpu.SMEM)
    vmem = pl.BlockSpec(memory_space=pltpu.VMEM)
    hbm = pl.BlockSpec(memory_space=pl.ANY)
    pairs = 300 * TILE * TILE * heads
    wide_tiles = 3 * LAYER if heads == 1 else 1
    return pl.pallas_call(
        functools.partial(video_kernel, heads),
        in_specs=[smem, smem, vmem, hbm, hbm, hbm, vmem, vmem, vmem],
        out_specs=vmem,
        out_shape=jax.ShapeDtypeStruct(queries.shape, BF16),
        scratch_shapes=[
            pltpu.VMEM((3 * LAYER,) + own.shape[1:], BF16),
            pltpu.VMEM((wide_tiles, 2 * TILE, LANES), BF16),
            pltpu.VMEM((2 + SLOTS, rows, LANES), F32),
            pltpu.VMEM((rows, LANES), F32),
            pltpu.VMEM((rows, LANES), F32),
            pltpu.VMEM((rows, LANES), F32),
            pltpu.SemaphoreType.DMA((3,)),
        ],
        compiler_params=pltpu.CompilerParams(vmem_limit_bytes=VMEM_LIMIT),
        cost_estimate=pl.CostEstimate(flops=16 * HD * pairs, bytes_accessed=8 * own.size, transcendentals=pairs),
        name=f"video_attention_{heads}",
    )(counts, table, queries, before, own, after, text_k, text_v, text_bias)


def text_kernel(
    pair_q_ref, pair_kv_ref, pair_k_ref, pair_v_ref, single_q_ref, single_kv_ref, single_k_ref, single_v_ref, bias_ref,
    out_ref, wide_ref, score_ref, top_ref, total_ref, mixed_ref,
):
    def widen(t, carry):
        for n in range(2):
            wide_ref[t, n * TILE : (n + 1) * TILE, :] = spread_single(single_kv_ref[t, n * HALF : (n + 1) * HALF, :])
        return carry

    lax.fori_loop(0, LAYER, widen, 0)
    low = low_lanes(TEXT_ROWS)
    pair_q = pair_q_ref[...].astype(F32)
    single_q = single_q_ref[...].astype(F32)
    tops, totals, sums = [], [], []
    for head in range(3):
        if head < 2:
            queries = jnp.where(low if head == 0 else ~low, pair_q, 0.0).astype(BF16)
            text_k, text_v, tiles_ref = pair_k_ref[...], pair_v_ref[...], pair_kv_ref
        else:
            queries = jnp.where(low, single_q, 0.0).astype(BF16)
            text_k, text_v, tiles_ref = single_k_ref[...], single_v_ref[...], wide_ref
        highest, total = attend_rows(
            queries,
            text_k,
            text_v,
            bias_ref[...],
            LAYER,
            lambda slot: tiles_ref[slot, :TILE, :],
            lambda slot: tiles_ref[slot, TILE:, :],
            score_ref,
            top_ref,
            total_ref,
            mixed_ref,
        )
        tops.append(highest)
        totals.append(total)
        if head == 0:
            out_ref[:, :LANES] = mixed_ref[...]
        elif head == 1:
            out_ref[:, :LANES] = jnp.where(low, out_ref[:, :LANES], mixed_ref[...])
    lane = lax.broadcasted_iota(jnp.int32, (TEXT_ROWS, LANES), 1)
    last = jnp.where(low, mixed_ref[...], 0.0)
    for head in range(3):
        last = jnp.where(lane == HD + head, tops[head], last)
        last = jnp.where(lane == HD + 3 + head, totals[head], last)
    out_ref[:, LANES:] = last


def text_partial(pair_q, pair_kv, pair_k, pair_v, single_q, single_kv, single_k, single_v, bias):
    vmem = pl.BlockSpec(memory_space=pltpu.VMEM)
    pairs = 3 * TEXT_ROWS * (LAYER + 2) * TILE
    return pl.pallas_call(
        text_kernel,
        in_specs=[vmem] * 9,
        out_specs=vmem,
        out_shape=jax.ShapeDtypeStruct((TEXT_ROWS, 2 * LANES), F32),
        scratch_shapes=[
            pltpu.VMEM((LAYER, 2 * TILE, LANES), BF16),
            pltpu.VMEM((2 + LAYER, TEXT_ROWS, LANES), F32),
            pltpu.VMEM((TEXT_ROWS, LANES), F32),
            pltpu.VMEM((TEXT_ROWS, LANES), F32),
            pltpu.VMEM((TEXT_ROWS, LANES), F32),
        ],
        compiler_params=pltpu.CompilerParams(vmem_limit_bytes=VMEM_LIMIT),
        cost_estimate=pl.CostEstimate(flops=16 * HD * pairs, bytes_accessed=4 * pair_kv.size, transcendentals=pairs),
        name="text_partial",
    )(pair_q, pair_kv, pair_k, pair_v, single_q, single_kv, single_k, single_v, bias)


def combine_kernel(parts_ref, pair_ref, single_ref):
    parts = parts_ref[...]
    outs = []
    for head in range(3):
        tops = parts[:, :, LANES + HD + head : LANES + HD + head + 1]
        totals = parts[:, :, LANES + HD + 3 + head : LANES + HD + 4 + head]
        weight = jnp.exp2((tops - jnp.max(tops, axis=0, keepdims=True)) * FACTOR)
        mixed = parts[:, :, :LANES] if head < 2 else parts[:, :, LANES:]
        outs.append(jnp.sum(mixed * weight, axis=0) / jnp.sum(totals * weight, axis=0))
    low = low_lanes(outs[0].shape[0])
    pair_ref[...] = jnp.where(low, outs[0], outs[1]).astype(BF16)
    single_ref[...] = jnp.where(low, outs[2], 0.0).astype(BF16)


def combine(parts):
    rows = parts.shape[1]
    vmem = pl.BlockSpec(memory_space=pltpu.VMEM)
    return pl.pallas_call(
        combine_kernel,
        in_specs=[vmem],
        out_specs=[vmem, vmem],
        out_shape=[jax.ShapeDtypeStruct((rows, LANES), BF16)] * 2,
        name="text_combine",
    )(parts)


def exchange(blocks, axis):
    return lax.all_to_all(blocks, axis, split_axis=0, concat_axis=0, tiled=True)


def both_sides(layer):
    count = lax.axis_size("seq")
    up = [(i, i + 1) for i in range(count - 1)]
    down = [(i + 1, i) for i in range(count - 1)]
    return lax.ppermute(layer, "seq", up), lax.ppermute(layer, "seq", down)


def body(video_q, video_k, video_v, text_q, text_k, text_v, offsets, block_mask, text_mask):
    seq_count = lax.axis_size("seq")
    odd = lax.axis_index("head") % 2 == 1
    counts, table = neighbour_lists(offsets, block_mask)

    def split_text(text):
        grown = jnp.pad(text, ((0, TEXT_ROWS - TEXT), (0, 0)))
        pair = jnp.where(odd, grown[:, HD:], grown[:, : 2 * HD])
        single = jnp.where(odd, grown[:, :HD], grown[:, 2 * HD :])
        return pair, jnp.pad(single, ((0, 0), (0, LANES - HD)))

    (pair_tq, single_tq), (pair_tk, single_tk), (pair_tv, single_tv) = map(split_text, (text_q, text_k, text_v))
    text_live = jnp.pad(text_mask, (0, TEXT_ROWS - TEXT)) == 1
    bias = jnp.where(text_live, 0.0, NEG_FILL).astype(F32)[None, :]
    own_bias = jnp.where(lax.axis_index("seq") == 0, bias, NEG_FILL)

    single, pair_kv, pair_q = pack(video_q, video_k, video_v)
    single = exchange(single, "head")
    pair_kv = exchange(pair_kv, "head")
    pair_q = exchange(pair_q, "head")
    single_kv, single_q = single[:, : 2 * HALF], single[:, 2 * HALF :]
    single_before, single_after = both_sides(single_kv)
    pair_before, pair_after = both_sides(pair_kv)

    single_out = video_attention(
        1, counts, table, single_q, single_before, single_kv, single_after, single_tk, single_tv, bias
    )
    single_back = exchange(single_out, "head")
    partial = text_partial(
        pair_tq, pair_kv, pair_tk, pair_tv, single_tq, single_kv, single_tk, single_tv, own_bias
    )
    pair_out = video_attention(2, counts, table, pair_q, pair_before, pair_kv, pair_after, pair_tk, pair_tv, bias)
    pair_back = exchange(pair_out, "head")
    video_out = unpack(single_back, pair_back)

    rows = TEXT_ROWS // seq_count
    parts = exchange(partial.reshape(seq_count, rows, 2 * LANES), "seq")
    text_pair, text_single = combine(parts)
    mine = jnp.concatenate([text_pair, text_single], axis=1)
    whole = exchange(jnp.broadcast_to(mine[None], (seq_count,) + mine.shape), "seq").reshape(TEXT_ROWS, 2 * LANES)
    pair_part, single_part = whole[:TEXT, :LANES], whole[:TEXT, LANES : LANES + HD]
    text_out = jnp.where(
        odd,
        jnp.concatenate([single_part, pair_part], axis=1),
        jnp.concatenate([pair_part, single_part], axis=1),
    )
    return video_out, text_out


def solution(mesh):
    return jax.shard_map(
        body,
        mesh=mesh,
        in_specs=(
            P(("seq", "head"), None),
            P(("seq", "head"), None),
            P(("seq", "head"), None),
            P(None, "head"),
            P(None, "head"),
            P(None, "head"),
            P(),
            P("seq", None),
            P(),
        ),
        out_specs=(P(("seq", "head"), None), P(None, "head")),
        check_vma=False,
    )
```

time: 756 us -> 271 us (0.36)
  the two profiles are of different devices: /device:TPU:2 before, /device:TPU:3 now
where the time goes in v1:
time: 271 us; the launch traced here: 268 us
  Pallas kernels  106 us (39%)
  waiting for transfers between devices  62.6 us (23%)
  starting transfers between devices  50.2 us (19%)
  blocking collectives  32.1 us (12%)
  local copies, waits for them, and re-layouts  12.2 us (5%)
  other arithmetic  3.66 us (1%)
    pallas_call x2, Pallas kernels, video_attention(): pl.pallas_call(functools.partial(video_kernel, heads), in_specs=[smem, sm...  82.4 us
    all_to_all x6, waiting for transfers between devices, exchange(): return lax.all_to_all(blocks, axis, split_axis=0, concat_axis=0, tiled=True)  42.7 us
    all_to_all x6, starting transfers between devices, exchange(): return lax.all_to_all(blocks, axis, split_axis=0, concat_axis=0, tiled=True)  37 us
    all_to_all x1, blocking collectives, exchange(): return lax.all_to_all(blocks, axis, split_axis=0, concat_axis=0, tiled=True)  32.1 us
    ppermute x4, waiting for transfers between devices, both_sides(): return (lax.ppermute(layer, 'seq', up), lax.ppermute(layer, 'seq', down))  19.9 us
    ppermute x4, starting transfers between devices, both_sides(): return (lax.ppermute(layer, 'seq', up), lax.ppermute(layer, 'seq', down))  13.1 us
    pallas_call x1, Pallas kernels, text_partial(): pl.pallas_call(text_kernel, in_specs=[vmem] * 9, out_specs=vmem, out_shap...  10.5 us
    unnamed x32, local copies, waits for them, and re-layouts  6.91 us
  transfers between devices with their start and end apart: 10, of which 5 were waited for; matrix products, arithmetic and copies ran while one was open for 4% of the time, Pallas kernels for 32%

profile of v1, /device:TPU:3, one launch (start us, length us, event | category | flops | bytes accessed | tf_op | source)
XLA Modules:
  0.0 267.8 jit_solution(5284399276673892220)
XLA Ops:
  0.6 6.0 %pack.1 = (bf16[16,192,128]{2,1,0:T(8,128)(2,1)}, bf16[16,256,128]{2,1,0:T(8,128)(2,1)}, bf16[16,128,128]{2,1,0:T(8,128)(2,1)}) custom-call(bf16[128,3072]{1,0:T(8,128)(2,1)} %q_ref.1, bf16[128,3072]{1,0:T(8,128)(2,1)} %k_ref.1, bf16[128,3072]{1,0:T(8,128)(2,1)} %v_ref.1), custom_call_target="tpu_custom_call" | custom-call | bytes 4718592 | tf_op jit(solution)/shard_map/pack/pallas_call | solution.py:68
  6.6 32.1 %all_to_all.35 = bf16[16,192,128]{2,1,0:T(8,128)(2,1)S(1)} all-to-all(bf16[16,192,128]{2,1,0:T(8,128)(2,1)} %get-tuple-element.7), channel_id=1, replica_groups=mesh['seq'=16,'head'=16] {'head'}, dimensions={0} | all-to-all | bytes 1572864 | tf_op jit(solution)/shard_map/all_to_all | solution.py:357
  38.7 3.7 %all-to-all-start.3 = ((bf16[16,256,128]{2,1,0:T(8,128)(2,1)}), bf16[16,256,128]{2,1,0:T(8,128)(2,1)S(1)}, u32[]{:S(2)}, u32[]{:S(2)}) async-start(bf16[16,256,128]{2,1,0:T(8,128)(2,1)} %get-tuple-element.9), calls=%async_computation.3 | async-start | bytes 2097152 | tf_op jit(solution)/shard_map/all_to_all | solution.py:357
  49.1 0.8 slice.84.own_ref.single_kv_ref
  49.9 19.7 %all-to-all-done.3.own_ref.pair_kv_ref = bf16[16,256,128]{2,1,0:T(8,128)(2,1)S(1)} async-done(((bf16[16,256,128]{2,1,0:T(8,128)(2,1)}), bf16[16,256,128]{2,1,0:T(8,128)(2,1)S(1)}, u32[]{:S(2)}, u32[]{:S(2)}) %all-to-all-start.3) | async-done | bytes 1048608 | tf_op jit(solution)/shard_map/all_to_all | solution.py:357
  69.7 1.0 copy-done.1
  70.7 10.5 %text_partial.1 = f32[256,256]{1,0:T(8,128)} custom-call(bf16[256,128]{1,0:T(8,128)(2,1)} %fusion.5.pair_q_ref, bf16[16,256,128]{2,1,0:T(8,128)(2,1)} %copy-done.1, bf16[256,128]{1,0:T(8,128)(2,1)} %get-tuple-element.31.text_k_ref.pair_k_ref, bf16[256,128]{1,0:T(8,128)(2,1)} %get-tuple-element.32.text_v_ref.pair_v_ref, bf16[256,128]{1,0:T(8,128)(2,1)} %pad.30.single_q_ref, ...), custom_call_target="tpu_custom_call" | custom-call | flops 1811939328 | bytes 2097152 | tf_op jit(solution)/shard_map/text_partial/pallas_call | solution.py:312
  81.2 7.0 %all-to-all-start.5 = ((f32[16,16,256]{2,1,0:T(8,128)}), f32[16,16,256]{2,1,0:T(8,128)S(1)}, u32[]{:S(2)}, u32[]{:S(2)}) async-start(f32[16,16,256]{2,1,0:T(8,128)} %bitcast.17), calls=%async_computation.5 | async-start | bytes 524288 | tf_op jit(solution)/shard_map/all_to_all | solution.py:357
  88.5 6.5 %all-to-all-done.5.parts_ref = f32[16,16,256]{2,1,0:T(8,128)S(1)} async-done(((f32[16,16,256]{2,1,0:T(8,128)}), f32[16,16,256]{2,1,0:T(8,128)S(1)}, u32[]{:S(2)}, u32[]{:S(2)}) %all-to-all-start.5) | async-done | bytes 262176 | tf_op jit(solution)/shard_map/all_to_all | solution.py:357
  95.7 4.5 %all-to-all-start.2 = ((bf16[16,128,128]{2,1,0:T(8,128)(2,1)}), bf16[16,128,128]{2,1,0:T(8,128)(2,1)S(1)}, u32[]{:S(2)}, u32[]{:S(2)}) async-start(bf16[16,128,128]{2,1,0:T(8,128)(2,1)} %get-tuple-element.8), calls=%async_computation.2 | async-start | bytes 1048576 | tf_op jit(solution)/shard_map/all_to_all | solution.py:357
  100.6 3.8 %collective-permute-start.3 = (bf16[16,256,128]{2,1,0:T(8,128)(2,1)S(1)}, bf16[16,256,128]{2,1,0:T(8,128)(2,1)}, u32[]{:S(2)}, u32[]{:S(2)}) collective-permute-start(bf16[16,256,128]{2,1,0:T(8,128)(2,1)S(1)} %copy-done.2), channel_id=1, source_target_pairs={{16,0},{32,16},{48,32},{64,48},{80,64},{96,80},{112,96},{128,112},... | collective-permute-start | bytes 3145736 | tf_op jit(solution)/shard_map/ppermute | solution.py:364
  104.5 1.9 collective-permute-start.2
  106.7 5.5 %collective-permute-start.1 = (bf16[16,128,128]{2,1,0:T(8,128)(2,1)S(1)}, bf16[16,128,128]{2,1,0:T(8,128)(2,1)}, u32[]{:S(2)}, u32[]{:S(2)}) collective-permute-start(bf16[16,128,128]{2,1,0:T(8,128)(2,1)S(1)} %copy-done.5), channel_id=1, source_target_pairs={{16,0},{32,16},{48,32},{64,48},{80,64},{96,80},{112,96},{128,112},... | collective-permute-start | bytes 1572872 | tf_op jit(solution)/shard_map/ppermute | solution.py:364
  112.1 1.9 collective-permute-start
  116.1 2.0 text_combine.1
  119.6 5.8 %all-to-all-start.6 = ((bf16[16,16,256]{2,1,0:T(8,128)(2,1)}), bf16[16,16,256]{2,1,0:T(8,128)(2,1)S(1)}, u32[]{:S(2)}, u32[]{:S(2)}) async-start(bf16[16,16,256]{2,1,0:T(8,128)(2,1)} %broadcast_in_dim.83), calls=%async_computation.6 | async-start | bytes 262144 | tf_op jit(solution)/shard_map/all_to_all | solution.py:357
  125.4 14.2 %collective-permute-done.1.after_ref = bf16[16,128,128]{2,1,0:T(8,128)(2,1)} collective-permute-done((bf16[16,128,128]{2,1,0:T(8,128)(2,1)S(1)}, bf16[16,128,128]{2,1,0:T(8,128)(2,1)}, u32[]{:S(2)}, u32[]{:S(2)}) %collective-permute-start.1) | collective-permute-done | bytes 524320 | tf_op jit(solution)/shard_map/ppermute | solution.py:364
  139.6 5.7 %collective-permute-done.before_ref = bf16[16,128,128]{2,1,0:T(8,128)(2,1)} collective-permute-done((bf16[16,128,128]{2,1,0:T(8,128)(2,1)S(1)}, bf16[16,128,128]{2,1,0:T(8,128)(2,1)}, u32[]{:S(2)}, u32[]{:S(2)}) %collective-permute-start) | collective-permute-done | bytes 524320 | tf_op jit(solution)/shard_map/ppermute | solution.py:364
  145.3 40.2 %video_attention_1.1 = bf16[16,64,128]{2,1,0:T(8,128)(2,1)} custom-call(s32[16]{0:T(128)} %copy-done.11, s32[448]{0:T(512)} %select_n.103.table_ref, bf16[16,64,128]{2,1,0:T(8,128)(2,1)} %slice.83.q_ref, bf16[16,128,128]{2,1,0:T(8,128)(2,1)} %collective-permute-done.before_ref, bf16[16,128,128]{2,1,0:T(8,128)(2,1)} %slice.84.own_ref.single_kv_ref, ...), custom_call_target="tpu_custom_call" | custom-call | flops 5033164800 | bytes 2097152 | tf_op jit(solution)/shard_map/video_attention_1/pallas_call | solution.py:241
  185.5 8.7 %all-to-all-start.1 = ((bf16[16,64,128]{2,1,0:T(8,128)(2,1)}), bf16[16,64,128]{2,1,0:T(8,128)(2,1)S(1)}, u32[]{:S(2)}, u32[]{:S(2)}) async-start(bf16[16,64,128]{2,1,0:T(8,128)(2,1)} %video_attention_1.1), calls=%async_computation.1 | async-start | bytes 524288 | tf_op jit(solution)/shard_map/all_to_all | solution.py:357
  194.3 42.3 %video_attention_2.1 = bf16[16,128,128]{2,1,0:T(8,128)(2,1)} custom-call(s32[16]{0:T(128)} %copy-done.11, s32[448]{0:T(512)} %select_n.103.table_ref, bf16[16,128,128]{2,1,0:T(8,128)(2,1)} %copy-done.6, bf16[16,256,128]{2,1,0:T(8,128)(2,1)} %collective-permute-done.2.before_ref, bf16[16,256,128]{2,1,0:T(8,128)(2,1)} %copy-done.1, ...), custom_call_target="tpu_custom_call" | custom-call | flops 10066329600 | bytes 4194304 | tf_op jit(solution)/shard_map/video_attention_2/pallas_call | solution.py:241
  237.2 7.2 %all-to-all-start.4 = ((bf16[16,128,128]{2,1,0:T(8,128)(2,1)}), bf16[16,128,128]{2,1,0:T(8,128)(2,1)S(1)}, u32[]{:S(2)}, u32[]{:S(2)}) async-start(bf16[16,128,128]{2,1,0:T(8,128)(2,1)} %video_attention_2.1), calls=%async_computation.4 | async-start | bytes 1048576 | tf_op jit(solution)/shard_map/all_to_all | solution.py:357
  245.3 16.4 %all-to-all-done.4.pair_ref = bf16[16,128,128]{2,1,0:T(8,128)(2,1)S(1)} async-done(((bf16[16,128,128]{2,1,0:T(8,128)(2,1)}), bf16[16,128,128]{2,1,0:T(8,128)(2,1)S(1)}, u32[]{:S(2)}, u32[]{:S(2)}) %all-to-all-start.4) | async-done | bytes 524320 | tf_op jit(solution)/shard_map/all_to_all | solution.py:357
  262.6 5.2 %unpack.1 = bf16[128,3072]{1,0:T(8,128)(2,1)} custom-call(bf16[16,64,128]{2,1,0:T(8,128)(2,1)} %copy-done.4, bf16[16,128,128]{2,1,0:T(8,128)(2,1)} %copy-done), custom_call_target="tpu_custom_call" | custom-call | tf_op jit(solution)/shard_map/unpack/pallas_call | solution.py:91
  (66 shorter events, 14.1 us)
Async XLA Ops:
  38.7 3.7 %copy-start.7 = (bf16[226,192]{0,1:T(8,128)(2,1)S(1)}, bf16[226,192]{0,1:T(8,128)(2,1)}, u32[]{:S(2)}) copy-start(bf16[226,192]{0,1:T(8,128)(2,1)} %param.12) | copy-start | bytes 260356
  38.7 31.0 %all-to-all-start.3 = ((bf16[16,256,128]{2,1,0:T(8,128)(2,1)}), bf16[16,256,128]{2,1,0:T(8,128)(2,1)S(1)}, u32[]{:S(2)}, u32[]{:S(2)}) async-start(bf16[16,256,128]{2,1,0:T(8,128)(2,1)} %get-tuple-element.9), calls=%async_computation.3 | async-start | bytes 2097152 | tf_op jit(solution)/shard_map/all_to_all | solution.py:357
  42.4 0.9 copy-start.8
  43.3 0.9 copy-start.9
  46.3 0.7 copy-start.13
  48.3 0.8 copy-start.12
  69.7 1.0 copy-start.1
  70.7 17.6 %copy-start.10 = (s32[16,27]{1,0:T(8,128)S(1)}, s32[16,27]{1,0:T(8,128)}, u32[]{:S(2)}) copy-start(s32[16,27]{1,0:T(8,128)} %param.16) | copy-start | bytes 5188
  81.2 19.4 %copy-start.2 = (bf16[16,256,128]{2,1,0:T(8,128)(2,1)S(1)}, bf16[16,256,128]{2,1,0:T(8,128)(2,1)}, u32[]{:S(2)}) copy-start(bf16[16,256,128]{2,1,0:T(8,128)(2,1)} %copy-done.1) | copy-start | bytes 3145732
  81.2 13.9 %all-to-all-start.5 = ((f32[16,16,256]{2,1,0:T(8,128)}), f32[16,16,256]{2,1,0:T(8,128)S(1)}, u32[]{:S(2)}, u32[]{:S(2)}) async-start(f32[16,16,256]{2,1,0:T(8,128)} %bitcast.17), calls=%async_computation.5 | async-start | bytes 524288 | tf_op jit(solution)/shard_map/all_to_all | solution.py:357
  95.0 0.7 copy-start.3
  95.1 11.6 %copy-start.5 = (bf16[16,128,128]{2,1,0:T(8,128)(2,1)S(1)}, bf16[16,128,128]{2,1,0:T(8,128)(2,1)}, u32[]{:S(2)}) copy-start(bf16[16,128,128]{2,1,0:T(8,128)(2,1)} %slice.84.own_ref.single_kv_ref) | copy-start | bytes 1572868
  95.7 23.1 %all-to-all-start.2 = ((bf16[16,128,128]{2,1,0:T(8,128)(2,1)}), bf16[16,128,128]{2,1,0:T(8,128)(2,1)S(1)}, u32[]{:S(2)}, u32[]{:S(2)}) async-start(bf16[16,128,128]{2,1,0:T(8,128)(2,1)} %get-tuple-element.8), calls=%async_computation.2 | async-start | bytes 1048576 | tf_op jit(solution)/shard_map/all_to_all | solution.py:357
  100.6 93.6 %collective-permute-start.3 = (bf16[16,256,128]{2,1,0:T(8,128)(2,1)S(1)}, bf16[16,256,128]{2,1,0:T(8,128)(2,1)}, u32[]{:S(2)}, u32[]{:S(2)}) collective-permute-start(bf16[16,256,128]{2,1,0:T(8,128)(2,1)S(1)} %copy-done.2), channel_id=1, source_target_pairs={{16,0},{32,16},{48,32},{64,48},{80,64},{96,80},{112,96},{128,112},... | collective-permute-start | bytes 3145736 | tf_op jit(solution)/shard_map/ppermute | solution.py:364
  104.5 89.8 %collective-permute-start.2 = (bf16[16,256,128]{2,1,0:T(8,128)(2,1)S(1)}, bf16[16,256,128]{2,1,0:T(8,128)(2,1)}, u32[]{:S(2)}, u32[]{:S(2)}) collective-permute-start(bf16[16,256,128]{2,1,0:T(8,128)(2,1)S(1)} %copy-done.2), channel_id=1, source_target_pairs={{0,16},{16,32},{32,48},{48,64},{64,80},{80,96},{96,112},{112,128},... | collective-permute-start | bytes 3145736 | tf_op jit(solution)/shard_map/ppermute | solution.py:364
  106.7 33.0 %collective-permute-start.1 = (bf16[16,128,128]{2,1,0:T(8,128)(2,1)S(1)}, bf16[16,128,128]{2,1,0:T(8,128)(2,1)}, u32[]{:S(2)}, u32[]{:S(2)}) collective-permute-start(bf16[16,128,128]{2,1,0:T(8,128)(2,1)S(1)} %copy-done.5), channel_id=1, source_target_pairs={{16,0},{32,16},{48,32},{64,48},{80,64},{96,80},{112,96},{128,112},... | collective-permute-start | bytes 1572872 | tf_op jit(solution)/shard_map/ppermute | solution.py:364
  112.1 33.2 %collective-permute-start = (bf16[16,128,128]{2,1,0:T(8,128)(2,1)S(1)}, bf16[16,128,128]{2,1,0:T(8,128)(2,1)}, u32[]{:S(2)}, u32[]{:S(2)}) collective-permute-start(bf16[16,128,128]{2,1,0:T(8,128)(2,1)S(1)} %copy-done.5), channel_id=1, source_target_pairs={{0,16},{16,32},{32,48},{48,64},{64,80},{80,96},{96,112},{112,128},... | collective-permute-start | bytes 1572872 | tf_op jit(solution)/shard_map/ppermute | solution.py:364
  114.2 0.5 copy-start.11
  118.9 66.6 %copy-start.6 = (bf16[16,128,128]{2,1,0:T(8,128)(2,1)}, bf16[16,128,128]{2,1,0:T(8,128)(2,1)S(1)}, u32[]{:S(2)}) copy-start(bf16[16,128,128]{2,1,0:T(8,128)(2,1)S(1)} %all-to-all-done.2.q_ref) | copy-start | bytes 1572868
  119.6 65.9 %all-to-all-start.6 = ((bf16[16,16,256]{2,1,0:T(8,128)(2,1)}), bf16[16,16,256]{2,1,0:T(8,128)(2,1)S(1)}, u32[]{:S(2)}, u32[]{:S(2)}) async-start(bf16[16,16,256]{2,1,0:T(8,128)(2,1)} %broadcast_in_dim.83), calls=%async_computation.6 | async-start | bytes 262144 | tf_op jit(solution)/shard_map/all_to_all | solution.py:357
  185.5 51.0 %all-to-all-start.1 = ((bf16[16,64,128]{2,1,0:T(8,128)(2,1)}), bf16[16,64,128]{2,1,0:T(8,128)(2,1)S(1)}, u32[]{:S(2)}, u32[]{:S(2)}) async-start(bf16[16,64,128]{2,1,0:T(8,128)(2,1)} %video_attention_1.1), calls=%async_computation.1 | async-start | bytes 524288 | tf_op jit(solution)/shard_map/all_to_all | solution.py:357
  236.5 0.7 copy-start.4
  237.2 24.5 %all-to-all-start.4 = ((bf16[16,128,128]{2,1,0:T(8,128)(2,1)}), bf16[16,128,128]{2,1,0:T(8,128)(2,1)S(1)}, u32[]{:S(2)}, u32[]{:S(2)}) async-start(bf16[16,128,128]{2,1,0:T(8,128)(2,1)} %video_attention_2.1), calls=%async_computation.4 | async-start | bytes 1048576 | tf_op jit(solution)/shard_map/all_to_all | solution.py:357
  261.8 0.8 copy-start

commit v2 on v1

v2 whole, which is shorter than its diff:
```python
import functools
import math

import jax
import jax.numpy as jnp
from jax import lax
from jax.experimental import pallas as pl
from jax.experimental.pallas import tpu as pltpu
from jax.sharding import PartitionSpec as P

HD = 64
TEXT = 226
TEXT_ROWS = 256
TEXT_KEPT = 256
TILE = 128
TH = 4
TW = 4
LAYER = TH * TW
NB = 27
GROUP = 4
SLOTS = 28
LANES = 128
NEG_FILL = -jnp.inf
FACTOR = math.log2(math.e) / math.sqrt(HD)
BF16 = jnp.bfloat16
F32 = jnp.float32
VMEM_LIMIT = 56 * 1024 * 1024


def low_lanes(rows):
    return lax.broadcasted_iota(jnp.int32, (rows, LANES), 1) < HD


def dot_nt(a, b):
    return lax.dot_general(a, b, (((1,), (1,)), ((), ())), preferred_element_type=F32)


def dot_nn(a, b):
    return lax.dot_general(a, b, (((1,), (0,)), ((), ())), preferred_element_type=F32)


def pack_single_kernel(q_ref, k_ref, v_ref, out_ref, held_ref, sems):
    groups = out_ref.shape[0]

    def copy(n, u):
        ref = (k_ref, v_ref, q_ref)[n]
        return pltpu.make_async_copy(ref.at[:, pl.ds((3 * u + 1) * LANES, LANES)], held_ref.at[n, u], sems.at[n, u])

    parts = [(n, u) for u in range(groups // 2) for n in range(3)]
    for n, u in parts:
        copy(n, u).start()
    for n, u in parts:
        copy(n, u).wait()
        turned = jnp.transpose(held_ref[n, u])
        out_ref[2 * u, n * HD : (n + 1) * HD, :] = turned[:HD]
        out_ref[2 * u + 1, n * HD : (n + 1) * HD, :] = turned[HD:]


def pack_single(video_q, video_k, video_v):
    groups = video_q.shape[1] // (3 * HD)
    return pl.pallas_call(
        pack_single_kernel,
        in_specs=[pl.BlockSpec(memory_space=pl.ANY)] * 3,
        out_specs=pl.BlockSpec(memory_space=pltpu.VMEM),
        out_shape=jax.ShapeDtypeStruct((groups, 3 * HD, LANES), BF16),
        scratch_shapes=[
            pltpu.VMEM((3, groups // 2, TILE, LANES), BF16),
            pltpu.SemaphoreType.DMA((3, groups // 2)),
        ],
        cost_estimate=pl.CostEstimate(flops=0, bytes_accessed=4 * video_q.size, transcendentals=0),
        name="pack_single",
    )(video_q, video_k, video_v)


def pack_pair_kernel(q_ref, k_ref, v_ref, kv_ref, out_q_ref, sems):
    copies = []
    for n, ref in enumerate((k_ref, v_ref, q_ref)):
        for g in range(out_q_ref.shape[0]):
            source = ref.at[:, pl.ds((g // 2 * 3 + g % 2 * 2) * LANES, LANES)]
            target = kv_ref.at[g, pl.ds(n * TILE, TILE)] if n < 2 else out_q_ref.at[g]
            copies.append(pltpu.make_async_copy(source, target, sems.at[n, g]))
    for copy in copies:
        copy.start()
    for copy in copies:
        copy.wait()


def pack_pair(video_q, video_k, video_v):
    groups = video_q.shape[1] // (3 * HD)
    any_space = pl.BlockSpec(memory_space=pl.ANY)
    return pl.pallas_call(
        pack_pair_kernel,
        in_specs=[any_space] * 3,
        out_specs=[pl.BlockSpec(memory_space=pltpu.VMEM)] * 2,
        out_shape=[jax.ShapeDtypeStruct((groups, r, LANES), BF16) for r in (2 * TILE, TILE)],
        scratch_shapes=[pltpu.SemaphoreType.DMA((3, groups))],
        cost_estimate=pl.CostEstimate(flops=0, bytes_accessed=8 * video_q.size, transcendentals=0),
        name="pack_pair",
    )(video_q, video_k, video_v)


def unpack_kernel(single_ref, pair_ref, out_ref, held_ref, single_sems, pair_sems):
    groups = pair_ref.shape[0]

    def pair_copy(g):
        target = out_ref.at[:, pl.ds((g // 2 * 3 + g % 2 * 2) * LANES, LANES)]
        return pltpu.make_async_copy(pair_ref.at[g], target, pair_sems.at[g])

    def single_copy(u):
        return pltpu.make_async_copy(held_ref.at[u], out_ref.at[:, pl.ds((3 * u + 1) * LANES, LANES)], single_sems.at[u])

    for g in range(groups):
        pair_copy(g).start()
    for u in range(groups // 2):
        held_ref[u] = jnp.transpose(jnp.concatenate([single_ref[2 * u], single_ref[2 * u + 1]], axis=0))
        single_copy(u).start()
    for g in range(groups):
        pair_copy(g).wait()
    for u in range(groups // 2):
        single_copy(u).wait()


def unpack(single, pair):
    groups = single.shape[0]
    any_space = pl.BlockSpec(memory_space=pl.ANY)
    return pl.pallas_call(
        unpack_kernel,
        in_specs=[pl.BlockSpec(memory_space=pltpu.VMEM)] * 2,
        out_specs=any_space,
        out_shape=jax.ShapeDtypeStruct((TILE, groups * 3 * HD), BF16),
        scratch_shapes=[
            pltpu.VMEM((groups // 2, TILE, LANES), BF16),
            pltpu.SemaphoreType.DMA((groups // 2,)),
            pltpu.SemaphoreType.DMA((groups,)),
        ],
        name="unpack",
    )(single, pair)


def neighbour_lists(offsets, block_mask):
    spots = jnp.arange(LAYER, dtype=jnp.int32)
    layer = lax.axis_index("seq") + offsets[None, :, 0]
    moved_h = spots[:, None] // TW + offsets[None, :, 1]
    moved_w = spots[:, None] % TW + offsets[None, :, 2]
    live = (
        (moved_h >= 0)
        & (moved_h < TH)
        & (moved_w >= 0)
        & (moved_w < TW)
        & (layer >= 0)
        & (layer < lax.axis_size("seq"))
        & (block_mask == 1)
    )
    target = ((offsets[None, :, 0] + 1) * TH + moved_h) * TW + moved_w
    ones = live.astype(jnp.int32)
    earlier = jnp.arange(NB)[:, None] < jnp.arange(NB)[None, :]
    place = jnp.sum(jnp.where(earlier[None], ones[:, :, None], 0), axis=1)
    slots = jnp.arange(SLOTS, dtype=jnp.int32)
    chosen = live[:, :, None] & (place[:, :, None] == slots[None, None, :])
    table = jnp.sum(jnp.where(chosen, target[:, :, None], 0), axis=1)
    counts = jnp.sum(ones, axis=1)
    ahead = (counts[:, None] > counts[None, :]) | ((counts[:, None] == counts[None, :]) & (spots[:, None] < spots[None, :]))
    rank = jnp.sum(ahead.astype(jnp.int32), axis=0)
    order = jnp.sum(jnp.where(rank[:, None] == spots[None, :], spots[:, None], 0), axis=0)
    return counts, order, table.reshape(-1)


def attend_rows(units, text_bias, groups, score_ref):
    tops = []
    for n, unit in enumerate(units):
        scores = unit["score"](unit["queries"], unit["text_k"]) + text_bias
        parts = [scores[:, :LANES], scores[:, LANES:]]
        score_ref[n, 0] = parts[0]
        score_ref[n, 1] = parts[1]
        tops.append(jnp.maximum(parts[0], parts[1]))
    for g in range(groups):
        for n, unit in enumerate(units):
            keys = [unit["keys"](g * GROUP + j) for j in range(GROUP)]
            found = unit["score"](unit["queries"], jnp.concatenate(keys, axis=unit["key_axis"]))
            for j in range(GROUP):
                part = found[:, j * LANES : (j + 1) * LANES]
                if unit["bias"] is not None:
                    part = part + unit["bias"](g * GROUP + j)
                score_ref[n, 2 + g * GROUP + j] = part
                tops[n] = jnp.maximum(tops[n], part)
    highest = [jnp.max(top, axis=1, keepdims=True) for top in tops]
    shifts = [top * FACTOR for top in highest]
    totals, mixed = [], []
    for n, unit in enumerate(units):
        weights = [jnp.exp2(score_ref[n, j] * FACTOR - shifts[n]) for j in range(2)]
        totals.append(weights[0] + weights[1])
        mixed.append(unit["mix"](jnp.concatenate([w.astype(BF16) for w in weights], axis=1), unit["text_v"]))
    for g in range(groups):
        for n, unit in enumerate(units):
            weights = [jnp.exp2(score_ref[n, 2 + g * GROUP + j] * FACTOR - shifts[n]) for j in range(GROUP)]
            totals[n] = totals[n] + ((weights[0] + weights[1]) + (weights[2] + weights[3]))
            values = jnp.concatenate([unit["values"](g * GROUP + j) for j in range(GROUP)], axis=unit["value_axis"])
            mixed[n] = mixed[n] + unit["mix"](jnp.concatenate([w.astype(BF16) for w in weights], axis=1), values)
    return highest, [jnp.sum(total, axis=1, keepdims=True) for total in totals], mixed


PAIR = dict(score=dot_nt, key_axis=0, mix=dot_nn, value_axis=0)
SINGLE = dict(score=dot_nn, key_axis=1, mix=dot_nt, value_axis=1)


def video_kernel(
    heads, together, counts_ref, order_ref, table_ref, q_ref, before_ref, own_ref, after_ref, text_k_ref, text_v_ref, bias_ref,
    out_ref, kv_ref, score_ref, sems,
):
    copies = [
        pltpu.make_async_copy(ref, kv_ref.at[pl.ds(n * LAYER, LAYER)], sems.at[n])
        for n, ref in enumerate((before_ref, own_ref, after_ref))
    ]
    for copy in copies:
        copy.start()
    for copy in copies:
        copy.wait()
    rows = kv_ref.shape[1] // 2

    def unit_of(i):
        low = low_lanes(TILE)
        block = q_ref[i].astype(F32)
        if heads == 1:
            queries = jnp.transpose(block)
        else:
            queries = jnp.concatenate([jnp.where(low, block, 0.0), jnp.where(low, 0.0, block)], axis=0)
        count = counts_ref[i]
        return dict(
            SINGLE if heads == 1 else PAIR,
            queries=queries.astype(BF16),
            text_k=text_k_ref[...],
            text_v=text_v_ref[...],
            keys=lambda slot: kv_ref[table_ref[i * SLOTS + slot], :rows, :],
            values=lambda slot: kv_ref[table_ref[i * SLOTS + slot], rows:, :],
            bias=lambda slot: jnp.where(slot < count, 0.0, NEG_FILL),
        )

    def some_tiles(step, carry):
        tiles = [order_ref[step * together + n] for n in range(together)]
        longest = functools.reduce(jnp.maximum, [counts_ref[i] for i in tiles])
        for groups in range(SLOTS // GROUP + 1):

            @pl.when((longest + (GROUP - 1)) // GROUP == groups)
            def _():
                _, totals, mixed = attend_rows([unit_of(i) for i in tiles], bias_ref[...], groups, score_ref)
                for n, i in enumerate(tiles):
                    result = mixed[n] / totals[n]
                    if heads == 1:
                        out_ref[i] = jnp.transpose(result).astype(BF16)
                    else:
                        out_ref[i] = jnp.where(low_lanes(TILE), result[:TILE], result[TILE:]).astype(BF16)

        return carry

    lax.fori_loop(0, LAYER // together, some_tiles, 0)


def video_attention(heads, counts, order, table, queries, before, own, after, text_k, text_v, text_bias):
    rows = heads * TILE
    together = 2
    smem = pl.BlockSpec(memory_space=pltpu.SMEM)
    vmem = pl.BlockSpec(memory_space=pltpu.VMEM)
    hbm = pl.BlockSpec(memory_space=pl.ANY)
    pairs = 300 * TILE * TILE * heads
    return pl.pallas_call(
        functools.partial(video_kernel, heads, together),
        in_specs=[smem, smem, smem, vmem, hbm, hbm, hbm, vmem, vmem, vmem],
        out_specs=vmem,
        out_shape=jax.ShapeDtypeStruct(queries.shape, BF16),
        scratch_shapes=[
            pltpu.VMEM((3 * LAYER,) + own.shape[1:], BF16),
            pltpu.VMEM((together, 2 + SLOTS, rows, LANES), F32),
            pltpu.SemaphoreType.DMA((3,)),
        ],
        compiler_params=pltpu.CompilerParams(vmem_limit_bytes=VMEM_LIMIT),
        cost_estimate=pl.CostEstimate(flops=16 * HD * pairs, bytes_accessed=8 * own.size, transcendentals=pairs),
        name=f"video_attention_{heads}",
    )(counts, order, table, queries, before, own, after, text_k, text_v, text_bias)


def text_kernel(
    pair_q_ref, pair_kv_ref, pair_k_ref, pair_v_ref, single_q_ref, single_kv_ref, single_k_ref, single_v_ref, bias_ref,
    out_ref, score_ref,
):
    low = low_lanes(TEXT_ROWS)
    pair_q = pair_q_ref[...].astype(F32)

    def pair_unit(head):
        return dict(
            PAIR,
            queries=jnp.where(low if head == 0 else ~low, pair_q, 0.0).astype(BF16),
            text_k=pair_k_ref[...],
            text_v=pair_v_ref[...],
            keys=lambda slot: pair_kv_ref[slot, :TILE, :],
            values=lambda slot: pair_kv_ref[slot, TILE:, :],
            bias=None,
        )

    single_unit = dict(
        SINGLE,
        queries=single_q_ref[...],
        text_k=single_k_ref[...],
        text_v=single_v_ref[...],
        keys=lambda slot: single_kv_ref[slot, :HD, :],
        values=lambda slot: single_kv_ref[slot, HD:, :],
        bias=None,
    )
    tops, totals, mixed = attend_rows([pair_unit(0), pair_unit(1), single_unit], bias_ref[...], LAYER // GROUP, score_ref)
    means = [m / t for m, t in zip(mixed, totals)]
    weighs = [top * FACTOR + jnp.log2(total) for top, total in zip(tops, totals)]
    kept = out_ref.shape[0]
    out_ref[:, :LANES] = jnp.where(low, means[0], means[1])[:kept]
    out_ref[:, LANES : 2 * LANES] = jnp.where(low, weighs[0], weighs[1])[:kept]
    out_ref[:, 2 * LANES :] = jnp.concatenate([means[2], jnp.broadcast_to(weighs[2], means[2].shape)], axis=1)[:kept]


def text_partial(pair_q, pair_kv, pair_k, pair_v, single_q, single_kv, single_k, single_v, bias):
    vmem = pl.BlockSpec(memory_space=pltpu.VMEM)
    pairs = 3 * TEXT_ROWS * (LAYER + 2) * TILE
    return pl.pallas_call(
        text_kernel,
        in_specs=[vmem] * 9,
        out_specs=vmem,
        out_shape=jax.ShapeDtypeStruct((TEXT_KEPT, 3 * LANES), F32),
        scratch_shapes=[pltpu.VMEM((3, 2 + LAYER, TEXT_ROWS, LANES), F32)],
        compiler_params=pltpu.CompilerParams(vmem_limit_bytes=VMEM_LIMIT),
        cost_estimate=pl.CostEstimate(flops=16 * HD * pairs, bytes_accessed=4 * pair_kv.size, transcendentals=pairs),
        name="text_partial",
    )(pair_q, pair_kv, pair_k, pair_v, single_q, single_kv, single_k, single_v, bias)


def combine_kernel(parts_ref, pair_ref, single_ref):
    def merged(means, weighs):
        weights = jnp.exp2(weighs - jnp.max(weighs, axis=0, keepdims=True))
        return (jnp.sum(means * weights, axis=0) / jnp.sum(weights, axis=0)).astype(BF16)

    pair_ref[...] = merged(parts_ref[:, :, :LANES], parts_ref[:, :, LANES : 2 * LANES])
    single_ref[...] = merged(parts_ref[:, :, 2 * LANES : 2 * LANES + HD], parts_ref[:, :, 2 * LANES + HD :])


def combine(parts):
    slabs, rows, _ = parts.shape
    step = rows // 4
    return pl.pallas_call(
        combine_kernel,
        grid=(rows // step,),
        in_specs=[pl.BlockSpec((slabs, step, 3 * LANES), lambda i: (0, i, 0))],
        out_specs=[pl.BlockSpec((step, LANES), lambda i: (i, 0)), pl.BlockSpec((step, HD), lambda i: (i, 0))],
        out_shape=[jax.ShapeDtypeStruct((rows, LANES), BF16), jax.ShapeDtypeStruct((rows, HD), BF16)],
        name="text_combine",
    )(parts)


def exchange(blocks, axis):
    return lax.all_to_all(blocks, axis, split_axis=0, concat_axis=0, tiled=True)


def both_sides(layer):
    count = lax.axis_size("seq")
    up = [(i, i + 1) for i in range(count - 1)]
    down = [(i + 1, i) for i in range(count - 1)]
    return lax.ppermute(layer, "seq", up), lax.ppermute(layer, "seq", down)


def after(value, *others):
    return lax.optimization_barrier((value,) + others)[0]


def body(video_q, video_k, video_v, text_q, text_k, text_v, offsets, block_mask, text_mask):
    odd = lax.axis_index("head") % 2 == 1
    counts, order, table = neighbour_lists(offsets, block_mask)

    def split_text(text):
        grown = jnp.pad(text, ((0, TEXT_ROWS - TEXT), (0, 0)))
        return jnp.where(odd, grown[:, HD:], grown[:, : 2 * HD]), jnp.where(odd, grown[:, :HD], grown[:, 2 * HD :])

    (pair_tq, single_tq), (pair_tk, single_tk), (pair_tv, single_tv) = map(split_text, (text_q, text_k, text_v))
    single_tk, single_tv = single_tk.T, single_tv.T
    text_live = jnp.pad(text_mask, (0, TEXT_ROWS - TEXT)) == 1
    bias = jnp.where(text_live, 0.0, NEG_FILL).astype(F32)[None, :]
    own_bias = jnp.where(lax.axis_index("seq") == 0, bias, NEG_FILL)

    single = exchange(pack_single(video_q, video_k, video_v), "head")
    pair_kv, pair_q = pack_pair(video_q, video_k, video_v)
    pair_kv = exchange(after(pair_kv, single), "head")
    single_kv, single_q = single[:, : 2 * HD], single[:, 2 * HD :]
    single_before, single_after = both_sides(single_kv)
    single_out = video_attention(
        1, counts, order, table, single_q, single_before, single_kv, single_after, single_tk, single_tv, bias
    )
    pair_kv = after(pair_kv, single_out)
    pair_q = exchange(after(pair_q, pair_kv), "head")
    pair_before, pair_after = both_sides(pair_kv)
    partial = text_partial(
        pair_tq, pair_kv, pair_tk, pair_tv, single_tq, single_kv, single_tk, single_tv, own_bias
    )
    parts = lax.all_gather(partial, "seq")
    single_back = exchange(after(single_out, pair_q), "head")
    pair_out = video_attention(2, counts, order, table, pair_q, pair_before, pair_kv, pair_after, pair_tk, pair_tv, bias)
    pair_back = exchange(after(pair_out, single_back), "head")
    video_out = unpack(single_back, pair_back)

    pair_part, single_part = (part[:TEXT] for part in combine(parts))
    text_out = jnp.where(
        odd,
        jnp.concatenate([single_part, pair_part], axis=1),
        jnp.concatenate([pair_part, single_part], axis=1),
    )
    return video_out, text_out


def solution(mesh):
    return jax.shard_map(
        body,
        mesh=mesh,
        in_specs=(
            P(("seq", "head"), None),
            P(("seq", "head"), None),
            P(("seq", "head"), None),
            P(None, "head"),
            P(None, "head"),
            P(None, "head"),
            P(),
            P("seq", None),
            P(),
        ),
        out_specs=(P(("seq", "head"), None), P(None, "head")),
        check_vma=False,
    )
```

time: 271 us -> 195 us (0.72)
  Pallas kernels: 106 us -> 55 us
  waiting for transfers between devices: 62.6 us -> 28 us
  starting transfers between devices: 50.2 us -> 31.9 us
  blocking collectives: 32.1 us -> 48.9 us
  between operations: 0.88 us -> 14.3 us
    pallas_call x5 -> x6, Pallas kernels: 95.6 us -> 49.7 us  [the longest x2 36.1 us: video_attention(): pl.pallas_call(functools.partial(video_kernel, heads, together), in_specs...]
    all_to_all x6 -> x3, waiting for transfers between devices: 42.7 us -> 19.5 us  [exchange(): return lax.all_to_all(blocks, axis, split_axis=0, concat_axis=0, tiled=True)]
    all_to_all x6 -> x3, starting transfers between devices: 37 us -> 16.1 us  [exchange(): return lax.all_to_all(blocks, axis, split_axis=0, concat_axis=0, tiled=True)]
    all_to_all x1 -> x2, blocking collectives: 32.1 us -> 48.9 us  [exchange(): return lax.all_to_all(blocks, axis, split_axis=0, concat_axis=0, tiled=True)]
    ppermute x4, waiting for transfers between devices: 19.9 us -> 8.5 us  [both_sides(): return (lax.ppermute(layer, 'seq', up), lax.ppermute(layer, 'seq', down))]
    pallas_call x1, Pallas kernels: 10.5 us -> 5.32 us  [text_partial(): pl.pallas_call(text_kernel, in_specs=[vmem] * 9, out_specs=vmem, out_shap...]
    unnamed x32 -> x31, local copies, waits for them, and re-layouts: 6.91 us -> 4.54 us
  transfers between devices with their start and end apart: 10 -> 8, of which waited for: 5 -> 4; matrix products, arithmetic and copies ran while one was open for 4% -> 4% of each run, Pallas kernels for 32% -> 22%
where the time goes in v2:
time: 195 us; the launch traced here: 192 us
  Pallas kernels  55 us (28%)
  blocking collectives  48.9 us (25%)
  starting transfers between devices  31.9 us (16%)
  waiting for transfers between devices  28 us (14%)
  between operations  14.3 us (7%)
  local copies, waits for them, and re-layouts  11 us (6%)
  other arithmetic  2.72 us (1%)
    all_to_all x2, blocking collectives, exchange(): return lax.all_to_all(blocks, axis, split_axis=0, concat_axis=0, tiled=True)  48.9 us
    pallas_call x2, Pallas kernels, video_attention(): pl.pallas_call(functools.partial(video_kernel, heads, together), in_specs...  36.1 us
    all_to_all x3, waiting for transfers between devices, exchange(): return lax.all_to_all(blocks, axis, split_axis=0, concat_axis=0, tiled=True)  19.5 us
    all_to_all x3, starting transfers between devices, exchange(): return lax.all_to_all(blocks, axis, split_axis=0, concat_axis=0, tiled=True)  16.1 us
    ppermute x4, starting transfers between devices, both_sides(): return (lax.ppermute(layer, 'seq', up), lax.ppermute(layer, 'seq', down))  15.7 us
    ppermute x4, waiting for transfers between devices, both_sides(): return (lax.ppermute(layer, 'seq', up), lax.ppermute(layer, 'seq', down))  8.5 us
    pallas_call x1, Pallas kernels, text_partial(): pl.pallas_call(text_kernel, in_specs=[vmem] * 9, out_specs=vmem, out_shap...  5.32 us
    pallas_call x1, Pallas kernels, combine(): pl.pallas_call(combine_kernel, grid=(rows // step,), in_specs=[pl.BlockSp...  4.81 us
  transfers between devices with their start and end apart: 8, of which 4 were waited for; matrix products, arithmetic and copies ran while one was open for 4% of the time, Pallas kernels for 22%

profile of v2, /device:TPU:3, one launch (start us, length us, event | category | flops | bytes accessed | tf_op | source)
XLA Modules:
  0.0 191.8 jit_solution(6402390318450227455)
XLA Ops:
  7.2 3.6 %pack_single.1 = bf16[16,192,128]{2,1,0:T(8,128)(2,1)} custom-call(bf16[128,3072]{1,0:T(8,128)(2,1)} %q_ref.3, bf16[128,3072]{1,0:T(8,128)(2,1)} %k_ref.3, bf16[128,3072]{1,0:T(8,128)(2,1)} %v_ref.3), custom_call_target="tpu_custom_call" | custom-call | bytes 1572864 | tf_op jit(solution)/shard_map/pack_single/pallas_call | solution.py:61
  10.9 9.2 %all-to-all-start = ((bf16[16,192,128]{2,1,0:T(8,128)(2,1)}), bf16[16,192,128]{2,1,0:T(8,128)(2,1)S(1)}, u32[]{:S(2)}, u32[]{:S(2)}) async-start(bf16[16,192,128]{2,1,0:T(8,128)(2,1)} %pack_single.1), calls=%async_computation | async-start | bytes 1572864 | tf_op jit(solution)/shard_map/all_to_all | solution.py:355
  20.0 3.0 %pack_pair.1 = (bf16[16,256,128]{2,1,0:T(8,128)(2,1)}, bf16[16,128,128]{2,1,0:T(8,128)(2,1)}) custom-call(bf16[128,3072]{1,0:T(8,128)(2,1)} %q_ref.3, bf16[128,3072]{1,0:T(8,128)(2,1)} %k_ref.3, bf16[128,3072]{1,0:T(8,128)(2,1)} %v_ref.3), custom_call_target="tpu_custom_call" | custom-call | bytes 3145728 | tf_op jit(solution)/shard_map/pack_pair/pallas_call | solution.py:91
  23.2 19.5 %all-to-all-done = bf16[16,192,128]{2,1,0:T(8,128)(2,1)S(1)} async-done(((bf16[16,192,128]{2,1,0:T(8,128)(2,1)}), bf16[16,192,128]{2,1,0:T(8,128)(2,1)S(1)}, u32[]{:S(2)}, u32[]{:S(2)}) %all-to-all-start) | async-done | bytes 786464 | tf_op jit(solution)/shard_map/all_to_all | solution.py:355
  42.7 3.6 %all-to-all-start.1 = ((bf16[16,256,128]{2,1,0:T(8,128)(2,1)}), bf16[16,256,128]{2,1,0:T(8,128)(2,1)S(1)}, u32[]{:S(2)}, u32[]{:S(2)}) async-start(bf16[16,256,128]{2,1,0:T(8,128)(2,1)} %get-tuple-element.13), calls=%async_computation.1 | async-start | bytes 2097152 | tf_op jit(solution)/shard_map/all_to_all | solution.py:355
  50.8 3.2 %collective-permute-start = (bf16[16,128,128]{2,1,0:T(8,128)(2,1)S(1)}, bf16[16,128,128]{2,1,0:T(8,128)(2,1)S(1)}, u32[]{:S(2)}, u32[]{:S(2)}) collective-permute-start(bf16[16,128,128]{2,1,0:T(8,128)(2,1)S(1)} %slice.78.own_ref.single_kv_ref), channel_id=1, source_target_pairs={{0,16},{16,32},{32,48},{48,64},{64,80},{80,96},{96,112},{112,128},... | collective-permute-start | bytes 1572872 | tf_op jit(solution)/shard_map/ppermute | solution.py:362
  54.0 4.4 %collective-permute-start.1 = (bf16[16,128,128]{2,1,0:T(8,128)(2,1)S(1)}, bf16[16,128,128]{2,1,0:T(8,128)(2,1)S(1)}, u32[]{:S(2)}, u32[]{:S(2)}) collective-permute-start(bf16[16,128,128]{2,1,0:T(8,128)(2,1)S(1)} %slice.78.own_ref.single_kv_ref), channel_id=1, source_target_pairs={{16,0},{32,16},{48,32},{64,48},{80,64},{96,80},{112,96},{128,112},... | collective-permute-start | bytes 1572872 | tf_op jit(solution)/shard_map/ppermute | solution.py:362
  61.2 7.4 %collective-permute-done.before_ref = bf16[16,128,128]{2,1,0:T(8,128)(2,1)S(1)} collective-permute-done((bf16[16,128,128]{2,1,0:T(8,128)(2,1)S(1)}, bf16[16,128,128]{2,1,0:T(8,128)(2,1)S(1)}, u32[]{:S(2)}, u32[]{:S(2)}) %collective-permute-start) | collective-permute-done | bytes 524320 | tf_op jit(solution)/shard_map/ppermute | solution.py:362
  68.6 1.0 collective-permute-done.1.after_ref
  70.4 14.0 %video_attention_1.1 = bf16[16,64,128]{2,1,0:T(8,128)(2,1)} custom-call(s32[16]{0:T(128)} %copy-done.10, s32[16]{0:T(128)} %select_reduce_fusion.2.order_ref, s32[448]{0:T(512)} %reshape.182.table_ref, bf16[16,64,128]{2,1,0:T(8,128)(2,1)} %slice.77.q_ref, bf16[16,128,128]{2,1,0:T(8,128)(2,1)} %copy-done.13, bf16[16,128,128]{2,1,0:T(8,128)(2,1)} %copy-done.3, ...), custom_call_target="tpu_custom_call" | custom-call | flops 5033164800 | bytes 2097152 | tf_op jit(solution)/shard_map/video_attention_1/pallas_call | solution.py:265
  84.4 1.0 copy-done
  85.4 5.3 %text_partial.1 = f32[256,384]{1,0:T(8,128)} custom-call(bf16[256,128]{1,0:T(8,128)(2,1)} %copy.24.pair_q_ref, bf16[16,256,128]{2,1,0:T(8,128)(2,1)} %copy-done, bf16[256,128]{1,0:T(8,128)(2,1)} %copy.22.text_k_ref.pair_k_ref, bf16[256,128]{1,0:T(8,128)(2,1)} %copy.23.text_v_ref.pair_v_ref, bf16[256,64]{1,0:T(8,128)(2,1)} %copy.27.single_q_ref, ...), custom_call_target="tpu_custom_call" | custom-call | flops 1811939328 | bytes 2097152 | tf_op jit(solution)/shard_map/text_partial/pallas_call | solution.py:320
  90.7 2.9 %collective-permute-start.2 = (bf16[16,256,128]{2,1,0:T(8,128)(2,1)}, bf16[16,256,128]{2,1,0:T(8,128)(2,1)S(1)}, u32[]{:S(2)}, u32[]{:S(2)}) collective-permute-start(bf16[16,256,128]{2,1,0:T(8,128)(2,1)} %copy-done), channel_id=1, source_target_pairs={{0,16},{16,32},{32,48},{48,64},{64,80},{80,96},{96,112},{112,128},... | collective-permute-start | bytes 3145736 | tf_op jit(solution)/shard_map/ppermute | solution.py:362
  93.6 5.2 %collective-permute-start.3 = (bf16[16,256,128]{2,1,0:T(8,128)(2,1)}, bf16[16,256,128]{2,1,0:T(8,128)(2,1)S(1)}, u32[]{:S(2)}, u32[]{:S(2)}) collective-permute-start(bf16[16,256,128]{2,1,0:T(8,128)(2,1)} %copy-done), channel_id=1, source_target_pairs={{16,0},{32,16},{48,32},{64,48},{80,64},{96,80},{112,96},{128,112},... | collective-permute-start | bytes 3145736 | tf_op jit(solution)/shard_map/ppermute | solution.py:362
  98.9 24.7 %all_to_all.25.q_ref = bf16[16,128,128]{2,1,0:T(8,128)(2,1)} all-to-all(bf16[16,128,128]{2,1,0:T(8,128)(2,1)S(1)} %copy-done.2), channel_id=1, replica_groups=mesh['seq'=16,'head'=16] {'head'}, dimensions={0} | all-to-all | bytes 1048576 | tf_op jit(solution)/shard_map/all_to_all | solution.py:355
  123.6 3.4 %all-to-all-start.3 = ((bf16[16,64,128]{2,1,0:T(8,128)(2,1)}), bf16[16,64,128]{2,1,0:T(8,128)(2,1)S(1)}, u32[]{:S(2)}, u32[]{:S(2)}) async-start(bf16[16,64,128]{2,1,0:T(8,128)(2,1)} %video_attention_1.1), calls=%async_computation.3 | async-start | bytes 524288 | tf_op jit(solution)/shard_map/all_to_all | solution.py:355
  127.2 0.9 copy-done.11
  128.1 1.1 copy-done.12
  129.2 22.1 %video_attention_2.1 = bf16[16,128,128]{2,1,0:T(8,128)(2,1)} custom-call(s32[16]{0:T(128)} %copy-done.10, s32[16]{0:T(128)} %select_reduce_fusion.2.order_ref, s32[448]{0:T(512)} %reshape.182.table_ref, bf16[16,128,128]{2,1,0:T(8,128)(2,1)} %all_to_all.25.q_ref, bf16[16,256,128]{2,1,0:T(8,128)(2,1)} %copy-done.11, bf16[16,256,128]{2,1,0:T(8,128)(2,1)} %copy-done, ...), custom_call_target="tpu_custom_call" | custom-call | flops 10066329600 | bytes 4194304 | tf_op jit(solution)/shard_map/video_attention_2/pallas_call | solution.py:265
  151.3 24.1 %all_to_all.26.pair_ref = bf16[16,128,128]{2,1,0:T(8,128)(2,1)} all-to-all(bf16[16,128,128]{2,1,0:T(8,128)(2,1)} %video_attention_2.1), channel_id=1, replica_groups=mesh['seq'=16,'head'=16] {'head'}, dimensions={0} | all-to-all | bytes 1048576 | tf_op jit(solution)/shard_map/all_to_all | solution.py:355
  175.4 2.2 %unpack.1 = bf16[128,3072]{1,0:T(8,128)(2,1)} custom-call(bf16[16,64,128]{2,1,0:T(8,128)(2,1)} %copy-done.1, bf16[16,128,128]{2,1,0:T(8,128)(2,1)} %all_to_all.26.pair_ref), custom_call_target="tpu_custom_call" | custom-call | tf_op jit(solution)/shard_map/unpack/pallas_call | solution.py:126
  177.7 4.8 %text_combine.1 = (bf16[256,128]{1,0:T(8,128)(2,1)}, bf16[256,64]{1,0:T(8,128)(2,1)}) custom-call(f32[16,256,384]{2,1,0:T(8,128)} %bitcast.17), custom_call_target="tpu_custom_call" | custom-call | tf_op jit(solution)/shard_map/text_combine/pallas_call | solution.py:344
  182.5 0.8 slice.76
  183.3 0.8 slice.75
  (63 shorter events, 9.3 us)
Async XLA Ops:
  7.2 15.9 %copy-start.8 = (s32[27,3]{0,1:T(4,128)S(1)}, s32[27,3]{0,1:T(4,128)}, u32[]{:S(2)}) copy-start(s32[27,3]{0,1:T(4,128)} %param.15) | copy-start | bytes 976
  7.2 39.1 %copy-start.7 = (s32[16,27]{1,0:T(8,128)S(1)}, s32[16,27]{1,0:T(8,128)}, u32[]{:S(2)}) copy-start(s32[16,27]{1,0:T(8,128)} %param.16) | copy-start | bytes 5188
  7.2 40.6 %copy-start.5 = (bf16[226,192]{0,1:T(8,128)(2,1)S(1)}, bf16[226,192]{0,1:T(8,128)(2,1)}, u32[]{:S(2)}) copy-start(bf16[226,192]{0,1:T(8,128)(2,1)} %param.13) | copy-start | bytes 260356
  7.2 40.6 %copy-start.6 = (bf16[226,192]{0,1:T(8,128)(2,1)S(1)}, bf16[226,192]{0,1:T(8,128)(2,1)}, u32[]{:S(2)}) copy-start(bf16[226,192]{0,1:T(8,128)(2,1)} %param.14) | copy-start | bytes 260356
  7.2 42.1 %copy-start.4 = (bf16[226,192]{0,1:T(8,128)(2,1)S(1)}, bf16[226,192]{0,1:T(8,128)(2,1)}, u32[]{:S(2)}) copy-start(bf16[226,192]{0,1:T(8,128)(2,1)} %param.12) | copy-start | bytes 260356
  7.2 51.2 %copy-start.9 = (s32[226]{0:T(256)S(1)}, s32[226]{0:T(256)}, u32[]{:S(2)}) copy-start(s32[226]{0:T(256)} %param.17) | copy-start | bytes 2716
  10.9 31.8 %all-to-all-start = ((bf16[16,192,128]{2,1,0:T(8,128)(2,1)}), bf16[16,192,128]{2,1,0:T(8,128)(2,1)S(1)}, u32[]{:S(2)}, u32[]{:S(2)}) async-start(bf16[16,192,128]{2,1,0:T(8,128)(2,1)} %pack_single.1), calls=%async_computation | async-start | bytes 1572864 | tf_op jit(solution)/shard_map/all_to_all | solution.py:355
  42.7 41.7 %all-to-all-start.1 = ((bf16[16,256,128]{2,1,0:T(8,128)(2,1)}), bf16[16,256,128]{2,1,0:T(8,128)(2,1)S(1)}, u32[]{:S(2)}, u32[]{:S(2)}) async-start(bf16[16,256,128]{2,1,0:T(8,128)(2,1)} %get-tuple-element.13), calls=%async_computation.1 | async-start | bytes 2097152 | tf_op jit(solution)/shard_map/all_to_all | solution.py:355
  46.3 131.4 %all-gather.3.cloned.1.call-start = ((), (), s32[]{:S(2)}) async-start(), calls=%async_computation.5 | async-start | bytes 6684672 | tf_op jit(solution)/shard_map/all_gather | solution.py:397
  50.8 18.8 %copy-start.3 = (bf16[16,128,128]{2,1,0:T(8,128)(2,1)}, bf16[16,128,128]{2,1,0:T(8,128)(2,1)S(1)}, u32[]{:S(2)}) copy-start(bf16[16,128,128]{2,1,0:T(8,128)(2,1)S(1)} %slice.78.own_ref.single_kv_ref) | copy-start | bytes 1572868
  50.8 17.8 %collective-permute-start = (bf16[16,128,128]{2,1,0:T(8,128)(2,1)S(1)}, bf16[16,128,128]{2,1,0:T(8,128)(2,1)S(1)}, u32[]{:S(2)}, u32[]{:S(2)}) collective-permute-start(bf16[16,128,128]{2,1,0:T(8,128)(2,1)S(1)} %slice.78.own_ref.single_kv_ref), channel_id=1, source_target_pairs={{0,16},{16,32},{32,48},{48,64},{64,80},{80,96},{96,112},{112,128},... | collective-permute-start | bytes 1572872 | tf_op jit(solution)/shard_map/ppermute | solution.py:362
  54.0 15.5 %collective-permute-start.1 = (bf16[16,128,128]{2,1,0:T(8,128)(2,1)S(1)}, bf16[16,128,128]{2,1,0:T(8,128)(2,1)S(1)}, u32[]{:S(2)}, u32[]{:S(2)}) collective-permute-start(bf16[16,128,128]{2,1,0:T(8,128)(2,1)S(1)} %slice.78.own_ref.single_kv_ref), channel_id=1, source_target_pairs={{16,0},{32,16},{48,32},{64,48},{80,64},{96,80},{112,96},{128,112},... | collective-permute-start | bytes 1572872 | tf_op jit(solution)/shard_map/ppermute | solution.py:362
  59.1 10.5 %copy-start.10 = (s32[16]{0:T(128)}, s32[16]{0:T(128)S(1)}, u32[]{:S(2)}) copy-start(s32[16]{0:T(128)S(1)} %convert_reduce_fusion.1.counts_ref) | copy-start | bytes 196
  68.6 1.0 copy-start.13
  69.6 0.8 copy-start.14
  84.4 14.5 %copy-start.2 = (bf16[16,128,128]{2,1,0:T(8,128)(2,1)S(1)}, bf16[16,128,128]{2,1,0:T(8,128)(2,1)}, u32[]{:S(2)}) copy-start(bf16[16,128,128]{2,1,0:T(8,128)(2,1)} %get-tuple-element.15) | copy-start | bytes 1572868
  84.4 1.0 copy-start
  90.7 36.3 %collective-permute-start.2 = (bf16[16,256,128]{2,1,0:T(8,128)(2,1)}, bf16[16,256,128]{2,1,0:T(8,128)(2,1)S(1)}, u32[]{:S(2)}, u32[]{:S(2)}) collective-permute-start(bf16[16,256,128]{2,1,0:T(8,128)(2,1)} %copy-done), channel_id=1, source_target_pairs={{0,16},{16,32},{32,48},{48,64},{64,80},{80,96},{96,112},{112,128},... | collective-permute-start | bytes 3145736 | tf_op jit(solution)/shard_map/ppermute | solution.py:362
  93.6 33.6 %collective-permute-start.3 = (bf16[16,256,128]{2,1,0:T(8,128)(2,1)}, bf16[16,256,128]{2,1,0:T(8,128)(2,1)S(1)}, u32[]{:S(2)}, u32[]{:S(2)}) collective-permute-start(bf16[16,256,128]{2,1,0:T(8,128)(2,1)} %copy-done), channel_id=1, source_target_pairs={{16,0},{32,16},{48,32},{64,48},{80,64},{96,80},{112,96},{128,112},... | collective-permute-start | bytes 3145736 | tf_op jit(solution)/shard_map/ppermute | solution.py:362
  123.6 27.6 %all-to-all-start.3 = ((bf16[16,64,128]{2,1,0:T(8,128)(2,1)}), bf16[16,64,128]{2,1,0:T(8,128)(2,1)S(1)}, u32[]{:S(2)}, u32[]{:S(2)}) async-start(bf16[16,64,128]{2,1,0:T(8,128)(2,1)} %video_attention_1.1), calls=%async_computation.3 | async-start | bytes 524288 | tf_op jit(solution)/shard_map/all_to_all | solution.py:355
  127.1 1.1 copy-start.11
  128.1 1.1 copy-start.12
  151.3 24.1 %copy-start.1 = (bf16[16,64,128]{2,1,0:T(8,128)(2,1)}, bf16[16,64,128]{2,1,0:T(8,128)(2,1)S(1)}, u32[]{:S(2)}) copy-start(bf16[16,64,128]{2,1,0:T(8,128)(2,1)S(1)} %all-to-all-done.3.single_ref) | copy-start | bytes 786436
Sparse Core Ops, SparseCore 0:
  90.9 79.1 all-gather.2

commit v3 on v2

--- a/solution.py
+++ b/solution.py
@@ -11,7 +11,7 @@
 HD = 64
 TEXT = 226
 TEXT_ROWS = 256
-TEXT_KEPT = 256
+TEXT_KEPT = 232
 TILE = 128
 TH = 4
 TW = 4
@@ -101,6 +101,7 @@
 
 def unpack_kernel(single_ref, pair_ref, out_ref, held_ref, single_sems, pair_sems):
     groups = pair_ref.shape[0]
+    first = single_ref.shape[1] - HD
 
     def pair_copy(g):
         target = out_ref.at[:, pl.ds((g // 2 * 3 + g % 2 * 2) * LANES, LANES)]
@@ -112,7 +113,8 @@
     for g in range(groups):
         pair_copy(g).start()
     for u in range(groups // 2):
-        held_ref[u] = jnp.transpose(jnp.concatenate([single_ref[2 * u], single_ref[2 * u + 1]], axis=0))
+        both = [single_ref[2 * u + n, first:, :] for n in range(2)]
+        held_ref[u] = jnp.transpose(jnp.concatenate(both, axis=0))
         single_copy(u).start()
     for g in range(groups):
         pair_copy(g).wait()
@@ -204,18 +206,24 @@
 
 
 def video_kernel(
-    heads, together, counts_ref, order_ref, table_ref, q_ref, before_ref, own_ref, after_ref, text_k_ref, text_v_ref, bias_ref,
-    out_ref, kv_ref, score_ref, sems,
+    heads, together, query_row, counts_ref, order_ref, table_ref, q_any, before_any, own_any, after_any, passing_any,
+    text_k_ref, text_v_ref, bias_ref, out_ref, kv_ref, q_ref, score_ref, sems,
 ):
-    copies = [
-        pltpu.make_async_copy(ref, kv_ref.at[pl.ds(n * LAYER, LAYER)], sems.at[n])
-        for n, ref in enumerate((before_ref, own_ref, after_ref))
+    rows = kv_ref.shape[1] // 2
+    moves = [
+        (before_any, kv_ref.at[pl.ds(0, LAYER)]),
+        (own_any.at[:, pl.ds(0, 2 * rows)], kv_ref.at[pl.ds(LAYER, LAYER)]),
+        (after_any, kv_ref.at[pl.ds(2 * LAYER, LAYER)]),
+        (q_any.at[:, pl.ds(query_row, rows)], q_ref),
     ]
+    if passing_any is not None:
+        moves.append((passing_any, out_ref.at[:, pl.ds(0, passing_any.shape[1])]))
+    copies = [pltpu.make_async_copy(source, target, sems.at[n]) for n, (source, target) in enumerate(moves)]
     for copy in copies:
         copy.start()
     for copy in copies:
         copy.wait()
-    rows = kv_ref.shape[1] // 2
+    first = out_ref.shape[1] - rows
 
     def unit_of(i):
         low = low_lanes(TILE)
@@ -246,36 +254,103 @@
                 for n, i in enumerate(tiles):
                     result = mixed[n] / totals[n]
                     if heads == 1:
-                        out_ref[i] = jnp.transpose(result).astype(BF16)
+                        out_ref[i, first:, :] = jnp.transpose(result).astype(BF16)
                     else:
-                        out_ref[i] = jnp.where(low_lanes(TILE), result[:TILE], result[TILE:]).astype(BF16)
+                        out_ref[i, first:, :] = jnp.where(low_lanes(TILE), result[:TILE], result[TILE:]).astype(BF16)
 
         return carry
 
     lax.fori_loop(0, LAYER // together, some_tiles, 0)
 
 
-def video_attention(heads, counts, order, table, queries, before, own, after, text_k, text_v, text_bias):
-    rows = heads * TILE
+def video_attention(heads, lists, queries, query_row, before, own, after, passing, text_k, text_v, text_bias):
+    rows = heads * HD
     together = 2
     smem = pl.BlockSpec(memory_space=pltpu.SMEM)
     vmem = pl.BlockSpec(memory_space=pltpu.VMEM)
     hbm = pl.BlockSpec(memory_space=pl.ANY)
     pairs = 300 * TILE * TILE * heads
-    return pl.pallas_call(
-        functools.partial(video_kernel, heads, together),
-        in_specs=[smem, smem, smem, vmem, hbm, hbm, hbm, vmem, vmem, vmem],
+    kernel = functools.partial(video_kernel, heads, together, query_row)
+    if passing is None:
+        arrays, out_rows = (), rows
+        called = lambda *refs: kernel(*refs[:7], None, *refs[7:])
+    else:
+        arrays, out_rows = (passing,), rows + passing.shape[1]
+        called = kernel
+    return pl.pallas_call(
+        called,
+        in_specs=[smem] * 3 + [hbm] * (4 + len(arrays)) + [vmem] * 3,
         out_specs=vmem,
-        out_shape=jax.ShapeDtypeStruct(queries.shape, BF16),
+        out_shape=jax.ShapeDtypeStruct((LAYER, out_rows, LANES), BF16),
         scratch_shapes=[
-            pltpu.VMEM((3 * LAYER,) + own.shape[1:], BF16),
-            pltpu.VMEM((together, 2 + SLOTS, rows, LANES), F32),
-            pltpu.SemaphoreType.DMA((3,)),
+            pltpu.VMEM((3 * LAYER, 2 * rows, LANES), BF16),
+            pltpu.VMEM((LAYER, rows, LANES), BF16),
+            pltpu.VMEM((together, 2 + SLOTS, heads * TILE, LANES), F32),
+            pltpu.SemaphoreType.DMA((5,)),
         ],
         compiler_params=pltpu.CompilerParams(vmem_limit_bytes=VMEM_LIMIT),
-        cost_estimate=pl.CostEstimate(flops=16 * HD * pairs, bytes_accessed=8 * own.size, transcendentals=pairs),
+        cost_estimate=pl.CostEstimate(flops=16 * HD * pairs, bytes_accessed=8 * before.size, transcendentals=pairs),
         name=f"video_attention_{heads}",
-    )(counts, order, table, queries, before, own, after, text_k, text_v, text_bias)
+    )(*lists, queries, before, own, after, *arrays, text_k, text_v, text_bias)
+
+
+def put_text(ref, means, weighs):
+    kept = ref.shape[0]
+    low = low_lanes(kept)
+    ref[:, :LANES] = jnp.where(low, means[0][:kept], means[1][:kept])
+    lane = lax.broadcasted_iota(jnp.int32, (kept, HD), 1)
+    last = jnp.zeros((kept, HD), F32)
+    for head in range(3):
+        last = jnp.where(lane == head, weighs[head][:kept], last)
+    ref[:, LANES:] = jnp.concatenate([means[2][:kept], last], axis=1)
+
+
+def merge_text(refs):
+    means, weighs = [], []
+    for head in range(3):
+        lane = LANES + HD + head
+        columns = slice(0, LANES) if head < 2 else slice(LANES, LANES + HD)
+        marks = [ref[:, lane : lane + 1] for ref in refs]
+        top = jnp.maximum(jnp.maximum(marks[0], marks[2]), jnp.maximum(marks[1], marks[3]))
+        weights = [jnp.exp2(mark - top) for mark in marks]
+        total = (weights[0] + weights[2]) + (weights[1] + weights[3])
+        parts = [ref[:, columns] * (weight / total) for ref, weight in zip(refs, weights)]
+        means.append((parts[0] + parts[2]) + (parts[1] + parts[3]))
+        weighs.append(top + jnp.log2(total))
+    return means, weighs
+
+
+def merge_kernel(*refs):
+    put_text(refs[4], *merge_text(refs[:4]))
+
+
+def last_merge_kernel(*refs):
+    means, _ = merge_text(refs[:4])
+    pair_ref, single_ref = refs[4:]
+    pair_ref[...] = jnp.where(low_lanes(means[0].shape[0]), means[0], means[1]).astype(BF16)
+    single_ref[...] = means[2].astype(BF16)
+
+
+def merge(parts, last):
+    vmem = pl.BlockSpec(memory_space=pltpu.VMEM)
+    rows = parts[0].shape[0]
+    return pl.pallas_call(
+        last_merge_kernel if last else merge_kernel,
+        in_specs=[vmem] * 4,
+        out_specs=[vmem] * 2 if last else vmem,
+        out_shape=[jax.ShapeDtypeStruct((rows, n), BF16) for n in (LANES, HD)] if last else parts[0],
+        name="text_merge",
+    )(*parts)
+
+
+def from_others(part, stride):
+    count = lax.axis_size("seq")
+    ring = 4 * stride
+    parts = [part]
+    for step in range(1, 4):
+        pairs = [(i, i // ring * ring + (i + step * stride) % ring) for i in range(count)]
+        parts.append(lax.ppermute(part, "seq", pairs))
+    return parts
 
 
 def text_kernel(
@@ -302,16 +377,13 @@
         text_k=single_k_ref[...],
         text_v=single_v_ref[...],
         keys=lambda slot: single_kv_ref[slot, :HD, :],
-        values=lambda slot: single_kv_ref[slot, HD:, :],
+        values=lambda slot: single_kv_ref[slot, HD : 2 * HD, :],
         bias=None,
     )
     tops, totals, mixed = attend_rows([pair_unit(0), pair_unit(1), single_unit], bias_ref[...], LAYER // GROUP, score_ref)
     means = [m / t for m, t in zip(mixed, totals)]
     weighs = [top * FACTOR + jnp.log2(total) for top, total in zip(tops, totals)]
-    kept = out_ref.shape[0]
-    out_ref[:, :LANES] = jnp.where(low, means[0], means[1])[:kept]
-    out_ref[:, LANES : 2 * LANES] = jnp.where(low, weighs[0], weighs[1])[:kept]
-    out_ref[:, 2 * LANES :] = jnp.concatenate([means[2], jnp.broadcast_to(weighs[2], means[2].shape)], axis=1)[:kept]
+    put_text(out_ref, means, weighs)
 
 
 def text_partial(pair_q, pair_kv, pair_k, pair_v, single_q, single_kv, single_k, single_v, bias):
@@ -321,7 +393,7 @@
         text_kernel,
         in_specs=[vmem] * 9,
         out_specs=vmem,
-        out_shape=jax.ShapeDtypeStruct((TEXT_KEPT, 3 * LANES), F32),
+        out_shape=jax.ShapeDtypeStruct((TEXT_KEPT, 2 * LANES), F32),
         scratch_shapes=[pltpu.VMEM((3, 2 + LAYER, TEXT_ROWS, LANES), F32)],
         compiler_params=pltpu.CompilerParams(vmem_limit_bytes=VMEM_LIMIT),
         cost_estimate=pl.CostEstimate(flops=16 * HD * pairs, bytes_accessed=4 * pair_kv.size, transcendentals=pairs),
@@ -329,28 +401,6 @@
     )(pair_q, pair_kv, pair_k, pair_v, single_q, single_kv, single_k, single_v, bias)
 
 
-def combine_kernel(parts_ref, pair_ref, single_ref):
-    def merged(means, weighs):
-        weights = jnp.exp2(weighs - jnp.max(weighs, axis=0, keepdims=True))
-        return (jnp.sum(means * weights, axis=0) / jnp.sum(weights, axis=0)).astype(BF16)
-
-    pair_ref[...] = merged(parts_ref[:, :, :LANES], parts_ref[:, :, LANES : 2 * LANES])
-    single_ref[...] = merged(parts_ref[:, :, 2 * LANES : 2 * LANES + HD], parts_ref[:, :, 2 * LANES + HD :])
-
-
-def combine(parts):
-    slabs, rows, _ = parts.shape
-    step = rows // 4
-    return pl.pallas_call(
-        combine_kernel,
-        grid=(rows // step,),
-        in_specs=[pl.BlockSpec((slabs, step, 3 * LANES), lambda i: (0, i, 0))],
-        out_specs=[pl.BlockSpec((step, LANES), lambda i: (i, 0)), pl.BlockSpec((step, HD), lambda i: (i, 0))],
-        out_shape=[jax.ShapeDtypeStruct((rows, LANES), BF16), jax.ShapeDtypeStruct((rows, HD), BF16)],
-        name="text_combine",
-    )(parts)
-
-
 def exchange(blocks, axis):
     return lax.all_to_all(blocks, axis, split_axis=0, concat_axis=0, tiled=True)
 
@@ -368,7 +418,6 @@
 
 def body(video_q, video_k, video_v, text_q, text_k, text_v, offsets, block_mask, text_mask):
     odd = lax.axis_index("head") % 2 == 1
-    counts, order, table = neighbour_lists(offsets, block_mask)
 
     def split_text(text):
         grown = jnp.pad(text, ((0, TEXT_ROWS - TEXT), (0, 0)))
@@ -380,27 +429,25 @@
     bias = jnp.where(text_live, 0.0, NEG_FILL).astype(F32)[None, :]
     own_bias = jnp.where(lax.axis_index("seq") == 0, bias, NEG_FILL)
 
+    lists = neighbour_lists(offsets, block_mask)
     single = exchange(pack_single(video_q, video_k, video_v), "head")
+    single = after(single, *lists)
     pair_kv, pair_q = pack_pair(video_q, video_k, video_v)
     pair_kv = exchange(after(pair_kv, single), "head")
-    single_kv, single_q = single[:, : 2 * HD], single[:, 2 * HD :]
-    single_before, single_after = both_sides(single_kv)
-    single_out = video_attention(
-        1, counts, order, table, single_q, single_before, single_kv, single_after, single_tk, single_tv, bias
+    single_before, single_after = both_sides(single[:, : 2 * HD])
+    mixed = video_attention(
+        1, lists, single, 2 * HD, single_before, single, single_after, pair_q, single_tk, single_tv, bias
     )
-    pair_kv = after(pair_kv, single_out)
-    pair_q = exchange(after(pair_q, pair_kv), "head")
+    pair_kv = after(pair_kv, mixed)
+    mixed = exchange(after(mixed, pair_kv), "head")
     pair_before, pair_after = both_sides(pair_kv)
-    partial = text_partial(
-        pair_tq, pair_kv, pair_tk, pair_tv, single_tq, single_kv, single_tk, single_tv, own_bias
-    )
-    parts = lax.all_gather(partial, "seq")
-    single_back = exchange(after(single_out, pair_q), "head")
-    pair_out = video_attention(2, counts, order, table, pair_q, pair_before, pair_kv, pair_after, pair_tk, pair_tv, bias)
-    pair_back = exchange(after(pair_out, single_back), "head")
-    video_out = unpack(single_back, pair_back)
-
-    pair_part, single_part = (part[:TEXT] for part in combine(parts))
+    partial = text_partial(pair_tq, pair_kv, pair_tk, pair_tv, single_tq, single, single_tk, single_tv, own_bias)
+    partial = merge(from_others(partial, 4), False)
+    mixed = after(mixed, partial)
+    pair_out = video_attention(2, lists, mixed, 0, pair_before, pair_kv, pair_after, None, pair_tk, pair_tv, bias)
+    video_out = unpack(mixed, exchange(pair_out, "head"))
+
+    pair_part, single_part = (part[:TEXT] for part in merge(from_others(partial, 1), True))
     text_out = jnp.where(
         odd,
         jnp.concatenate([single_part, pair_part], axis=1),

time: 195 us -> 184 us (0.944)
  blocking collectives: 48.9 us -> 0 us
  waiting for transfers between devices: 28 us -> 61.3 us
  starting transfers between devices: 31.9 us -> 47.3 us
  between operations: 14.3 us -> 1.1 us
  other arithmetic: 2.72 us -> 5.2 us
    all_to_all x2 -> x0, blocking collectives: 48.9 us -> none  [exchange(): return lax.all_to_all(blocks, axis, split_axis=0, concat_axis=0, tiled=True)]
    ppermute x0 -> x6, waiting for transfers between devices: none -> 33.4 us  [from_others(): parts.append(lax.ppermute(part, 'seq', pairs))]
    all_to_all x3 -> x4, starting transfers between devices: 16.1 us -> 27.8 us  [exchange(): return lax.all_to_all(blocks, axis, split_axis=0, concat_axis=0, tiled=True)]
    ppermute x0 -> x6, starting transfers between devices: none -> 7.53 us  [from_others(): parts.append(lax.ppermute(part, 'seq', pairs))]
    all_to_all x3 -> x4, waiting for transfers between devices: 19.5 us -> 15.3 us  [exchange(): return lax.all_to_all(blocks, axis, split_axis=0, concat_axis=0, tiled=True)]
    ppermute x4, waiting for transfers between devices: 8.5 us -> 12.5 us  [both_sides(): return (lax.ppermute(layer, 'seq', up), lax.ppermute(layer, 'seq', down))]
    unnamed x31 -> x44, local copies, waits for them, and re-layouts: 4.54 us -> 8.26 us
    ppermute x4, starting transfers between devices: 15.7 us -> 12 us  [both_sides(): return (lax.ppermute(layer, 'seq', up), lax.ppermute(layer, 'seq', down))]
  transfers between devices with their start and end apart: 8 -> 14, of which waited for: 4 -> 7; matrix products, arithmetic and copies ran while one was open for 4% -> 5% of each run, Pallas kernels for 22% -> 15%
where the time goes in v3:
time: 184 us; the launch traced here: 182 us
  waiting for transfers between devices  61.3 us (33%)
  Pallas kernels  56.3 us (31%)
  starting transfers between devices  47.3 us (26%)
  local copies, waits for them, and re-layouts  10.8 us (6%)
  other arithmetic  5.2 us (3%)
    pallas_call x2, Pallas kernels, video_attention(): pl.pallas_call(called, in_specs=[smem] * 3 + [hbm] * (4 + len(arrays)) +...  37 us
    ppermute x6, waiting for transfers between devices, from_others(): parts.append(lax.ppermute(part, 'seq', pairs))  33.4 us
    all_to_all x4, starting transfers between devices, exchange(): return lax.all_to_all(blocks, axis, split_axis=0, concat_axis=0, tiled=True)  27.8 us
    all_to_all x4, waiting for transfers between devices, exchange(): return lax.all_to_all(blocks, axis, split_axis=0, concat_axis=0, tiled=True)  15.3 us
    ppermute x4, waiting for transfers between devices, both_sides(): return (lax.ppermute(layer, 'seq', up), lax.ppermute(layer, 'seq', down))  12.5 us
    ppermute x4, starting transfers between devices, both_sides(): return (lax.ppermute(layer, 'seq', up), lax.ppermute(layer, 'seq', down))  12 us
    unnamed x44, local copies, waits for them, and re-layouts  8.26 us
    ppermute x6, starting transfers between devices, from_others(): parts.append(lax.ppermute(part, 'seq', pairs))  7.53 us
  transfers between devices with their start and end apart: 14, of which 7 were waited for; matrix products, arithmetic and copies ran while one was open for 5% of the time, Pallas kernels for 15%

profile of v3, /device:TPU:3, one launch (start us, length us, event | category | flops | bytes accessed | tf_op | source)
XLA Modules:
  0.0 182.0 jit_solution(11673571106416287858)
XLA Ops:
  0.6 3.6 %pack_single.1 = bf16[16,192,128]{2,1,0:T(8,128)(2,1)} custom-call(bf16[128,3072]{1,0:T(8,128)(2,1)} %q_ref.3, bf16[128,3072]{1,0:T(8,128)(2,1)} %k_ref.3, bf16[128,3072]{1,0:T(8,128)(2,1)} %v_ref.3), custom_call_target="tpu_custom_call" | custom-call | bytes 1572864 | tf_op jit(solution)/shard_map/pack_single/pallas_call | solution.py:61
  4.2 9.2 %all-to-all-start = ((bf16[16,192,128]{2,1,0:T(8,128)(2,1)}), bf16[16,192,128]{2,1,0:T(8,128)(2,1)S(1)}, u32[]{:S(2)}, u32[]{:S(2)}) async-start(bf16[16,192,128]{2,1,0:T(8,128)(2,1)} %pack_single.1), calls=%async_computation | async-start | bytes 1572864 | tf_op jit(solution)/shard_map/all_to_all | solution.py:405
  13.4 3.0 %pack_pair.1 = (bf16[16,256,128]{2,1,0:T(8,128)(2,1)}, bf16[16,128,128]{2,1,0:T(8,128)(2,1)}) custom-call(bf16[128,3072]{1,0:T(8,128)(2,1)} %q_ref.3, bf16[128,3072]{1,0:T(8,128)(2,1)} %k_ref.3, bf16[128,3072]{1,0:T(8,128)(2,1)} %v_ref.3), custom_call_target="tpu_custom_call" | custom-call | bytes 3145728 | tf_op jit(solution)/shard_map/pack_pair/pallas_call | solution.py:91
  20.7 15.3 %all-to-all-done.q_any.own_any.single_kv_ref = bf16[16,192,128]{2,1,0:T(8,128)(2,1)S(1)} async-done(((bf16[16,192,128]{2,1,0:T(8,128)(2,1)}), bf16[16,192,128]{2,1,0:T(8,128)(2,1)S(1)}, u32[]{:S(2)}, u32[]{:S(2)}) %all-to-all-start) | async-done | bytes 786464 | tf_op jit(solution)/shard_map/all_to_all | solution.py:405
  36.0 3.6 %all-to-all-start.1 = ((bf16[16,256,128]{2,1,0:T(8,128)(2,1)}), bf16[16,256,128]{2,1,0:T(8,128)(2,1)S(1)}, u32[]{:S(2)}, u32[]{:S(2)}) async-start(bf16[16,256,128]{2,1,0:T(8,128)(2,1)} %get-tuple-element.14), calls=%async_computation.1 | async-start | bytes 2097152 | tf_op jit(solution)/shard_map/all_to_all | solution.py:405
  39.7 4.6 %collective-permute-start.1 = (bf16[16,128,128]{2,1,0:T(8,128)(2,1)S(1)}, bf16[16,128,128]{2,1,0:T(8,128)(2,1)S(1)}, u32[]{:S(2)}, u32[]{:S(2)}) collective-permute-start(bf16[16,128,128]{2,1,0:T(8,128)(2,1)S(1)} %slice.58), channel_id=1, source_target_pairs={{16,0},{32,16},{48,32},{64,48},{80,64},{96,80},{112,96},{128,112},... | collective-permute-start | bytes 1572872 | tf_op jit(solution)/shard_map/ppermute | solution.py:412
  49.3 6.5 %collective-permute-done.1.after_any = bf16[16,128,128]{2,1,0:T(8,128)(2,1)S(1)} collective-permute-done((bf16[16,128,128]{2,1,0:T(8,128)(2,1)S(1)}, bf16[16,128,128]{2,1,0:T(8,128)(2,1)S(1)}, u32[]{:S(2)}, u32[]{:S(2)}) %collective-permute-start.1) | collective-permute-done | bytes 524320 | tf_op jit(solution)/shard_map/ppermute | solution.py:412
  55.8 6.0 %collective-permute-done.before_any = bf16[16,128,128]{2,1,0:T(8,128)(2,1)S(1)} collective-permute-done((bf16[16,128,128]{2,1,0:T(8,128)(2,1)S(1)}, bf16[16,128,128]{2,1,0:T(8,128)(2,1)S(1)}, u32[]{:S(2)}, u32[]{:S(2)}) %collective-permute-start) | collective-permute-done | bytes 524320 | tf_op jit(solution)/shard_map/ppermute | solution.py:412
  62.6 14.5 %video_attention_1.1 = bf16[16,192,128]{2,1,0:T(8,128)(2,1)} custom-call(s32[16]{0:T(128)} %copy-done.17, s32[16]{0:T(128)} %select_reduce_fusion.2.order_ref.refs_1_, s32[448]{0:T(512)} %reshape.182.table_ref.refs_2_, bf16[16,192,128]{2,1,0:T(8,128)(2,1)} %copy-done.1, bf16[16,128,128]{2,1,0:T(8,128)(2,1)} %copy-done.19, bf16[16,192,128]{2,1,0:T(8,128)(2,1)} %copy-done.1, ...), custom_call_target="tpu_custom_call" | custom-call | flops 5033164800 | bytes 2097152 | tf_op jit(solution)/shard_map/video_attention_1/pallas_call | solution.py:280
  77.2 7.4 %all-to-all-start.2 = ((bf16[16,192,128]{2,1,0:T(8,128)(2,1)}), bf16[16,192,128]{2,1,0:T(8,128)(2,1)S(1)}, u32[]{:S(2)}, u32[]{:S(2)}) async-start(bf16[16,192,128]{2,1,0:T(8,128)(2,1)} %video_attention_1.1), calls=%async_computation.2 | async-start | bytes 1572864 | tf_op jit(solution)/shard_map/all_to_all | solution.py:405
  86.5 3.6 %collective-permute-start.5 = (bf16[16,256,128]{2,1,0:T(8,128)(2,1)S(1)}, bf16[16,256,128]{2,1,0:T(8,128)(2,1)}, u32[]{:S(2)}, u32[]{:S(2)}) collective-permute-start(bf16[16,256,128]{2,1,0:T(8,128)(2,1)S(1)} %all-to-all-done.1.pair_kv_ref.refs_5_), channel_id=1, source_target_pairs={{0,16},{16,32},{32,48},{48,64},{64,80},{80,96},{96,112},{112,128},... | collective-permute-start | bytes 3145736 | tf_op jit(solution)/shard_map/ppermute | solution.py:412
  92.4 5.3 %text_partial.1.refs_0_ = f32[232,256]{1,0:T(8,128)} custom-call(bf16[256,128]{1,0:T(8,128)(2,1)} %fusion.7.pair_q_ref, bf16[16,256,128]{2,1,0:T(8,128)(2,1)} %copy-done.3, bf16[256,128]{1,0:T(8,128)(2,1)} %get-tuple-element.37.pair_k_ref.refs_7_, bf16[256,128]{1,0:T(8,128)(2,1)} %get-tuple-element.38.pair_v_ref.refs_8_, ...), custom_call_target="tpu_custom_call" | custom-call | flops 1811939328 | bytes 2097152 | tf_op jit(solution)/shard_map/text_partial/pallas_call | solution.py:392
  97.7 2.0 %collective-permute-start.3 = (f32[232,256]{1,0:T(8,128)}, f32[232,256]{1,0:T(8,128)S(1)}, u32[]{:S(2)}, u32[]{:S(2)}) collective-permute-start(f32[232,256]{1,0:T(8,128)} %text_partial.1.refs_0_), channel_id=1, source_target_pairs={{0,128},{16,144},{32,160},{48,176},{64,192},{80,208},{96,224},{112... | collective-permute-start | bytes 712712 | tf_op jit(solution)/shard_map/ppermute | solution.py:352
  99.6 2.0 %collective-permute-start.2 = (f32[232,256]{1,0:T(8,128)}, f32[232,256]{1,0:T(8,128)S(1)}, u32[]{:S(2)}, u32[]{:S(2)}) collective-permute-start(f32[232,256]{1,0:T(8,128)} %text_partial.1.refs_0_), channel_id=1, source_target_pairs={{0,64},{16,80},{32,96},{48,112},{64,128},{80,144},{96,160},{112,17... | collective-permute-start | bytes 712712 | tf_op jit(solution)/shard_map/ppermute | solution.py:352
  101.6 14.3 %collective-permute-done.4.refs_3_ = f32[232,256]{1,0:T(8,128)S(1)} collective-permute-done((f32[232,256]{1,0:T(8,128)}, f32[232,256]{1,0:T(8,128)S(1)}, u32[]{:S(2)}, u32[]{:S(2)}) %collective-permute-start.4) | collective-permute-done | bytes 237600 | tf_op jit(solution)/shard_map/ppermute | solution.py:352
  115.9 6.1 %collective-permute-done.3.refs_2_ = f32[232,256]{1,0:T(8,128)S(1)} collective-permute-done((f32[232,256]{1,0:T(8,128)}, f32[232,256]{1,0:T(8,128)S(1)}, u32[]{:S(2)}, u32[]{:S(2)}) %collective-permute-start.3) | collective-permute-done | bytes 237600 | tf_op jit(solution)/shard_map/ppermute | solution.py:352
  123.4 2.7 %text_merge.2.refs_0_ = f32[232,256]{1,0:T(8,128)} custom-call(f32[232,256]{1,0:T(8,128)} %text_partial.1.refs_0_, f32[232,256]{1,0:T(8,128)} %copy-done.7, f32[232,256]{1,0:T(8,128)} %copy-done.6, f32[232,256]{1,0:T(8,128)} %copy-done.5), custom_call_target="tpu_custom_call" | custom-call | tf_op jit(solution)/shard_map/text_merge/pallas_call | solution.py:337
  127.0 22.5 %video_attention_2.1 = bf16[16,128,128]{2,1,0:T(8,128)(2,1)} custom-call(s32[16]{0:T(128)} %copy-done.17, s32[16]{0:T(128)} %select_reduce_fusion.2.order_ref.refs_1_, s32[448]{0:T(512)} %reshape.182.table_ref.refs_2_, bf16[16,192,128]{2,1,0:T(8,128)(2,1)} %copy-done, bf16[16,256,128]{2,1,0:T(8,128)(2,1)} %collective-permute-done.5.refs_4_, ...), custom_call_target="tpu_custom_call" | custom-call | flops 10066329600 | bytes 4194304 | tf_op jit(solution)/shard_map/video_attention_2/pallas_call | solution.py:280
  149.5 7.7 %all-to-all-start.3 = ((bf16[16,128,128]{2,1,0:T(8,128)(2,1)}), bf16[16,128,128]{2,1,0:T(8,128)(2,1)S(1)}, u32[]{:S(2)}, u32[]{:S(2)}) async-start(bf16[16,128,128]{2,1,0:T(8,128)(2,1)} %video_attention_2.1), calls=%async_computation.3 | async-start | bytes 1048576 | tf_op jit(solution)/shard_map/all_to_all | solution.py:405
  157.1 2.9 %collective-permute-start.9 = (f32[232,256]{1,0:T(8,128)S(1)}, f32[232,256]{1,0:T(8,128)S(1)}, u32[]{:S(2)}, u32[]{:S(2)}) collective-permute-start(f32[232,256]{1,0:T(8,128)S(1)} %copy-done.4), channel_id=1, source_target_pairs={{0,48},{16,0},{32,16},{48,32},{64,112},{80,64},{96,80},{112,96},{1... | collective-permute-start | bytes 712712 | tf_op jit(solution)/shard_map/ppermute | solution.py:352
  160.7 9.4 %collective-permute-done.9.refs_3_ = f32[232,256]{1,0:T(8,128)S(1)} collective-permute-done((f32[232,256]{1,0:T(8,128)S(1)}, f32[232,256]{1,0:T(8,128)S(1)}, u32[]{:S(2)}, u32[]{:S(2)}) %collective-permute-start.9) | collective-permute-done | bytes 237600 | tf_op jit(solution)/shard_map/ppermute | solution.py:352
  170.1 3.7 %collective-permute-done.7.refs_1_ = f32[232,256]{1,0:T(8,128)S(1)} collective-permute-done((f32[232,256]{1,0:T(8,128)S(1)}, f32[232,256]{1,0:T(8,128)S(1)}, u32[]{:S(2)}, u32[]{:S(2)}) %collective-permute-start.7) | collective-permute-done | bytes 237600 | tf_op jit(solution)/shard_map/ppermute | solution.py:352
  174.5 2.5 %text_merge.3 = (bf16[232,128]{1,0:T(8,128)(2,1)}, bf16[232,64]{1,0:T(8,128)(2,1)}) custom-call(f32[232,256]{1,0:T(8,128)} %text_merge.2.refs_0_, f32[232,256]{1,0:T(8,128)} %copy-done.10, f32[232,256]{1,0:T(8,128)} %copy-done.9, f32[232,256]{1,0:T(8,128)} %copy-done.8), custom_call_target="tpu_custom_call" | custom-call | tf_op jit(solution)/shard_map/text_merge/pallas_call | solution.py:337
  179.5 2.3 %unpack.1 = bf16[128,3072]{1,0:T(8,128)(2,1)} custom-call(bf16[16,192,128]{2,1,0:T(8,128)(2,1)} %copy-done, bf16[16,128,128]{2,1,0:T(8,128)(2,1)} %copy-done.2), custom_call_target="tpu_custom_call" | custom-call | tf_op jit(solution)/shard_map/unpack/pallas_call | solution.py:128
  (81 shorter events, 20.5 us)
Async XLA Ops:
  4.2 31.8 %all-to-all-start = ((bf16[16,192,128]{2,1,0:T(8,128)(2,1)}), bf16[16,192,128]{2,1,0:T(8,128)(2,1)S(1)}, u32[]{:S(2)}, u32[]{:S(2)}) async-start(bf16[16,192,128]{2,1,0:T(8,128)(2,1)} %pack_single.1), calls=%async_computation | async-start | bytes 1572864 | tf_op jit(solution)/shard_map/all_to_all | solution.py:405
  36.0 3.6 %copy-start.1 = (bf16[16,192,128]{2,1,0:T(8,128)(2,1)}, bf16[16,192,128]{2,1,0:T(8,128)(2,1)S(1)}, u32[]{:S(2)}) copy-start(bf16[16,192,128]{2,1,0:T(8,128)(2,1)S(1)} %all-to-all-done.q_any.own_any.single_kv_ref) | copy-start | bytes 2359300
  36.0 41.2 %all-to-all-start.1 = ((bf16[16,256,128]{2,1,0:T(8,128)(2,1)}), bf16[16,256,128]{2,1,0:T(8,128)(2,1)S(1)}, u32[]{:S(2)}, u32[]{:S(2)}) async-start(bf16[16,256,128]{2,1,0:T(8,128)(2,1)} %get-tuple-element.14), calls=%async_computation.1 | async-start | bytes 2097152 | tf_op jit(solution)/shard_map/all_to_all | solution.py:405
  39.6 6.6 %copy-start.11 = (bf16[226,192]{0,1:T(8,128)(2,1)S(1)}, bf16[226,192]{0,1:T(8,128)(2,1)}, u32[]{:S(2)}) copy-start(bf16[226,192]{0,1:T(8,128)(2,1)} %param.13) | copy-start | bytes 260356
  39.7 16.2 %collective-permute-start.1 = (bf16[16,128,128]{2,1,0:T(8,128)(2,1)S(1)}, bf16[16,128,128]{2,1,0:T(8,128)(2,1)S(1)}, u32[]{:S(2)}, u32[]{:S(2)}) collective-permute-start(bf16[16,128,128]{2,1,0:T(8,128)(2,1)S(1)} %slice.58), channel_id=1, source_target_pairs={{16,0},{32,16},{48,32},{64,48},{80,64},{96,80},{112,96},{128,112},... | collective-permute-start | bytes 1572872 | tf_op jit(solution)/shard_map/ppermute | solution.py:412
  44.3 17.6 %collective-permute-start = (bf16[16,128,128]{2,1,0:T(8,128)(2,1)S(1)}, bf16[16,128,128]{2,1,0:T(8,128)(2,1)S(1)}, u32[]{:S(2)}, u32[]{:S(2)}) collective-permute-start(bf16[16,128,128]{2,1,0:T(8,128)(2,1)S(1)} %slice.58), channel_id=1, source_target_pairs={{0,16},{16,32},{32,48},{48,64},{64,80},{80,96},{96,112},{112,128},... | collective-permute-start | bytes 1572872 | tf_op jit(solution)/shard_map/ppermute | solution.py:412
  46.2 0.9 copy-start.12
  55.8 6.0 %copy-start.18 = (bf16[16,128,128]{2,1,0:T(8,128)(2,1)}, bf16[16,128,128]{2,1,0:T(8,128)(2,1)S(1)}, u32[]{:S(2)}) copy-start(bf16[16,128,128]{2,1,0:T(8,128)(2,1)S(1)} %collective-permute-done.1.after_any) | copy-start | bytes 1572868
  77.2 12.9 %copy-start.13 = (bf16[226,192]{0,1:T(8,128)(2,1)S(1)}, bf16[226,192]{0,1:T(8,128)(2,1)}, u32[]{:S(2)}) copy-start(bf16[226,192]{0,1:T(8,128)(2,1)} %param.12) | copy-start | bytes 260356
  77.2 14.4 %copy-start.3 = (bf16[16,256,128]{2,1,0:T(8,128)(2,1)}, bf16[16,256,128]{2,1,0:T(8,128)(2,1)S(1)}, u32[]{:S(2)}) copy-start(bf16[16,256,128]{2,1,0:T(8,128)(2,1)S(1)} %all-to-all-done.1.pair_kv_ref.refs_5_) | copy-start | bytes 3145732
  77.2 48.9 %all-to-all-start.2 = ((bf16[16,192,128]{2,1,0:T(8,128)(2,1)}), bf16[16,192,128]{2,1,0:T(8,128)(2,1)S(1)}, u32[]{:S(2)}, u32[]{:S(2)}) async-start(bf16[16,192,128]{2,1,0:T(8,128)(2,1)} %video_attention_1.1), calls=%async_computation.2 | async-start | bytes 1572864 | tf_op jit(solution)/shard_map/all_to_all | solution.py:405
  84.6 41.5 %collective-permute-start.6 = (bf16[16,256,128]{2,1,0:T(8,128)(2,1)S(1)}, bf16[16,256,128]{2,1,0:T(8,128)(2,1)}, u32[]{:S(2)}, u32[]{:S(2)}) collective-permute-start(bf16[16,256,128]{2,1,0:T(8,128)(2,1)S(1)} %all-to-all-done.1.pair_kv_ref.refs_5_), channel_id=1, source_target_pairs={{16,0},{32,16},{48,32},{64,48},{80,64},{96,80},{112,96},{128,112},... | collective-permute-start | bytes 3145736 | tf_op jit(solution)/shard_map/ppermute | solution.py:412
  86.5 39.6 %collective-permute-start.5 = (bf16[16,256,128]{2,1,0:T(8,128)(2,1)S(1)}, bf16[16,256,128]{2,1,0:T(8,128)(2,1)}, u32[]{:S(2)}, u32[]{:S(2)}) collective-permute-start(bf16[16,256,128]{2,1,0:T(8,128)(2,1)S(1)} %all-to-all-done.1.pair_kv_ref.refs_5_), channel_id=1, source_target_pairs={{0,16},{16,32},{32,48},{48,64},{64,80},{80,96},{96,112},{112,128},... | collective-permute-start | bytes 3145736 | tf_op jit(solution)/shard_map/ppermute | solution.py:412
  97.7 18.3 %collective-permute-start.4 = (f32[232,256]{1,0:T(8,128)}, f32[232,256]{1,0:T(8,128)S(1)}, u32[]{:S(2)}, u32[]{:S(2)}) collective-permute-start(f32[232,256]{1,0:T(8,128)} %text_partial.1.refs_0_), channel_id=1, source_target_pairs={{0,192},{16,208},{32,224},{48,240},{64,0},{80,16},{96,32},{112,48}... | collective-permute-start | bytes 712712 | tf_op jit(solution)/shard_map/ppermute | solution.py:352
  97.7 24.3 %collective-permute-start.3 = (f32[232,256]{1,0:T(8,128)}, f32[232,256]{1,0:T(8,128)S(1)}, u32[]{:S(2)}, u32[]{:S(2)}) collective-permute-start(f32[232,256]{1,0:T(8,128)} %text_partial.1.refs_0_), channel_id=1, source_target_pairs={{0,128},{16,144},{32,160},{48,176},{64,192},{80,208},{96,224},{112... | collective-permute-start | bytes 712712 | tf_op jit(solution)/shard_map/ppermute | solution.py:352
  99.6 22.4 %collective-permute-start.2 = (f32[232,256]{1,0:T(8,128)}, f32[232,256]{1,0:T(8,128)S(1)}, u32[]{:S(2)}, u32[]{:S(2)}) collective-permute-start(f32[232,256]{1,0:T(8,128)} %text_partial.1.refs_0_), channel_id=1, source_target_pairs={{0,64},{16,80},{32,96},{48,112},{64,128},{80,144},{96,160},{112,17... | collective-permute-start | bytes 712712 | tf_op jit(solution)/shard_map/ppermute | solution.py:352
  115.9 6.1 %copy-start.5 = (f32[232,256]{1,0:T(8,128)}, f32[232,256]{1,0:T(8,128)S(1)}, u32[]{:S(2)}) copy-start(f32[232,256]{1,0:T(8,128)S(1)} %collective-permute-done.4.refs_3_) | copy-start | bytes 712708
  149.4 7.7 %copy-start.4 = (f32[232,256]{1,0:T(8,128)S(1)}, f32[232,256]{1,0:T(8,128)}, u32[]{:S(2)}) copy-start(f32[232,256]{1,0:T(8,128)} %text_merge.2.refs_0_) | copy-start | bytes 712708
  149.5 29.2 %all-to-all-start.3 = ((bf16[16,128,128]{2,1,0:T(8,128)(2,1)}), bf16[16,128,128]{2,1,0:T(8,128)(2,1)S(1)}, u32[]{:S(2)}, u32[]{:S(2)}) async-start(bf16[16,128,128]{2,1,0:T(8,128)(2,1)} %video_attention_2.1), calls=%async_computation.3 | async-start | bytes 1048576 | tf_op jit(solution)/shard_map/all_to_all | solution.py:405
  157.1 12.9 %collective-permute-start.9 = (f32[232,256]{1,0:T(8,128)S(1)}, f32[232,256]{1,0:T(8,128)S(1)}, u32[]{:S(2)}, u32[]{:S(2)}) collective-permute-start(f32[232,256]{1,0:T(8,128)S(1)} %copy-done.4), channel_id=1, source_target_pairs={{0,48},{16,0},{32,16},{48,32},{64,112},{80,64},{96,80},{112,96},{1... | collective-permute-start | bytes 712712 | tf_op jit(solution)/shard_map/ppermute | solution.py:352
  160.0 10.1 %collective-permute-start.8 = (f32[232,256]{1,0:T(8,128)S(1)}, f32[232,256]{1,0:T(8,128)S(1)}, u32[]{:S(2)}, u32[]{:S(2)}) collective-permute-start(f32[232,256]{1,0:T(8,128)S(1)} %copy-done.4), channel_id=1, source_target_pairs={{0,32},{16,48},{32,0},{48,16},{64,96},{80,112},{96,64},{112,80},{1... | collective-permute-start | bytes 712712 | tf_op jit(solution)/shard_map/ppermute | solution.py:352
  160.0 13.7 %collective-permute-start.7 = (f32[232,256]{1,0:T(8,128)S(1)}, f32[232,256]{1,0:T(8,128)S(1)}, u32[]{:S(2)}, u32[]{:S(2)}) collective-permute-start(f32[232,256]{1,0:T(8,128)S(1)} %copy-done.4), channel_id=1, source_target_pairs={{0,16},{16,32},{32,48},{48,0},{64,80},{80,96},{96,112},{112,64},{1... | collective-permute-start | bytes 712712 | tf_op jit(solution)/shard_map/ppermute | solution.py:352
  170.1 3.7 %copy-start.8 = (f32[232,256]{1,0:T(8,128)}, f32[232,256]{1,0:T(8,128)S(1)}, u32[]{:S(2)}) copy-start(f32[232,256]{1,0:T(8,128)S(1)} %collective-permute-done.9.refs_3_) | copy-start | bytes 712708
  170.1 3.7 %copy-start.9 = (f32[232,256]{1,0:T(8,128)}, f32[232,256]{1,0:T(8,128)S(1)}, u32[]{:S(2)}) copy-start(f32[232,256]{1,0:T(8,128)S(1)} %collective-permute-done.8.refs_2_) | copy-start | bytes 712708
  (10 other events, 7.3 us)

commit v4 on v3

--- a/solution.py
+++ b/solution.py
@@ -39,64 +39,68 @@
     return lax.dot_general(a, b, (((1,), (0,)), ((), ())), preferred_element_type=F32)
 
 
-def pack_single_kernel(q_ref, k_ref, v_ref, out_ref, held_ref, sems):
+def pack_kernel(*refs):
+    count = len(refs) - 3
+    arrays, (out_ref, held_ref, sems) = refs[:count], refs[count:]
     groups = out_ref.shape[0]
 
-    def copy(n, u):
-        ref = (k_ref, v_ref, q_ref)[n]
-        return pltpu.make_async_copy(ref.at[:, pl.ds((3 * u + 1) * LANES, LANES)], held_ref.at[n, u], sems.at[n, u])
-
-    parts = [(n, u) for u in range(groups // 2) for n in range(3)]
-    for n, u in parts:
-        copy(n, u).start()
-    for n, u in parts:
-        copy(n, u).wait()
+    def single_copy(n, u):
+        source = arrays[n].at[:, pl.ds((3 * u + 1) * LANES, LANES)]
+        return pltpu.make_async_copy(source, held_ref.at[n, u], sems.at[n, groups + u])
+
+    def pair_copy(n, g):
+        source = arrays[n].at[:, pl.ds((g // 2 * 3 + g % 2 * 2) * LANES, LANES)]
+        return pltpu.make_async_copy(source, out_ref.at[g, pl.ds(count * HD + n * TILE, TILE)], sems.at[n, g])
+
+    singles = [(n, u) for u in range(groups // 2) for n in range(count)]
+    pairs = [(n, g) for g in range(groups) for n in range(count)]
+    for n, u in singles:
+        single_copy(n, u).start()
+    for n, g in pairs:
+        pair_copy(n, g).start()
+    for n, u in singles:
+        single_copy(n, u).wait()
         turned = jnp.transpose(held_ref[n, u])
         out_ref[2 * u, n * HD : (n + 1) * HD, :] = turned[:HD]
         out_ref[2 * u + 1, n * HD : (n + 1) * HD, :] = turned[HD:]
-
-
-def pack_single(video_q, video_k, video_v):
-    groups = video_q.shape[1] // (3 * HD)
-    return pl.pallas_call(
-        pack_single_kernel,
-        in_specs=[pl.BlockSpec(memory_space=pl.ANY)] * 3,
+    for n, g in pairs:
+        pair_copy(n, g).wait()
+
+
+def pack(*arrays):
+    count = len(arrays)
+    groups = arrays[0].shape[1] // (3 * HD)
+    return pl.pallas_call(
+        pack_kernel,
+        in_specs=[pl.BlockSpec(memory_space=pl.ANY)] * count,
         out_specs=pl.BlockSpec(memory_space=pltpu.VMEM),
-        out_shape=jax.ShapeDtypeStruct((groups, 3 * HD, LANES), BF16),
+        out_shape=jax.ShapeDtypeStruct((groups, count * 3 * HD, LANES), BF16),
         scratch_shapes=[
-            pltpu.VMEM((3, groups // 2, TILE, LANES), BF16),
-            pltpu.SemaphoreType.DMA((3, groups // 2)),
+            pltpu.VMEM((count, groups // 2, TILE, LANES), BF16),
+            pltpu.SemaphoreType.DMA((count, groups + groups // 2)),
         ],
-        cost_estimate=pl.CostEstimate(flops=0, bytes_accessed=4 * video_q.size, transcendentals=0),
-        name="pack_single",
-    )(video_q, video_k, video_v)
-
-
-def pack_pair_kernel(q_ref, k_ref, v_ref, kv_ref, out_q_ref, sems):
-    copies = []
-    for n, ref in enumerate((k_ref, v_ref, q_ref)):
-        for g in range(out_q_ref.shape[0]):
-            source = ref.at[:, pl.ds((g // 2 * 3 + g % 2 * 2) * LANES, LANES)]
-            target = kv_ref.at[g, pl.ds(n * TILE, TILE)] if n < 2 else out_q_ref.at[g]
-            copies.append(pltpu.make_async_copy(source, target, sems.at[n, g]))
-    for copy in copies:
-        copy.start()
-    for copy in copies:
-        copy.wait()
-
-
-def pack_pair(video_q, video_k, video_v):
-    groups = video_q.shape[1] // (3 * HD)
+        cost_estimate=pl.CostEstimate(flops=0, bytes_accessed=4 * count * arrays[0].size, transcendentals=0),
+        name="pack",
+    )(*arrays)
+
+
+def take_pair_kernel(kv_ref, token_ref, out_ref, sem):
+    del token_ref
+    copy = pltpu.make_async_copy(kv_ref.at[:, pl.ds(2 * HD, 2 * TILE)], out_ref, sem)
+    copy.start()
+    copy.wait()
+
+
+def take_pair(kv, token):
     any_space = pl.BlockSpec(memory_space=pl.ANY)
     return pl.pallas_call(
-        pack_pair_kernel,
-        in_specs=[any_space] * 3,
-        out_specs=[pl.BlockSpec(memory_space=pltpu.VMEM)] * 2,
-        out_shape=[jax.ShapeDtypeStruct((groups, r, LANES), BF16) for r in (2 * TILE, TILE)],
-        scratch_shapes=[pltpu.SemaphoreType.DMA((3, groups))],
-        cost_estimate=pl.CostEstimate(flops=0, bytes_accessed=8 * video_q.size, transcendentals=0),
-        name="pack_pair",
-    )(video_q, video_k, video_v)
+        take_pair_kernel,
+        in_specs=[any_space] * 2,
+        out_specs=pl.BlockSpec(memory_space=pltpu.VMEM),
+        out_shape=jax.ShapeDtypeStruct((kv.shape[0], 2 * TILE, LANES), BF16),
+        scratch_shapes=[pltpu.SemaphoreType.DMA],
+        name="take_pair",
+    )(kv, token)
 
 
 def unpack_kernel(single_ref, pair_ref, out_ref, held_ref, single_sems, pair_sems):
@@ -206,24 +210,21 @@
 
 
 def video_kernel(
-    heads, together, query_row, counts_ref, order_ref, table_ref, q_any, before_any, own_any, after_any, passing_any,
+    heads, together, query_row, own_row, counts_ref, order_ref, table_ref, q_any, before_any, own_any, after_any,
     text_k_ref, text_v_ref, bias_ref, out_ref, kv_ref, q_ref, score_ref, sems,
 ):
     rows = kv_ref.shape[1] // 2
     moves = [
         (before_any, kv_ref.at[pl.ds(0, LAYER)]),
-        (own_any.at[:, pl.ds(0, 2 * rows)], kv_ref.at[pl.ds(LAYER, LAYER)]),
+        (own_any.at[:, pl.ds(own_row, 2 * rows)], kv_ref.at[pl.ds(LAYER, LAYER)]),
         (after_any, kv_ref.at[pl.ds(2 * LAYER, LAYER)]),
         (q_any.at[:, pl.ds(query_row, rows)], q_ref),
     ]
-    if passing_any is not None:
-        moves.append((passing_any, out_ref.at[:, pl.ds(0, passing_any.shape[1])]))
     copies = [pltpu.make_async_copy(source, target, sems.at[n]) for n, (source, target) in enumerate(moves)]
     for copy in copies:
         copy.start()
     for copy in copies:
         copy.wait()
-    first = out_ref.shape[1] - rows
 
     def unit_of(i):
         low = low_lanes(TILE)
@@ -254,44 +255,37 @@
                 for n, i in enumerate(tiles):
                     result = mixed[n] / totals[n]
                     if heads == 1:
-                        out_ref[i, first:, :] = jnp.transpose(result).astype(BF16)
+                        out_ref[i] = jnp.transpose(result).astype(BF16)
                     else:
-                        out_ref[i, first:, :] = jnp.where(low_lanes(TILE), result[:TILE], result[TILE:]).astype(BF16)
+                        out_ref[i] = jnp.where(low_lanes(TILE), result[:TILE], result[TILE:]).astype(BF16)
 
         return carry
 
     lax.fori_loop(0, LAYER // together, some_tiles, 0)
 
 
-def video_attention(heads, lists, queries, query_row, before, own, after, passing, text_k, text_v, text_bias):
+def video_attention(heads, lists, queries, query_row, before, own, own_row, after, text_k, text_v, text_bias):
     rows = heads * HD
     together = 2
     smem = pl.BlockSpec(memory_space=pltpu.SMEM)
     vmem = pl.BlockSpec(memory_space=pltpu.VMEM)
     hbm = pl.BlockSpec(memory_space=pl.ANY)
     pairs = 300 * TILE * TILE * heads
-    kernel = functools.partial(video_kernel, heads, together, query_row)
-    if passing is None:
-        arrays, out_rows = (), rows
-        called = lambda *refs: kernel(*refs[:7], None, *refs[7:])
-    else:
-        arrays, out_rows = (passing,), rows + passing.shape[1]
-        called = kernel
-    return pl.pallas_call(
-        called,
-        in_specs=[smem] * 3 + [hbm] * (4 + len(arrays)) + [vmem] * 3,
+    return pl.pallas_call(
+        functools.partial(video_kernel, heads, together, query_row, own_row),
+        in_specs=[smem] * 3 + [hbm] * 4 + [vmem] * 3,
         out_specs=vmem,
-        out_shape=jax.ShapeDtypeStruct((LAYER, out_rows, LANES), BF16),
+        out_shape=jax.ShapeDtypeStruct((LAYER, rows, LANES), BF16),
         scratch_shapes=[
             pltpu.VMEM((3 * LAYER, 2 * rows, LANES), BF16),
             pltpu.VMEM((LAYER, rows, LANES), BF16),
             pltpu.VMEM((together, 2 + SLOTS, heads * TILE, LANES), F32),
-            pltpu.SemaphoreType.DMA((5,)),
+            pltpu.SemaphoreType.DMA((4,)),
         ],
         compiler_params=pltpu.CompilerParams(vmem_limit_bytes=VMEM_LIMIT),
         cost_estimate=pl.CostEstimate(flops=16 * HD * pairs, bytes_accessed=8 * before.size, transcendentals=pairs),
         name=f"video_attention_{heads}",
-    )(*lists, queries, before, own, after, *arrays, text_k, text_v, text_bias)
+    )(*lists, queries, before, own, after, text_k, text_v, text_bias)
 
 
 def put_text(ref, means, weighs):
@@ -354,9 +348,10 @@
 
 
 def text_kernel(
-    pair_q_ref, pair_kv_ref, pair_k_ref, pair_v_ref, single_q_ref, single_kv_ref, single_k_ref, single_v_ref, bias_ref,
-    out_ref, score_ref,
+    kv_ref, pair_q_ref, pair_k_ref, pair_v_ref, single_q_ref, single_k_ref, single_v_ref, bias_ref,
+    before_any, after_any, out_ref, score_ref,
 ):
+    del before_any, after_any
     low = low_lanes(TEXT_ROWS)
     pair_q = pair_q_ref[...].astype(F32)
 
@@ -366,8 +361,8 @@
             queries=jnp.where(low if head == 0 else ~low, pair_q, 0.0).astype(BF16),
             text_k=pair_k_ref[...],
             text_v=pair_v_ref[...],
-            keys=lambda slot: pair_kv_ref[slot, :TILE, :],
-            values=lambda slot: pair_kv_ref[slot, TILE:, :],
+            keys=lambda slot: kv_ref[slot, 2 * HD : 2 * HD + TILE, :],
+            values=lambda slot: kv_ref[slot, 2 * HD + TILE :, :],
             bias=None,
         )
 
@@ -376,8 +371,8 @@
         queries=single_q_ref[...],
         text_k=single_k_ref[...],
         text_v=single_v_ref[...],
-        keys=lambda slot: single_kv_ref[slot, :HD, :],
-        values=lambda slot: single_kv_ref[slot, HD : 2 * HD, :],
+        keys=lambda slot: kv_ref[slot, :HD, :],
+        values=lambda slot: kv_ref[slot, HD : 2 * HD, :],
         bias=None,
     )
     tops, totals, mixed = attend_rows([pair_unit(0), pair_unit(1), single_unit], bias_ref[...], LAYER // GROUP, score_ref)
@@ -386,19 +381,19 @@
     put_text(out_ref, means, weighs)
 
 
-def text_partial(pair_q, pair_kv, pair_k, pair_v, single_q, single_kv, single_k, single_v, bias):
+def text_partial(kv, pair_q, pair_k, pair_v, single_q, single_k, single_v, bias, earlier):
     vmem = pl.BlockSpec(memory_space=pltpu.VMEM)
     pairs = 3 * TEXT_ROWS * (LAYER + 2) * TILE
     return pl.pallas_call(
         text_kernel,
-        in_specs=[vmem] * 9,
+        in_specs=[vmem] * 8 + [pl.BlockSpec(memory_space=pl.ANY)] * len(earlier),
         out_specs=vmem,
         out_shape=jax.ShapeDtypeStruct((TEXT_KEPT, 2 * LANES), F32),
         scratch_shapes=[pltpu.VMEM((3, 2 + LAYER, TEXT_ROWS, LANES), F32)],
         compiler_params=pltpu.CompilerParams(vmem_limit_bytes=VMEM_LIMIT),
-        cost_estimate=pl.CostEstimate(flops=16 * HD * pairs, bytes_accessed=4 * pair_kv.size, transcendentals=pairs),
+        cost_estimate=pl.CostEstimate(flops=16 * HD * pairs, bytes_accessed=4 * kv.size, transcendentals=pairs),
         name="text_partial",
-    )(pair_q, pair_kv, pair_k, pair_v, single_q, single_kv, single_k, single_v, bias)
+    )(kv, pair_q, pair_k, pair_v, single_q, single_k, single_v, bias, *earlier)
 
 
 def exchange(blocks, axis):
@@ -430,24 +425,29 @@
     own_bias = jnp.where(lax.axis_index("seq") == 0, bias, NEG_FILL)
 
     lists = neighbour_lists(offsets, block_mask)
-    single = exchange(pack_single(video_q, video_k, video_v), "head")
-    single = after(single, *lists)
-    pair_kv, pair_q = pack_pair(video_q, video_k, video_v)
-    pair_kv = exchange(after(pair_kv, single), "head")
-    single_before, single_after = both_sides(single[:, : 2 * HD])
-    mixed = video_attention(
-        1, lists, single, 2 * HD, single_before, single, single_after, pair_q, single_tk, single_tv, bias
+    text = (pair_tq, pair_tk, pair_tv, single_tq, single_tk, single_tv)
+    kv = exchange(pack(video_k, video_v), "head")
+    kv, queries, *rest = lax.optimization_barrier((kv, pack(video_q)) + lists + text)
+    lists, (pair_tq, pair_tk, pair_tv, single_tq, single_tk, single_tv) = rest[:3], rest[3:]
+    queries = exchange(after(queries, kv), "head")
+    single_before, single_after = both_sides(kv[:, : 2 * HD])
+    token, _ = both_sides(kv[0, :16])
+    pair_before, pair_after = both_sides(take_pair(kv, token))
+    partial = text_partial(kv, pair_tq, pair_tk, pair_tv, single_tq, single_tk, single_tv, own_bias, (single_before, single_after))
+    partial = from_others(partial, 4)
+
+    single_out = video_attention(
+        1, lists, queries, 0, single_before, kv, 0, single_after, single_tk, single_tv, bias
     )
-    pair_kv = after(pair_kv, mixed)
-    mixed = exchange(after(mixed, pair_kv), "head")
-    pair_before, pair_after = both_sides(pair_kv)
-    partial = text_partial(pair_tq, pair_kv, pair_tk, pair_tv, single_tq, single, single_tk, single_tv, own_bias)
-    partial = merge(from_others(partial, 4), False)
-    mixed = after(mixed, partial)
-    pair_out = video_attention(2, lists, mixed, 0, pair_before, pair_kv, pair_after, None, pair_tk, pair_tv, bias)
-    video_out = unpack(mixed, exchange(pair_out, "head"))
-
-    pair_part, single_part = (part[:TEXT] for part in merge(from_others(partial, 1), True))
+    *partial, single_out = lax.optimization_barrier((*partial, single_out))
+    single_back = exchange(single_out, "head")
+    partial = from_others(merge(partial, False), 1)
+    pair_q = after(queries, single_out)
+    pair_out = video_attention(2, lists, pair_q, HD, pair_before, kv, 2 * HD, pair_after, pair_tk, pair_tv, bias)
+    pair_back = exchange(after(pair_out, single_back, *partial), "head")
+    video_out = unpack(single_back, pair_back)
+
+    pair_part, single_part = (part[:TEXT] for part in merge(partial, True))
     text_out = jnp.where(
         odd,
         jnp.concatenate([single_part, pair_part], axis=1),

time: 184 us -> 184 us (level)
  starting transfers between devices: 47.3 us -> 53.1 us
  local copies, waits for them, and re-layouts: 10.8 us -> 7.38 us
  waiting for transfers between devices: 61.3 us -> 58.6 us
    all_to_all x4, waiting for transfers between devices: 15.3 us -> 43.9 us  [exchange(): return lax.all_to_all(blocks, axis, split_axis=0, concat_axis=0, tiled=True)]
    ppermute x6, waiting for transfers between devices: 33.4 us -> 6.47 us  [from_others(): parts.append(lax.ppermute(part, 'seq', pairs))]
    ppermute x4 -> x5, starting transfers between devices: 12 us -> 16.7 us  [both_sides(): return (lax.ppermute(layer, 'seq', up), lax.ppermute(layer, 'seq', down))]
    ppermute x4 -> x5, waiting for transfers between devices: 12.5 us -> 8.22 us  [both_sides(): return (lax.ppermute(layer, 'seq', up), lax.ppermute(layer, 'seq', down))]
    unnamed x44 -> x42, local copies, waits for them, and re-layouts: 8.26 us -> 4.91 us
    all_to_all x4, starting transfers between devices: 27.8 us -> 29.8 us  [exchange(): return lax.all_to_all(blocks, axis, split_axis=0, concat_axis=0, tiled=True)]
    pallas_call x5 -> x6, Pallas kernels: 48.9 us -> 50.2 us  [the longest x2 36.6 us: video_attention(): pl.pallas_call(functools.partial(video_kernel, heads, together, query_row...]
  transfers between devices with their start and end apart: 14 -> 15, of which waited for: 7 -> 5; matrix products, arithmetic and copies ran while one was open for 5% -> 5% of each run, Pallas kernels for 15% -> 28%
where the time goes in v4:
time: 184 us; the launch traced here: 183 us
  waiting for transfers between devices  58.6 us (32%)
  Pallas kernels  57.5 us (31%)
  starting transfers between devices  53.1 us (29%)
  local copies, waits for them, and re-layouts  7.38 us (4%)
  other arithmetic  5.19 us (3%)
    all_to_all x4, waiting for transfers between devices, exchange(): return lax.all_to_all(blocks, axis, split_axis=0, concat_axis=0, tiled=True)  43.9 us
    pallas_call x2, Pallas kernels, video_attention(): pl.pallas_call(functools.partial(video_kernel, heads, together, query_row...  36.6 us
    all_to_all x4, starting transfers between devices, exchange(): return lax.all_to_all(blocks, axis, split_axis=0, concat_axis=0, tiled=True)  29.8 us
    ppermute x5, starting transfers between devices, both_sides(): return (lax.ppermute(layer, 'seq', up), lax.ppermute(layer, 'seq', down))  16.7 us
    ppermute x5, waiting for transfers between devices, both_sides(): return (lax.ppermute(layer, 'seq', up), lax.ppermute(layer, 'seq', down))  8.22 us
    ppermute x6, starting transfers between devices, from_others(): parts.append(lax.ppermute(part, 'seq', pairs))  6.59 us
    ppermute x6, waiting for transfers between devices, from_others(): parts.append(lax.ppermute(part, 'seq', pairs))  6.47 us
    pallas_call x2, Pallas kernels, pack(): pl.pallas_call(pack_kernel, in_specs=[pl.BlockSpec(memory_space=pl.ANY)]...  6.1 us
  transfers between devices with their start and end apart: 15, of which 5 were waited for; matrix products, arithmetic and copies ran while one was open for 5% of the time, Pallas kernels for 28%

profile of v4, /device:TPU:3, one launch (start us, length us, event | category | flops | bytes accessed | tf_op | source)
XLA Modules:
  0.0 183.1 jit_solution(7491553758287446938)
XLA Ops:
  0.6 3.6 %pack.2 = bf16[16,384,128]{2,1,0:T(8,128)(2,1)} custom-call(bf16[128,3072]{1,0:T(8,128)(2,1)} %refs_0_.2, bf16[128,3072]{1,0:T(8,128)(2,1)} %refs_1_.1), custom_call_target="tpu_custom_call" | custom-call | bytes 3145728 | tf_op jit(solution)/shard_map/pack/pallas_call | solution.py:73
  4.2 9.2 %all-to-all-start = ((bf16[16,384,128]{2,1,0:T(8,128)(2,1)}), bf16[16,384,128]{2,1,0:T(8,128)(2,1)S(1)}, u32[]{:S(2)}, u32[]{:S(2)}) async-start(bf16[16,384,128]{2,1,0:T(8,128)(2,1)} %pack.2), calls=%async_computation | async-start | bytes 3145728 | tf_op jit(solution)/shard_map/all_to_all | solution.py:400
  13.4 2.5 %pack.3 = bf16[16,192,128]{2,1,0:T(8,128)(2,1)} custom-call(bf16[128,3072]{1,0:T(8,128)(2,1)} %refs_0_.3), custom_call_target="tpu_custom_call" | custom-call | bytes 1572864 | tf_op jit(solution)/shard_map/pack/pallas_call | solution.py:73
  21.0 30.8 %all-to-all-done.kv_ref.own_any = bf16[16,384,128]{2,1,0:T(8,128)(2,1)S(1)} async-done(((bf16[16,384,128]{2,1,0:T(8,128)(2,1)}), bf16[16,384,128]{2,1,0:T(8,128)(2,1)S(1)}, u32[]{:S(2)}, u32[]{:S(2)}) %all-to-all-start) | async-done | bytes 1572896 | tf_op jit(solution)/shard_map/all_to_all | solution.py:400
  51.8 4.3 %all-to-all-start.1 = ((bf16[16,192,128]{2,1,0:T(8,128)(2,1)}), bf16[16,192,128]{2,1,0:T(8,128)(2,1)S(1)}, u32[]{:S(2)}, u32[]{:S(2)}) async-start(bf16[16,192,128]{2,1,0:T(8,128)(2,1)} %pack.3), calls=%async_computation.1 | async-start | bytes 1572864 | tf_op jit(solution)/shard_map/all_to_all | solution.py:400
  56.1 3.2 %collective-permute-start = (bf16[16,128,128]{2,1,0:T(8,128)(2,1)S(1)}, bf16[16,128,128]{2,1,0:T(8,128)(2,1)S(1)}, u32[]{:S(2)}, u32[]{:S(2)}) collective-permute-start(bf16[16,128,128]{2,1,0:T(8,128)(2,1)S(1)} %slice.73), channel_id=1, source_target_pairs={{0,16},{16,32},{32,48},{48,64},{64,80},{80,96},{96,112},{112,128},... | collective-permute-start | bytes 1572872 | tf_op jit(solution)/shard_map/ppermute | solution.py:407
  59.4 4.2 %collective-permute-start.1 = (bf16[16,128,128]{2,1,0:T(8,128)(2,1)S(1)}, bf16[16,128,128]{2,1,0:T(8,128)(2,1)}, u32[]{:S(2)}, u32[]{:S(2)}) collective-permute-start(bf16[16,128,128]{2,1,0:T(8,128)(2,1)S(1)} %slice.73), channel_id=1, source_target_pairs={{16,0},{32,16},{48,32},{64,48},{80,64},{96,80},{112,96},{128,112},... | collective-permute-start | bytes 1572872 | tf_op jit(solution)/shard_map/ppermute | solution.py:407
  65.5 8.2 %collective-permute-done.5.token_ref = bf16[16,128]{1,0:T(8,128)(2,1)S(1)} collective-permute-done((bf16[16,128]{1,0:T(8,128)(2,1)S(1)}, bf16[16,128]{1,0:T(8,128)(2,1)S(1)}, u32[]{:S(2)}, u32[]{:S(2)}) %collective-permute-start.5) | collective-permute-done | bytes 4128 | tf_op jit(solution)/shard_map/ppermute | solution.py:407
  74.3 2.2 %take_pair.1 = bf16[16,256,128]{2,1,0:T(8,128)(2,1)} custom-call(bf16[16,384,128]{2,1,0:T(8,128)(2,1)} %copy-done, bf16[16,128]{1,0:T(8,128)(2,1)} %copy-done.14), custom_call_target="tpu_custom_call" | custom-call | tf_op jit(solution)/shard_map/take_pair/pallas_call | solution.py:96
  76.5 1.9 %collective-permute-start.6 = (bf16[16,256,128]{2,1,0:T(8,128)(2,1)}, bf16[16,256,128]{2,1,0:T(8,128)(2,1)}, u32[]{:S(2)}, u32[]{:S(2)}) collective-permute-start(bf16[16,256,128]{2,1,0:T(8,128)(2,1)} %take_pair.1), channel_id=1, source_target_pairs={{0,16},{16,32},{32,48},{48,64},{64,80},{80,96},{96,112},{112,128},... | collective-permute-start | bytes 3145736 | tf_op jit(solution)/shard_map/ppermute | solution.py:407
  78.5 5.5 %collective-permute-start.7 = (bf16[16,256,128]{2,1,0:T(8,128)(2,1)}, bf16[16,256,128]{2,1,0:T(8,128)(2,1)}, u32[]{:S(2)}, u32[]{:S(2)}) collective-permute-start(bf16[16,256,128]{2,1,0:T(8,128)(2,1)} %take_pair.1), channel_id=1, source_target_pairs={{16,0},{32,16},{48,32},{64,48},{80,64},{96,80},{112,96},{128,112},... | collective-permute-start | bytes 3145736 | tf_op jit(solution)/shard_map/ppermute | solution.py:407
  86.8 5.4 %text_partial.1.refs_0_ = f32[232,256]{1,0:T(8,128)} custom-call(bf16[16,384,128]{2,1,0:T(8,128)(2,1)} %copy-done, bf16[256,128]{1,0:T(8,128)(2,1)} %get-tuple-element.24.pair_q_ref, bf16[256,128]{1,0:T(8,128)(2,1)} %get-tuple-element.25.pair_k_ref.text_k_ref, bf16[256,128]{1,0:T(8,128)(2,1)} %fusion.6.pair_v_ref.text_v_ref, ...), custom_call_target="tpu_custom_call" | custom-call | flops 1811939328 | bytes 3145728 | tf_op jit(solution)/shard_map/text_partial/pallas_call | solution.py:387
  94.0 2.1 %collective-permute-start.4 = (f32[232,256]{1,0:T(8,128)}, f32[232,256]{1,0:T(8,128)S(1)}, u32[]{:S(2)}, u32[]{:S(2)}) collective-permute-start(f32[232,256]{1,0:T(8,128)} %text_partial.1.refs_0_), channel_id=1, source_target_pairs={{0,192},{16,208},{32,224},{48,240},{64,0},{80,16},{96,32},{112,48}... | collective-permute-start | bytes 712712 | tf_op jit(solution)/shard_map/ppermute | solution.py:346
  96.9 14.1 %video_attention_1.1 = bf16[16,64,128]{2,1,0:T(8,128)(2,1)} custom-call(s32[16]{0:T(128)} %copy-done.17, s32[16]{0:T(128)} %select_reduce_fusion.2.order_ref, s32[448]{0:T(512)} %reshape.182.table_ref, bf16[16,192,128]{2,1,0:T(8,128)(2,1)} %copy-done.3, bf16[16,128,128]{2,1,0:T(8,128)(2,1)} %copy-done.18, bf16[16,384,128]{2,1,0:T(8,128)(2,1)} %copy-done, ...), custom_call_target="tpu_custom_call" | custom-call | flops 5033164800 | bytes 2097152 | tf_op jit(solution)/shard_map/video_attention_1/pallas_call | solution.py:274
  111.1 2.1 %collective-permute-done.3.refs_2_ = f32[232,256]{1,0:T(8,128)S(1)} collective-permute-done((f32[232,256]{1,0:T(8,128)}, f32[232,256]{1,0:T(8,128)S(1)}, u32[]{:S(2)}, u32[]{:S(2)}) %collective-permute-start.3) | collective-permute-done | bytes 237600 | tf_op jit(solution)/shard_map/ppermute | solution.py:346
  113.1 4.4 %collective-permute-done.4.refs_3_ = f32[232,256]{1,0:T(8,128)S(1)} collective-permute-done((f32[232,256]{1,0:T(8,128)}, f32[232,256]{1,0:T(8,128)S(1)}, u32[]{:S(2)}, u32[]{:S(2)}) %collective-permute-start.4) | collective-permute-done | bytes 237600 | tf_op jit(solution)/shard_map/ppermute | solution.py:346
  118.3 2.7 %text_merge.2.refs_0_ = f32[232,256]{1,0:T(8,128)} custom-call(f32[232,256]{1,0:T(8,128)} %text_partial.1.refs_0_, f32[232,256]{1,0:T(8,128)} %copy-done.4, f32[232,256]{1,0:T(8,128)} %copy-done.5, f32[232,256]{1,0:T(8,128)} %copy-done.6), custom_call_target="tpu_custom_call" | custom-call | tf_op jit(solution)/shard_map/text_merge/pallas_call | solution.py:331
  120.9 2.7 %collective-permute-start.10 = (f32[232,256]{1,0:T(8,128)}, f32[232,256]{1,0:T(8,128)S(1)}, u32[]{:S(2)}, u32[]{:S(2)}) collective-permute-start(f32[232,256]{1,0:T(8,128)} %text_merge.2.refs_0_), channel_id=1, source_target_pairs={{0,48},{16,0},{32,16},{48,32},{64,112},{80,64},{96,80},{112,96},{1... | collective-permute-start | bytes 712712 | tf_op jit(solution)/shard_map/ppermute | solution.py:346
  123.6 9.2 %all-to-all-start.2 = ((bf16[16,64,128]{2,1,0:T(8,128)(2,1)}), bf16[16,64,128]{2,1,0:T(8,128)(2,1)S(1)}, u32[]{:S(2)}, u32[]{:S(2)}) async-start(bf16[16,64,128]{2,1,0:T(8,128)(2,1)} %video_attention_1.1), calls=%async_computation.2 | async-start | bytes 524288 | tf_op jit(solution)/shard_map/all_to_all | solution.py:400
  132.8 22.4 %video_attention_2.1 = bf16[16,128,128]{2,1,0:T(8,128)(2,1)} custom-call(s32[16]{0:T(128)} %copy-done.17, s32[16]{0:T(128)} %select_reduce_fusion.2.order_ref, s32[448]{0:T(512)} %reshape.182.table_ref, bf16[16,192,128]{2,1,0:T(8,128)(2,1)} %copy-done.3, bf16[16,256,128]{2,1,0:T(8,128)(2,1)} %collective-permute-done.6.before_any, ...), custom_call_target="tpu_custom_call" | custom-call | flops 10066329600 | bytes 4194304 | tf_op jit(solution)/shard_map/video_attention_2/pallas_call | solution.py:274
  155.3 7.2 %all-to-all-start.3 = ((bf16[16,128,128]{2,1,0:T(8,128)(2,1)}), bf16[16,128,128]{2,1,0:T(8,128)(2,1)S(1)}, u32[]{:S(2)}, u32[]{:S(2)}) async-start(bf16[16,128,128]{2,1,0:T(8,128)(2,1)} %video_attention_2.1), calls=%async_computation.3 | async-start | bytes 1048576 | tf_op jit(solution)/shard_map/all_to_all | solution.py:400
  162.6 2.5 %text_merge.3 = (bf16[232,128]{1,0:T(8,128)(2,1)}, bf16[232,64]{1,0:T(8,128)(2,1)}) custom-call(f32[232,256]{1,0:T(8,128)} %text_merge.2.refs_0_, f32[232,256]{1,0:T(8,128)} %copy-done.7, f32[232,256]{1,0:T(8,128)} %copy-done.8, f32[232,256]{1,0:T(8,128)} %copy-done.9), custom_call_target="tpu_custom_call" | custom-call | tf_op jit(solution)/shard_map/text_merge/pallas_call | solution.py:331
  166.8 13.1 %all-to-all-done.3.pair_ref = bf16[16,128,128]{2,1,0:T(8,128)(2,1)S(1)} async-done(((bf16[16,128,128]{2,1,0:T(8,128)(2,1)}), bf16[16,128,128]{2,1,0:T(8,128)(2,1)S(1)}, u32[]{:S(2)}, u32[]{:S(2)}) %all-to-all-start.3) | async-done | bytes 524320 | tf_op jit(solution)/shard_map/all_to_all | solution.py:400
  180.7 2.2 %unpack.1 = bf16[128,3072]{1,0:T(8,128)(2,1)} custom-call(bf16[16,64,128]{2,1,0:T(8,128)(2,1)} %copy-done.2, bf16[16,128,128]{2,1,0:T(8,128)(2,1)} %copy-done.1), custom_call_target="tpu_custom_call" | custom-call | tf_op jit(solution)/shard_map/unpack/pallas_call | solution.py:132
  (83 shorter events, 16.4 us)
Async XLA Ops:
  4.2 47.6 %all-to-all-start = ((bf16[16,384,128]{2,1,0:T(8,128)(2,1)}), bf16[16,384,128]{2,1,0:T(8,128)(2,1)S(1)}, u32[]{:S(2)}, u32[]{:S(2)}) async-start(bf16[16,384,128]{2,1,0:T(8,128)(2,1)} %pack.2), calls=%async_computation | async-start | bytes 3145728 | tf_op jit(solution)/shard_map/all_to_all | solution.py:400
  13.4 4.4 %copy-start.12 = (bf16[226,192]{0,1:T(8,128)(2,1)S(1)}, bf16[226,192]{0,1:T(8,128)(2,1)}, u32[]{:S(2)}) copy-start(bf16[226,192]{0,1:T(8,128)(2,1)} %param.14) | copy-start | bytes 260356
  18.1 38.0 %copy-start.17 = (s32[16]{0:T(128)}, s32[16]{0:T(128)S(1)}, u32[]{:S(2)}) copy-start(s32[16]{0:T(128)S(1)} %convert_reduce_fusion.1.counts_ref) | copy-start | bytes 196
  51.8 21.9 %copy-start = (bf16[16,384,128]{2,1,0:T(8,128)(2,1)}, bf16[16,384,128]{2,1,0:T(8,128)(2,1)S(1)}, u32[]{:S(2)}) copy-start(bf16[16,384,128]{2,1,0:T(8,128)(2,1)S(1)} %all-to-all-done.kv_ref.own_any) | copy-start | bytes 4718596
  51.8 44.2 %all-to-all-start.1 = ((bf16[16,192,128]{2,1,0:T(8,128)(2,1)}), bf16[16,192,128]{2,1,0:T(8,128)(2,1)S(1)}, u32[]{:S(2)}, u32[]{:S(2)}) async-start(bf16[16,192,128]{2,1,0:T(8,128)(2,1)} %pack.3), calls=%async_computation.1 | async-start | bytes 1572864 | tf_op jit(solution)/shard_map/all_to_all | solution.py:400
  56.1 27.8 %copy-start.16 = (s32[226]{0:T(256)S(1)}, s32[226]{0:T(256)}, u32[]{:S(2)}) copy-start(s32[226]{0:T(256)} %param.17) | copy-start | bytes 2716
  56.1 29.8 %collective-permute-start = (bf16[16,128,128]{2,1,0:T(8,128)(2,1)S(1)}, bf16[16,128,128]{2,1,0:T(8,128)(2,1)S(1)}, u32[]{:S(2)}, u32[]{:S(2)}) collective-permute-start(bf16[16,128,128]{2,1,0:T(8,128)(2,1)S(1)} %slice.73), channel_id=1, source_target_pairs={{0,16},{16,32},{32,48},{48,64},{64,80},{80,96},{96,112},{112,128},... | collective-permute-start | bytes 1572872 | tf_op jit(solution)/shard_map/ppermute | solution.py:407
  59.4 26.6 %collective-permute-start.1 = (bf16[16,128,128]{2,1,0:T(8,128)(2,1)S(1)}, bf16[16,128,128]{2,1,0:T(8,128)(2,1)}, u32[]{:S(2)}, u32[]{:S(2)}) collective-permute-start(bf16[16,128,128]{2,1,0:T(8,128)(2,1)S(1)} %slice.73), channel_id=1, source_target_pairs={{16,0},{32,16},{48,32},{64,48},{80,64},{96,80},{112,96},{128,112},... | collective-permute-start | bytes 1572872 | tf_op jit(solution)/shard_map/ppermute | solution.py:407
  63.6 10.1 %collective-permute-start.5 = (bf16[16,128]{1,0:T(8,128)(2,1)S(1)}, bf16[16,128]{1,0:T(8,128)(2,1)S(1)}, u32[]{:S(2)}, u32[]{:S(2)}) collective-permute-start(bf16[16,128]{1,0:T(8,128)(2,1)S(1)} %slice_bitcast_fusion), channel_id=1, source_target_pairs={{0,16},{16,32},{32,48},{48,64},{64,80},{80,96},{96,112},{112,128},... | collective-permute-start | bytes 12296 | tf_op jit(solution)/shard_map/ppermute | solution.py:407
  76.5 56.2 %collective-permute-start.6 = (bf16[16,256,128]{2,1,0:T(8,128)(2,1)}, bf16[16,256,128]{2,1,0:T(8,128)(2,1)}, u32[]{:S(2)}, u32[]{:S(2)}) collective-permute-start(bf16[16,256,128]{2,1,0:T(8,128)(2,1)} %take_pair.1), channel_id=1, source_target_pairs={{0,16},{16,32},{32,48},{48,64},{64,80},{80,96},{96,112},{112,128},... | collective-permute-start | bytes 3145736 | tf_op jit(solution)/shard_map/ppermute | solution.py:407
  78.5 54.3 %collective-permute-start.7 = (bf16[16,256,128]{2,1,0:T(8,128)(2,1)}, bf16[16,256,128]{2,1,0:T(8,128)(2,1)}, u32[]{:S(2)}, u32[]{:S(2)}) collective-permute-start(bf16[16,256,128]{2,1,0:T(8,128)(2,1)} %take_pair.1), channel_id=1, source_target_pairs={{16,0},{32,16},{48,32},{64,48},{80,64},{96,80},{112,96},{128,112},... | collective-permute-start | bytes 3145736 | tf_op jit(solution)/shard_map/ppermute | solution.py:407
  92.1 19.0 %collective-permute-start.2 = (f32[232,256]{1,0:T(8,128)}, f32[232,256]{1,0:T(8,128)S(1)}, u32[]{:S(2)}, u32[]{:S(2)}) collective-permute-start(f32[232,256]{1,0:T(8,128)} %text_partial.1.refs_0_), channel_id=1, source_target_pairs={{0,64},{16,80},{32,96},{48,112},{64,128},{80,144},{96,160},{112,17... | collective-permute-start | bytes 712712 | tf_op jit(solution)/shard_map/ppermute | solution.py:346
  93.3 19.8 %collective-permute-start.3 = (f32[232,256]{1,0:T(8,128)}, f32[232,256]{1,0:T(8,128)S(1)}, u32[]{:S(2)}, u32[]{:S(2)}) collective-permute-start(f32[232,256]{1,0:T(8,128)} %text_partial.1.refs_0_), channel_id=1, source_target_pairs={{0,128},{16,144},{32,160},{48,176},{64,192},{80,208},{96,224},{112... | collective-permute-start | bytes 712712 | tf_op jit(solution)/shard_map/ppermute | solution.py:346
  94.0 23.6 %collective-permute-start.4 = (f32[232,256]{1,0:T(8,128)}, f32[232,256]{1,0:T(8,128)S(1)}, u32[]{:S(2)}, u32[]{:S(2)}) collective-permute-start(f32[232,256]{1,0:T(8,128)} %text_partial.1.refs_0_), channel_id=1, source_target_pairs={{0,192},{16,208},{32,224},{48,240},{64,0},{80,16},{96,32},{112,48}... | collective-permute-start | bytes 712712 | tf_op jit(solution)/shard_map/ppermute | solution.py:346
  111.1 6.5 %copy-start.4 = (f32[232,256]{1,0:T(8,128)}, f32[232,256]{1,0:T(8,128)S(1)}, u32[]{:S(2)}) copy-start(f32[232,256]{1,0:T(8,128)S(1)} %collective-permute-done.2.refs_1_) | copy-start | bytes 712708
  120.9 34.3 %collective-permute-start.8 = (f32[232,256]{1,0:T(8,128)}, f32[232,256]{1,0:T(8,128)S(1)}, u32[]{:S(2)}, u32[]{:S(2)}) collective-permute-start(f32[232,256]{1,0:T(8,128)} %text_merge.2.refs_0_), channel_id=1, source_target_pairs={{0,16},{16,32},{32,48},{48,0},{64,80},{80,96},{96,112},{112,64},{1... | collective-permute-start | bytes 712712 | tf_op jit(solution)/shard_map/ppermute | solution.py:346
  120.9 34.3 %collective-permute-start.9 = (f32[232,256]{1,0:T(8,128)}, f32[232,256]{1,0:T(8,128)S(1)}, u32[]{:S(2)}, u32[]{:S(2)}) collective-permute-start(f32[232,256]{1,0:T(8,128)} %text_merge.2.refs_0_), channel_id=1, source_target_pairs={{0,32},{16,48},{32,0},{48,16},{64,96},{80,112},{96,64},{112,80},{1... | collective-permute-start | bytes 712712 | tf_op jit(solution)/shard_map/ppermute | solution.py:346
  120.9 34.3 %collective-permute-start.10 = (f32[232,256]{1,0:T(8,128)}, f32[232,256]{1,0:T(8,128)S(1)}, u32[]{:S(2)}, u32[]{:S(2)}) collective-permute-start(f32[232,256]{1,0:T(8,128)} %text_merge.2.refs_0_), channel_id=1, source_target_pairs={{0,48},{16,0},{32,16},{48,32},{64,112},{80,64},{96,80},{112,96},{1... | collective-permute-start | bytes 712712 | tf_op jit(solution)/shard_map/ppermute | solution.py:346
  123.6 31.7 %all-to-all-start.2 = ((bf16[16,64,128]{2,1,0:T(8,128)(2,1)}), bf16[16,64,128]{2,1,0:T(8,128)(2,1)S(1)}, u32[]{:S(2)}, u32[]{:S(2)}) async-start(bf16[16,64,128]{2,1,0:T(8,128)(2,1)} %video_attention_1.1), calls=%async_computation.2 | async-start | bytes 524288 | tf_op jit(solution)/shard_map/all_to_all | solution.py:400
  155.2 7.3 %copy-start.7 = (f32[232,256]{1,0:T(8,128)}, f32[232,256]{1,0:T(8,128)S(1)}, u32[]{:S(2)}) copy-start(f32[232,256]{1,0:T(8,128)S(1)} %collective-permute-done.8.refs_1_) | copy-start | bytes 712708
  155.3 7.3 %copy-start.8 = (f32[232,256]{1,0:T(8,128)}, f32[232,256]{1,0:T(8,128)S(1)}, u32[]{:S(2)}) copy-start(f32[232,256]{1,0:T(8,128)S(1)} %collective-permute-done.9.refs_2_) | copy-start | bytes 712708
  155.3 7.3 %copy-start.9 = (f32[232,256]{1,0:T(8,128)}, f32[232,256]{1,0:T(8,128)S(1)}, u32[]{:S(2)}) copy-start(f32[232,256]{1,0:T(8,128)S(1)} %collective-permute-done.10.refs_3_) | copy-start | bytes 712708
  155.3 24.6 %copy-start.2 = (bf16[16,64,128]{2,1,0:T(8,128)(2,1)}, bf16[16,64,128]{2,1,0:T(8,128)(2,1)S(1)}, u32[]{:S(2)}) copy-start(bf16[16,64,128]{2,1,0:T(8,128)(2,1)S(1)} %all-to-all-done.2.single_ref) | copy-start | bytes 786436
  155.3 24.6 %all-to-all-start.3 = ((bf16[16,128,128]{2,1,0:T(8,128)(2,1)}), bf16[16,128,128]{2,1,0:T(8,128)(2,1)S(1)}, u32[]{:S(2)}, u32[]{:S(2)}) async-start(bf16[16,128,128]{2,1,0:T(8,128)(2,1)} %video_attention_2.1), calls=%async_computation.3 | async-start | bytes 1048576 | tf_op jit(solution)/shard_map/all_to_all | solution.py:400
  (10 other events, 22.2 us)

commit v5 on v4

--- a/solution.py
+++ b/solution.py
@@ -82,25 +82,6 @@
         cost_estimate=pl.CostEstimate(flops=0, bytes_accessed=4 * count * arrays[0].size, transcendentals=0),
         name="pack",
     )(*arrays)
-
-
-def take_pair_kernel(kv_ref, token_ref, out_ref, sem):
-    del token_ref
-    copy = pltpu.make_async_copy(kv_ref.at[:, pl.ds(2 * HD, 2 * TILE)], out_ref, sem)
-    copy.start()
-    copy.wait()
-
-
-def take_pair(kv, token):
-    any_space = pl.BlockSpec(memory_space=pl.ANY)
-    return pl.pallas_call(
-        take_pair_kernel,
-        in_specs=[any_space] * 2,
-        out_specs=pl.BlockSpec(memory_space=pltpu.VMEM),
-        out_shape=jax.ShapeDtypeStruct((kv.shape[0], 2 * TILE, LANES), BF16),
-        scratch_shapes=[pltpu.SemaphoreType.DMA],
-        name="take_pair",
-    )(kv, token)
 
 
 def unpack_kernel(single_ref, pair_ref, out_ref, held_ref, single_sems, pair_sems):
@@ -349,9 +330,9 @@
 
 def text_kernel(
     kv_ref, pair_q_ref, pair_k_ref, pair_v_ref, single_q_ref, single_k_ref, single_v_ref, bias_ref,
-    before_any, after_any, out_ref, score_ref,
+    earlier_ref, out_ref, score_ref,
 ):
-    del before_any, after_any
+    del earlier_ref
     low = low_lanes(TEXT_ROWS)
     pair_q = pair_q_ref[...].astype(F32)
 
@@ -386,14 +367,14 @@
     pairs = 3 * TEXT_ROWS * (LAYER + 2) * TILE
     return pl.pallas_call(
         text_kernel,
-        in_specs=[vmem] * 8 + [pl.BlockSpec(memory_space=pl.ANY)] * len(earlier),
+        in_specs=[vmem] * 8 + [pl.BlockSpec(memory_space=pl.ANY)],
         out_specs=vmem,
         out_shape=jax.ShapeDtypeStruct((TEXT_KEPT, 2 * LANES), F32),
         scratch_shapes=[pltpu.VMEM((3, 2 + LAYER, TEXT_ROWS, LANES), F32)],
         compiler_params=pltpu.CompilerParams(vmem_limit_bytes=VMEM_LIMIT),
         cost_estimate=pl.CostEstimate(flops=16 * HD * pairs, bytes_accessed=4 * kv.size, transcendentals=pairs),
         name="text_partial",
-    )(kv, pair_q, pair_k, pair_v, single_q, single_k, single_v, bias, *earlier)
+    )(kv, pair_q, pair_k, pair_v, single_q, single_k, single_v, bias, earlier)
 
 
 def exchange(blocks, axis):
@@ -430,21 +411,24 @@
     kv, queries, *rest = lax.optimization_barrier((kv, pack(video_q)) + lists + text)
     lists, (pair_tq, pair_tk, pair_tv, single_tq, single_tk, single_tv) = rest[:3], rest[3:]
     queries = exchange(after(queries, kv), "head")
-    single_before, single_after = both_sides(kv[:, : 2 * HD])
+    single_kv = kv[:, : 2 * HD]
+    single_before, single_after = both_sides(single_kv)
     token, _ = both_sides(kv[0, :16])
-    pair_before, pair_after = both_sides(take_pair(kv, token))
-    partial = text_partial(kv, pair_tq, pair_tk, pair_tv, single_tq, single_tk, single_tv, own_bias, (single_before, single_after))
+    pair_before, pair_after = both_sides(kv[:, 2 * HD :])
+    partial = text_partial(kv, pair_tq, pair_tk, pair_tv, single_tq, single_tk, single_tv, own_bias, token)
     partial = from_others(partial, 4)
 
+    partial = merge(partial, False)
+    pair_q = after(queries, partial)
+    partial = from_others(partial, 1)
+
+    pair_out = video_attention(2, lists, pair_q, HD, pair_before, kv, 2 * HD, pair_after, pair_tk, pair_tv, bias)
+    pair_back = exchange(pair_out, "head")
+    single_q = after(queries, pair_out)
     single_out = video_attention(
-        1, lists, queries, 0, single_before, kv, 0, single_after, single_tk, single_tv, bias
+        1, lists, single_q, 0, single_before, kv, 0, single_after, single_tk, single_tv, bias
     )
-    *partial, single_out = lax.optimization_barrier((*partial, single_out))
-    single_back = exchange(single_out, "head")
-    partial = from_others(merge(partial, False), 1)
-    pair_q = after(queries, single_out)
-    pair_out = video_attention(2, lists, pair_q, HD, pair_before, kv, 2 * HD, pair_after, pair_tk, pair_tv, bias)
-    pair_back = exchange(after(pair_out, single_back, *partial), "head")
+    single_back = exchange(after(single_out, pair_back, *partial), "head")
     video_out = unpack(single_back, pair_back)
 
     pair_part, single_part = (part[:TEXT] for part in merge(partial, True))

time: 184 us -> 184 us (level)
  local copies, waits for them, and re-layouts: 7.38 us -> 10.4 us
  waiting for transfers between devices: 58.6 us -> 55.9 us
  Pallas kernels: 57.5 us -> 55.4 us
  starting transfers between devices: 53.1 us -> 55.1 us
    ppermute x5, waiting for transfers between devices: 8.22 us -> 14.4 us  [both_sides(): return (lax.ppermute(layer, 'seq', up), lax.ppermute(layer, 'seq', down))]
    all_to_all x4, waiting for transfers between devices: 43.9 us -> 39.2 us  [exchange(): return lax.all_to_all(blocks, axis, split_axis=0, concat_axis=0, tiled=True)]
    ppermute x6, waiting for transfers between devices: 6.47 us -> 2.26 us  [from_others(): parts.append(lax.ppermute(part, 'seq', pairs))]
    optimization_barrier x2 -> x4, local copies, waits for them, and re-layouts: 1.4 us -> 4.51 us  [body(): lax.optimization_barrier((kv, pack(video_q)) + lists + text)]
    pallas_call x1 -> x0, Pallas kernels: 2.21 us -> none  [take_pair(): pl.pallas_call(take_pair_kernel, in_specs=[any_space] * 2, out_specs=pl.B...]
    unnamed x42 -> x39, local copies, waits for them, and re-layouts: 4.91 us -> 3.67 us
  transfers between devices with their start and end apart: 15 -> 15, of which waited for: 5 -> 6; matrix products, arithmetic and copies ran while one was open for 5% -> 7% of each run, Pallas kernels for 28% -> 27%
where the time goes in v5:
time: 184 us; the launch traced here: 183 us
  waiting for transfers between devices  55.9 us (30%)
  Pallas kernels  55.4 us (30%)
  starting transfers between devices  55.1 us (30%)
  local copies, waits for them, and re-layouts  10.4 us (6%)
  other arithmetic  4.92 us (3%)
    all_to_all x4, waiting for transfers between devices, exchange(): return lax.all_to_all(blocks, axis, split_axis=0, concat_axis=0, tiled=True)  39.2 us
    pallas_call x2, Pallas kernels, video_attention(): pl.pallas_call(functools.partial(video_kernel, heads, together, query_row...  36.6 us
    all_to_all x4, starting transfers between devices, exchange(): return lax.all_to_all(blocks, axis, split_axis=0, concat_axis=0, tiled=True)  29.9 us
    ppermute x5, starting transfers between devices, both_sides(): return (lax.ppermute(layer, 'seq', up), lax.ppermute(layer, 'seq', down))  18.5 us
    ppermute x5, waiting for transfers between devices, both_sides(): return (lax.ppermute(layer, 'seq', up), lax.ppermute(layer, 'seq', down))  14.4 us
    ppermute x6, starting transfers between devices, from_others(): parts.append(lax.ppermute(part, 'seq', pairs))  6.69 us
    pallas_call x2, Pallas kernels, pack(): pl.pallas_call(pack_kernel, in_specs=[pl.BlockSpec(memory_space=pl.ANY)]...  6.1 us
    pallas_call x1, Pallas kernels, text_partial(): pl.pallas_call(text_kernel, in_specs=[vmem] * 8 + [pl.BlockSpec(memory_sp...  5.35 us
  transfers between devices with their start and end apart: 15, of which 6 were waited for; matrix products, arithmetic and copies ran while one was open for 7% of the time, Pallas kernels for 27%

profile of v5, /device:TPU:3, one launch (start us, length us, event | category | flops | bytes accessed | tf_op | source)
XLA Modules:
  0.0 182.9 jit_solution(3939643193760923839)
XLA Ops:
  0.6 3.6 %pack.2 = bf16[16,384,128]{2,1,0:T(8,128)(2,1)} custom-call(bf16[128,3072]{1,0:T(8,128)(2,1)} %refs_0_.2, bf16[128,3072]{1,0:T(8,128)(2,1)} %refs_1_.1), custom_call_target="tpu_custom_call" | custom-call | bytes 3145728 | tf_op jit(solution)/shard_map/pack/pallas_call | solution.py:73
  4.2 9.2 %all-to-all-start = ((bf16[16,384,128]{2,1,0:T(8,128)(2,1)}), bf16[16,384,128]{2,1,0:T(8,128)(2,1)S(1)}, u32[]{:S(2)}, u32[]{:S(2)}) async-start(bf16[16,384,128]{2,1,0:T(8,128)(2,1)} %pack.2), calls=%async_computation | async-start | bytes 3145728 | tf_op jit(solution)/shard_map/all_to_all | solution.py:381
  13.4 2.5 %pack.3 = bf16[16,192,128]{2,1,0:T(8,128)(2,1)} custom-call(bf16[128,3072]{1,0:T(8,128)(2,1)} %refs_0_.3), custom_call_target="tpu_custom_call" | custom-call | bytes 1572864 | tf_op jit(solution)/shard_map/pack/pallas_call | solution.py:73
  20.4 31.4 %all-to-all-done.kv_ref.own_any = bf16[16,384,128]{2,1,0:T(8,128)(2,1)S(1)} async-done(((bf16[16,384,128]{2,1,0:T(8,128)(2,1)}), bf16[16,384,128]{2,1,0:T(8,128)(2,1)S(1)}, u32[]{:S(2)}, u32[]{:S(2)}) %all-to-all-start) | async-done | bytes 1572896 | tf_op jit(solution)/shard_map/all_to_all | solution.py:381
  51.8 4.4 %all-to-all-start.1 = ((bf16[16,192,128]{2,1,0:T(8,128)(2,1)}), bf16[16,192,128]{2,1,0:T(8,128)(2,1)S(1)}, u32[]{:S(2)}, u32[]{:S(2)}) async-start(bf16[16,192,128]{2,1,0:T(8,128)(2,1)} %pack.3), calls=%async_computation.1 | async-start | bytes 1572864 | tf_op jit(solution)/shard_map/all_to_all | solution.py:381
  56.3 3.2 %collective-permute-start.4 = (bf16[16,256,128]{2,1,0:T(8,128)(2,1)S(1)}, bf16[16,256,128]{2,1,0:T(8,128)(2,1)}, u32[]{:S(2)}, u32[]{:S(2)}) collective-permute-start(bf16[16,256,128]{2,1,0:T(8,128)(2,1)S(1)} %slice.77), channel_id=1, source_target_pairs={{0,16},{16,32},{32,48},{48,64},{64,80},{80,96},{96,112},{112,128},... | collective-permute-start | bytes 3145736 | tf_op jit(solution)/shard_map/ppermute | solution.py:388
  59.6 4.2 %collective-permute-start.5 = (bf16[16,256,128]{2,1,0:T(8,128)(2,1)S(1)}, bf16[16,256,128]{2,1,0:T(8,128)(2,1)}, u32[]{:S(2)}, u32[]{:S(2)}) collective-permute-start(bf16[16,256,128]{2,1,0:T(8,128)(2,1)S(1)} %slice.77), channel_id=1, source_target_pairs={{16,0},{32,16},{48,32},{64,48},{80,64},{96,80},{112,96},{128,112},... | collective-permute-start | bytes 3145736 | tf_op jit(solution)/shard_map/ppermute | solution.py:388
  63.8 1.9 %collective-permute-start = (bf16[16,128]{1,0:T(8,128)(2,1)S(1)}, bf16[16,128]{1,0:T(8,128)(2,1)S(1)}, u32[]{:S(2)}, u32[]{:S(2)}) collective-permute-start(bf16[16,128]{1,0:T(8,128)(2,1)S(1)} %slice_bitcast_fusion), channel_id=1, source_target_pairs={{0,16},{16,32},{32,48},{48,64},{64,80},{80,96},{96,112},{112,128},... | collective-permute-start | bytes 12296 | tf_op jit(solution)/shard_map/ppermute | solution.py:388
  66.3 1.6 copy.22.pair_q_ref
  70.8 14.4 %collective-permute-done.earlier_ref = bf16[16,128]{1,0:T(8,128)(2,1)S(1)} collective-permute-done((bf16[16,128]{1,0:T(8,128)(2,1)S(1)}, bf16[16,128]{1,0:T(8,128)(2,1)S(1)}, u32[]{:S(2)}, u32[]{:S(2)}) %collective-permute-start) | collective-permute-done | bytes 4128 | tf_op jit(solution)/shard_map/ppermute | solution.py:388
  85.8 5.4 %text_partial.1.refs_0_ = f32[232,256]{1,0:T(8,128)} custom-call(bf16[16,384,128]{2,1,0:T(8,128)(2,1)} %copy-done, bf16[256,128]{1,0:T(8,128)(2,1)} %copy.22.pair_q_ref, bf16[256,128]{1,0:T(8,128)(2,1)} %copy.23.pair_k_ref.text_k_ref, bf16[256,128]{1,0:T(8,128)(2,1)} %copy.24.pair_v_ref.text_v_ref, bf16[256,64]{1,0:T(8,128)(2,1)} %copy.25.single_q_ref, ...), custom_call_target="tpu_custom_call" | custom-call | flops 1811939328 | bytes 3145728 | tf_op jit(solution)/shard_map/text_partial/pallas_call | solution.py:368
  93.0 2.1 %collective-permute-start.3 = (f32[232,256]{1,0:T(8,128)}, f32[232,256]{1,0:T(8,128)S(1)}, u32[]{:S(2)}, u32[]{:S(2)}) collective-permute-start(f32[232,256]{1,0:T(8,128)} %text_partial.1.refs_0_), channel_id=1, source_target_pairs={{0,192},{16,208},{32,224},{48,240},{64,0},{80,16},{96,32},{112,48}... | collective-permute-start | bytes 712712 | tf_op jit(solution)/shard_map/ppermute | solution.py:327
  96.2 1.7 collective-permute-done.1.refs_1_
  97.9 1.9 %collective-permute-start.6 = (bf16[16,128,128]{2,1,0:T(8,128)(2,1)S(1)}, bf16[16,128,128]{2,1,0:T(8,128)(2,1)}, u32[]{:S(2)}, u32[]{:S(2)}) collective-permute-start(bf16[16,128,128]{2,1,0:T(8,128)(2,1)S(1)} %slice.78), channel_id=1, source_target_pairs={{0,16},{16,32},{32,48},{48,64},{64,80},{80,96},{96,112},{112,128},... | collective-permute-start | bytes 1572872 | tf_op jit(solution)/shard_map/ppermute | solution.py:388
  100.4 7.3 %collective-permute-start.7 = (bf16[16,128,128]{2,1,0:T(8,128)(2,1)S(1)}, bf16[16,128,128]{2,1,0:T(8,128)(2,1)}, u32[]{:S(2)}, u32[]{:S(2)}) collective-permute-start(bf16[16,128,128]{2,1,0:T(8,128)(2,1)S(1)} %slice.78), channel_id=1, source_target_pairs={{16,0},{32,16},{48,32},{64,48},{80,64},{96,80},{112,96},{128,112},... | collective-permute-start | bytes 1572872 | tf_op jit(solution)/shard_map/ppermute | solution.py:388
  108.4 2.6 %text_merge.2.refs_0_ = f32[232,256]{1,0:T(8,128)} custom-call(f32[232,256]{1,0:T(8,128)} %text_partial.1.refs_0_, f32[232,256]{1,0:T(8,128)} %copy-done.8, f32[232,256]{1,0:T(8,128)} %copy-done.9, f32[232,256]{1,0:T(8,128)} %copy-done.10), custom_call_target="tpu_custom_call" | custom-call | tf_op jit(solution)/shard_map/text_merge/pallas_call | solution.py:312
  111.9 22.5 %video_attention_2.1 = bf16[16,128,128]{2,1,0:T(8,128)(2,1)} custom-call(s32[16]{0:T(128)} %copy-done.17, s32[16]{0:T(128)} %select_reduce_fusion.2.order_ref, s32[448]{0:T(512)} %reshape.182.table_ref, bf16[16,192,128]{2,1,0:T(8,128)(2,1)} %copy-done.4, bf16[16,256,128]{2,1,0:T(8,128)(2,1)} %collective-permute-done.4.before_any, ...), custom_call_target="tpu_custom_call" | custom-call | flops 10066329600 | bytes 4194304 | tf_op jit(solution)/shard_map/video_attention_2/pallas_call | solution.py:255
  134.4 8.9 %all-to-all-start.2 = ((bf16[16,128,128]{2,1,0:T(8,128)(2,1)}), bf16[16,128,128]{2,1,0:T(8,128)(2,1)S(1)}, u32[]{:S(2)}, u32[]{:S(2)}) async-start(bf16[16,128,128]{2,1,0:T(8,128)(2,1)} %video_attention_2.1), calls=%async_computation.2 | async-start | bytes 1048576 | tf_op jit(solution)/shard_map/all_to_all | solution.py:381
  143.5 2.5 %collective-permute-start.10 = (f32[232,256]{1,0:T(8,128)S(1)}, f32[232,256]{1,0:T(8,128)S(1)}, u32[]{:S(2)}, u32[]{:S(2)}) collective-permute-start(f32[232,256]{1,0:T(8,128)S(1)} %copy-done.3), channel_id=1, source_target_pairs={{0,48},{16,0},{32,16},{48,32},{64,112},{80,64},{96,80},{112,96},{1... | collective-permute-start | bytes 712712 | tf_op jit(solution)/shard_map/ppermute | solution.py:327
  146.1 14.1 %video_attention_1.1 = bf16[16,64,128]{2,1,0:T(8,128)(2,1)} custom-call(s32[16]{0:T(128)} %copy-done.17, s32[16]{0:T(128)} %select_reduce_fusion.2.order_ref, s32[448]{0:T(512)} %reshape.182.table_ref, bf16[16,192,128]{2,1,0:T(8,128)(2,1)} %copy-done.4, bf16[16,128,128]{2,1,0:T(8,128)(2,1)} %collective-permute-done.6.before_any, ...), custom_call_target="tpu_custom_call" | custom-call | flops 5033164800 | bytes 2097152 | tf_op jit(solution)/shard_map/video_attention_1/pallas_call | solution.py:255
  160.6 7.5 %all-to-all-start.3 = ((bf16[16,64,128]{2,1,0:T(8,128)(2,1)}), bf16[16,64,128]{2,1,0:T(8,128)(2,1)S(1)}, u32[]{:S(2)}, u32[]{:S(2)}) async-start(bf16[16,64,128]{2,1,0:T(8,128)(2,1)} %video_attention_1.1), calls=%async_computation.3 | async-start | bytes 524288 | tf_op jit(solution)/shard_map/all_to_all | solution.py:381
  168.1 2.5 %text_merge.3 = (bf16[232,128]{1,0:T(8,128)(2,1)}, bf16[232,64]{1,0:T(8,128)(2,1)}) custom-call(f32[232,256]{1,0:T(8,128)} %text_merge.2.refs_0_, f32[232,256]{1,0:T(8,128)} %copy-done.11, f32[232,256]{1,0:T(8,128)} %copy-done.12, f32[232,256]{1,0:T(8,128)} %copy-done.13), custom_call_target="tpu_custom_call" | custom-call | tf_op jit(solution)/shard_map/text_merge/pallas_call | solution.py:312
  172.3 7.5 %all-to-all-done.3.single_ref = bf16[16,64,128]{2,1,0:T(8,128)(2,1)S(1)} async-done(((bf16[16,64,128]{2,1,0:T(8,128)(2,1)}), bf16[16,64,128]{2,1,0:T(8,128)(2,1)S(1)}, u32[]{:S(2)}, u32[]{:S(2)}) %all-to-all-start.3) | async-done | bytes 262176 | tf_op jit(solution)/shard_map/all_to_all | solution.py:381
  180.5 2.2 %unpack.1 = bf16[128,3072]{1,0:T(8,128)(2,1)} custom-call(bf16[16,64,128]{2,1,0:T(8,128)(2,1)} %copy-done.2, bf16[16,128,128]{2,1,0:T(8,128)(2,1)} %copy-done.1), custom_call_target="tpu_custom_call" | custom-call | tf_op jit(solution)/shard_map/unpack/pallas_call | solution.py:113
  (82 shorter events, 16.7 us)
Async XLA Ops:
  4.2 47.6 %all-to-all-start = ((bf16[16,384,128]{2,1,0:T(8,128)(2,1)}), bf16[16,384,128]{2,1,0:T(8,128)(2,1)S(1)}, u32[]{:S(2)}, u32[]{:S(2)}) async-start(bf16[16,384,128]{2,1,0:T(8,128)(2,1)} %pack.2), calls=%async_computation | async-start | bytes 3145728 | tf_op jit(solution)/shard_map/all_to_all | solution.py:381
  17.7 38.6 %copy-start.17 = (s32[16]{0:T(128)}, s32[16]{0:T(128)S(1)}, u32[]{:S(2)}) copy-start(s32[16]{0:T(128)S(1)} %convert_reduce_fusion.1.counts_ref) | copy-start | bytes 196
  51.8 11.9 %copy-start = (bf16[16,384,128]{2,1,0:T(8,128)(2,1)}, bf16[16,384,128]{2,1,0:T(8,128)(2,1)S(1)}, u32[]{:S(2)}) copy-start(bf16[16,384,128]{2,1,0:T(8,128)(2,1)S(1)} %all-to-all-done.kv_ref.own_any) | copy-start | bytes 4718596
  51.8 13.9 %copy-start.16 = (s32[226]{0:T(256)S(1)}, s32[226]{0:T(256)}, u32[]{:S(2)}) copy-start(s32[226]{0:T(256)} %param.17) | copy-start | bytes 2716
  51.8 59.2 %all-to-all-start.1 = ((bf16[16,192,128]{2,1,0:T(8,128)(2,1)}), bf16[16,192,128]{2,1,0:T(8,128)(2,1)S(1)}, u32[]{:S(2)}, u32[]{:S(2)}) async-start(bf16[16,192,128]{2,1,0:T(8,128)(2,1)} %pack.3), calls=%async_computation.1 | async-start | bytes 1572864 | tf_op jit(solution)/shard_map/all_to_all | solution.py:381
  56.3 54.7 %collective-permute-start.4 = (bf16[16,256,128]{2,1,0:T(8,128)(2,1)S(1)}, bf16[16,256,128]{2,1,0:T(8,128)(2,1)}, u32[]{:S(2)}, u32[]{:S(2)}) collective-permute-start(bf16[16,256,128]{2,1,0:T(8,128)(2,1)S(1)} %slice.77), channel_id=1, source_target_pairs={{0,16},{16,32},{32,48},{48,64},{64,80},{80,96},{96,112},{112,128},... | collective-permute-start | bytes 3145736 | tf_op jit(solution)/shard_map/ppermute | solution.py:388
  59.6 51.5 %collective-permute-start.5 = (bf16[16,256,128]{2,1,0:T(8,128)(2,1)S(1)}, bf16[16,256,128]{2,1,0:T(8,128)(2,1)}, u32[]{:S(2)}, u32[]{:S(2)}) collective-permute-start(bf16[16,256,128]{2,1,0:T(8,128)(2,1)S(1)} %slice.77), channel_id=1, source_target_pairs={{16,0},{32,16},{48,32},{64,48},{80,64},{96,80},{112,96},{128,112},... | collective-permute-start | bytes 3145736 | tf_op jit(solution)/shard_map/ppermute | solution.py:388
  63.8 21.5 %collective-permute-start = (bf16[16,128]{1,0:T(8,128)(2,1)S(1)}, bf16[16,128]{1,0:T(8,128)(2,1)S(1)}, u32[]{:S(2)}, u32[]{:S(2)}) collective-permute-start(bf16[16,128]{1,0:T(8,128)(2,1)S(1)} %slice_bitcast_fusion), channel_id=1, source_target_pairs={{0,16},{16,32},{32,48},{48,64},{64,80},{80,96},{96,112},{112,128},... | collective-permute-start | bytes 12296 | tf_op jit(solution)/shard_map/ppermute | solution.py:388
  91.2 6.7 %collective-permute-start.1 = (f32[232,256]{1,0:T(8,128)}, f32[232,256]{1,0:T(8,128)S(1)}, u32[]{:S(2)}, u32[]{:S(2)}) collective-permute-start(f32[232,256]{1,0:T(8,128)} %text_partial.1.refs_0_), channel_id=1, source_target_pairs={{0,64},{16,80},{32,96},{48,112},{64,128},{80,144},{96,160},{112,17... | collective-permute-start | bytes 712712 | tf_op jit(solution)/shard_map/ppermute | solution.py:327
  92.4 8.0 %collective-permute-start.2 = (f32[232,256]{1,0:T(8,128)}, f32[232,256]{1,0:T(8,128)S(1)}, u32[]{:S(2)}, u32[]{:S(2)}) collective-permute-start(f32[232,256]{1,0:T(8,128)} %text_partial.1.refs_0_), channel_id=1, source_target_pairs={{0,128},{16,144},{32,160},{48,176},{64,192},{80,208},{96,224},{112... | collective-permute-start | bytes 712712 | tf_op jit(solution)/shard_map/ppermute | solution.py:327
  93.0 14.6 %collective-permute-start.3 = (f32[232,256]{1,0:T(8,128)}, f32[232,256]{1,0:T(8,128)S(1)}, u32[]{:S(2)}, u32[]{:S(2)}) collective-permute-start(f32[232,256]{1,0:T(8,128)} %text_partial.1.refs_0_), channel_id=1, source_target_pairs={{0,192},{16,208},{32,224},{48,240},{64,0},{80,16},{96,32},{112,48}... | collective-permute-start | bytes 712712 | tf_op jit(solution)/shard_map/ppermute | solution.py:327
  97.9 9.8 %copy-start.8 = (f32[232,256]{1,0:T(8,128)}, f32[232,256]{1,0:T(8,128)S(1)}, u32[]{:S(2)}) copy-start(f32[232,256]{1,0:T(8,128)S(1)} %collective-permute-done.1.refs_1_) | copy-start | bytes 712708
  97.9 48.2 %collective-permute-start.6 = (bf16[16,128,128]{2,1,0:T(8,128)(2,1)S(1)}, bf16[16,128,128]{2,1,0:T(8,128)(2,1)}, u32[]{:S(2)}, u32[]{:S(2)}) collective-permute-start(bf16[16,128,128]{2,1,0:T(8,128)(2,1)S(1)} %slice.78), channel_id=1, source_target_pairs={{0,16},{16,32},{32,48},{48,64},{64,80},{80,96},{96,112},{112,128},... | collective-permute-start | bytes 1572872 | tf_op jit(solution)/shard_map/ppermute | solution.py:388
  100.4 45.7 %collective-permute-start.7 = (bf16[16,128,128]{2,1,0:T(8,128)(2,1)S(1)}, bf16[16,128,128]{2,1,0:T(8,128)(2,1)}, u32[]{:S(2)}, u32[]{:S(2)}) collective-permute-start(bf16[16,128,128]{2,1,0:T(8,128)(2,1)S(1)} %slice.78), channel_id=1, source_target_pairs={{16,0},{32,16},{48,32},{64,48},{80,64},{96,80},{112,96},{128,112},... | collective-permute-start | bytes 1572872 | tf_op jit(solution)/shard_map/ppermute | solution.py:388
  111.9 31.4 %copy-start.3 = (f32[232,256]{1,0:T(8,128)S(1)}, f32[232,256]{1,0:T(8,128)}, u32[]{:S(2)}) copy-start(f32[232,256]{1,0:T(8,128)} %text_merge.2.refs_0_) | copy-start | bytes 712708
  134.4 26.2 %all-to-all-start.2 = ((bf16[16,128,128]{2,1,0:T(8,128)(2,1)}), bf16[16,128,128]{2,1,0:T(8,128)(2,1)S(1)}, u32[]{:S(2)}, u32[]{:S(2)}) async-start(bf16[16,128,128]{2,1,0:T(8,128)(2,1)} %video_attention_2.1), calls=%async_computation.2 | async-start | bytes 1048576 | tf_op jit(solution)/shard_map/all_to_all | solution.py:381
  143.3 16.9 %collective-permute-start.8 = (f32[232,256]{1,0:T(8,128)S(1)}, f32[232,256]{1,0:T(8,128)S(1)}, u32[]{:S(2)}, u32[]{:S(2)}) collective-permute-start(f32[232,256]{1,0:T(8,128)S(1)} %copy-done.3), channel_id=1, source_target_pairs={{0,16},{16,32},{32,48},{48,0},{64,80},{80,96},{96,112},{112,64},{1... | collective-permute-start | bytes 712712 | tf_op jit(solution)/shard_map/ppermute | solution.py:327
  143.4 16.9 %collective-permute-start.9 = (f32[232,256]{1,0:T(8,128)S(1)}, f32[232,256]{1,0:T(8,128)S(1)}, u32[]{:S(2)}, u32[]{:S(2)}) collective-permute-start(f32[232,256]{1,0:T(8,128)S(1)} %copy-done.3), channel_id=1, source_target_pairs={{0,32},{16,48},{32,0},{48,16},{64,96},{80,112},{96,64},{112,80},{1... | collective-permute-start | bytes 712712 | tf_op jit(solution)/shard_map/ppermute | solution.py:327
  143.5 16.7 %collective-permute-start.10 = (f32[232,256]{1,0:T(8,128)S(1)}, f32[232,256]{1,0:T(8,128)S(1)}, u32[]{:S(2)}, u32[]{:S(2)}) collective-permute-start(f32[232,256]{1,0:T(8,128)S(1)} %copy-done.3), channel_id=1, source_target_pairs={{0,48},{16,0},{32,16},{48,32},{64,112},{80,64},{96,80},{112,96},{1... | collective-permute-start | bytes 712712 | tf_op jit(solution)/shard_map/ppermute | solution.py:327
  160.2 7.9 %copy-start.11 = (f32[232,256]{1,0:T(8,128)}, f32[232,256]{1,0:T(8,128)S(1)}, u32[]{:S(2)}) copy-start(f32[232,256]{1,0:T(8,128)S(1)} %collective-permute-done.8.refs_1_) | copy-start | bytes 712708
  160.2 7.8 %copy-start.12 = (f32[232,256]{1,0:T(8,128)}, f32[232,256]{1,0:T(8,128)S(1)}, u32[]{:S(2)}) copy-start(f32[232,256]{1,0:T(8,128)S(1)} %collective-permute-done.9.refs_2_) | copy-start | bytes 712708
  160.3 7.8 %copy-start.13 = (f32[232,256]{1,0:T(8,128)}, f32[232,256]{1,0:T(8,128)S(1)}, u32[]{:S(2)}) copy-start(f32[232,256]{1,0:T(8,128)S(1)} %collective-permute-done.10.refs_3_) | copy-start | bytes 712708
  160.6 19.2 %copy-start.1 = (bf16[16,128,128]{2,1,0:T(8,128)(2,1)}, bf16[16,128,128]{2,1,0:T(8,128)(2,1)S(1)}, u32[]{:S(2)}) copy-start(bf16[16,128,128]{2,1,0:T(8,128)(2,1)S(1)} %all-to-all-done.2.pair_ref) | copy-start | bytes 1572868
  160.6 19.2 %all-to-all-start.3 = ((bf16[16,64,128]{2,1,0:T(8,128)(2,1)}), bf16[16,64,128]{2,1,0:T(8,128)(2,1)S(1)}, u32[]{:S(2)}, u32[]{:S(2)}) async-start(bf16[16,64,128]{2,1,0:T(8,128)(2,1)} %video_attention_1.1), calls=%async_computation.3 | async-start | bytes 524288 | tf_op jit(solution)/shard_map/all_to_all | solution.py:381
  (10 other events, 31.8 us)
